TPU v7x, 32 devices: a whole 2x2x4 slice. The times are simulated.
32 devices in a mesh: pp: 2 (over y), ep: 16 (over z, x, core).
Axes of the slice: x: 2, y: 2, z: 4, core: 2. Of those that a mesh axis runs over, the one named last changes fastest.
Arguments:
- fwd_tokens: bfloat16 [2, 2048, 4096], P('pp', 'ep'), may hold values from -6 to 6
- fwd_routes: int32 [2, 2048, 1], P('pp', 'ep'), may hold values from 0 to 3; in each aligned block of 128 rows (0 to 127, 128 to 255, ..., all dimensions but the last counted through in order) at most 48 rows name the same one
- fwd_gates: float32 [2, 2048, 1], P('pp', 'ep'), may hold values from 0.05 to 0.6
- bwd_tokens: bfloat16 [2, 2048, 4096], P('pp', 'ep'), may hold values from -6 to 6
- bwd_grads: bfloat16 [2, 2048, 4096], P('pp', 'ep'), may hold values from -6 to 6
- bwd_routes: int32 [2, 2048, 1], P('pp', 'ep'), may hold values from 0 to 3; in each aligned block of 128 rows (0 to 127, 128 to 255, ..., all dimensions but the last counted through in order) at most 48 rows name the same one
- bwd_gates: float32 [2, 2048, 1], P('pp', 'ep'), may hold values from 0.05 to 0.6
- gate_proj: bfloat16 [2, 16, 1024, 768], P('pp', 'ep'), may hold values from -0.09375 to 0.09375
- up_proj: bfloat16 [2, 16, 1024, 768], P('pp', 'ep'), may hold values from -0.09375 to 0.09375
- down_proj: bfloat16 [2, 16, 768, 1024], P('pp', 'ep'), may hold values from -0.21875 to 0.21875
Outputs:
- handed_forward: bfloat16 [2, 2048, 4096], P('pp', 'ep')
- handed_backward: bfloat16 [2, 2048, 4096], P('pp', 'ep')
Inputs may be any that keep to these rules, and one draw needn't show every extreme that they name: `fwd_routes`: among the 128 tokens of one index of ep, no expert is named by more than 48 tokens, and in some such block an expert is named exactly 48 times. `bwd_routes`: among the 128 tokens of one index of ep, no expert is named by more than 48 tokens, and in some such block an expert is named exactly 48 times.
All inputs are finite; a program needn't handle non-finite values.
Results may differ from a plain program's by a relative error of at most 0.0071.
Values may be sent and summed in bfloat16 or wider, within the bound.
No kernel may reach another device: no remote copies, remote signals or barrier semaphores. Data moves between devices by JAX's collectives and lax.ppermute only.
A program may use at most 128 MiB of HBM per device.

v0:
```python
import jax
import jax.numpy as jnp
from jax import lax
from jax.sharding import PartitionSpec as P


def partner(block, axis, distance):
    count = lax.axis_size(axis)
    route = []
    for low in range(count):
        high = low | 1 << distance
        if high != low and high < count:
            route += [(low, high), (high, low)]
    return lax.ppermute(block, axis, route)


def shifted(shard, axis, by):
    count = lax.axis_size(axis)
    pairs = [(i, i + by) for i in range(count) if 0 <= i + by < count]
    return lax.ppermute(shard, axis, pairs)


def slot_places(routes, expert_count, slot_cap):
    tok_count = routes.shape[0]
    route_width = routes.shape[1]
    flat_routes = routes.reshape(-1)
    onehot = (flat_routes[:, None] == jnp.arange(expert_count, dtype=jnp.int32)[None, :]).astype(
        jnp.int32
    )
    before = jnp.cumsum(onehot, axis=0) - onehot
    position = jnp.sum(before * onehot, axis=1)
    slot_match = (position[:, None] == jnp.arange(slot_cap, dtype=jnp.int32)[None, :]).astype(
        jnp.float32
    )
    placed = onehot.astype(jnp.float32)[:, :, None] * slot_match[:, None, :]
    return placed.reshape(tok_count, route_width, expert_count, slot_cap)


def spread_rows(places, values):
    tok_count = values.shape[0]
    quarter_width = values.shape[1] // 4
    return jnp.einsum(
        "tkec,thf->ehcf",
        places.astype(jnp.bfloat16),
        values.reshape(tok_count, 4, quarter_width),
        preferred_element_type=jnp.float32,
    )


def device_rows(placed):
    return placed.astype(jnp.bfloat16).reshape(
        4 * placed.shape[0], placed.shape[2], placed.shape[3]
    )


def collect(places, returned):
    expert_count = places.shape[2]
    shaped = returned.reshape(expert_count, 4, returned.shape[1], returned.shape[2])
    return jnp.einsum(
        "tkec,ehcf->tkhf", places.astype(jnp.bfloat16), shaped, preferred_element_type=jnp.float32
    )


def contract_cols(left, right):
    return lax.dot_general(
        left, right, (((1,), (1,)), ((), ())), preferred_element_type=jnp.float32
    )


def forward_expert(row_block, w_gate, w_up, w_down):
    proj_width = w_gate.shape[1]
    partials = jnp.concatenate(
        [
            jnp.dot(row_block, w_gate, preferred_element_type=jnp.float32),
            jnp.dot(row_block, w_up, preferred_element_type=jnp.float32),
        ],
        axis=1,
    ).astype(jnp.bfloat16)
    partner_part = partner(partials, "ep", 0)
    pair_sum = partials.astype(jnp.float32) + partner_part.astype(jnp.float32)
    other_pair = partner(pair_sum, "ep", 1)
    summed = pair_sum + other_pair
    hidden = (jax.nn.silu(summed[:, :proj_width]) * summed[:, proj_width:]).astype(jnp.bfloat16)
    return jnp.dot(hidden, w_down, preferred_element_type=jnp.float32).astype(jnp.bfloat16)


def backward_expert(row_block, grad_block, w_gate, w_up, w_down):
    proj_width = w_gate.shape[1]
    partials = jnp.concatenate(
        [
            jnp.dot(row_block, w_gate, preferred_element_type=jnp.float32),
            jnp.dot(row_block, w_up, preferred_element_type=jnp.float32),
        ],
        axis=1,
    ).astype(jnp.bfloat16)
    grad_part = contract_cols(grad_block, w_down).astype(jnp.bfloat16)
    partner_part, partner_grad = partner((partials, grad_part), "ep", 0)
    pair_sum = partials.astype(jnp.float32) + partner_part.astype(jnp.float32)
    pair_grad = grad_part.astype(jnp.float32) + partner_grad.astype(jnp.float32)
    other_sum, other_grad = partner((pair_sum, pair_grad), "ep", 1)
    summed = pair_sum + other_sum
    grad_hidden = pair_grad + other_grad
    gate_value = summed[:, :proj_width]
    up_value = summed[:, proj_width:]
    sigmoid_value = jax.nn.sigmoid(gate_value)
    grad_gate = (
        grad_hidden * up_value * sigmoid_value * (1.0 + gate_value * (1.0 - sigmoid_value))
    ).astype(jnp.bfloat16)
    grad_up = (grad_hidden * gate_value * sigmoid_value).astype(jnp.bfloat16)
    result = contract_cols(grad_gate, w_gate) + contract_cols(grad_up, w_up)
    return result.astype(jnp.bfloat16)


def on_device(
    fwd_tokens,
    fwd_routes,
    fwd_gates,
    bwd_tokens,
    bwd_grads,
    bwd_routes,
    bwd_gates,
    gate_proj,
    up_proj,
    down_proj,
):
    expert_count = lax.axis_size("ep") // 4
    tokens_fwd = fwd_tokens[0]
    tok_count = tokens_fwd.shape[0]
    route_width = fwd_routes.shape[2]
    slot_cap = 3 * tok_count * route_width // (2 * expert_count)
    places_fwd = slot_places(fwd_routes[0], expert_count, slot_cap)
    places_bwd = slot_places(bwd_routes[0], expert_count, slot_cap)
    send_fwd = device_rows(spread_rows(places_fwd, tokens_fwd))
    send_rows = device_rows(spread_rows(places_bwd, bwd_tokens[0]))
    slot_gate = jnp.einsum("tkec,tk->ec", places_bwd, bwd_gates[0], precision=lax.Precision.HIGHEST)
    send_grads = device_rows(spread_rows(places_bwd, bwd_grads[0]) * slot_gate[:, None, :, None])
    recv_fwd = lax.all_to_all(send_fwd, "ep", split_axis=0, concat_axis=0, tiled=True)
    recv_rows, recv_grads = (
        lax.all_to_all(send_rows, "ep", split_axis=0, concat_axis=0, tiled=True),
        lax.all_to_all(send_grads, "ep", split_axis=0, concat_axis=0, tiled=True),
    )
    quarter_width = send_fwd.shape[2]
    w_gate = gate_proj[0, 0]
    w_up = up_proj[0, 0]
    w_down = down_proj[0, 0]
    out_fwd = forward_expert(recv_fwd.reshape(-1, quarter_width), w_gate, w_up, w_down).reshape(
        recv_fwd.shape
    )
    out_bwd = backward_expert(
        recv_rows.reshape(-1, quarter_width),
        recv_grads.reshape(-1, quarter_width),
        w_gate,
        w_up,
        w_down,
    ).reshape(recv_rows.shape)
    back_fwd = lax.all_to_all(out_fwd, "ep", split_axis=0, concat_axis=0, tiled=True)
    back_bwd = lax.all_to_all(out_bwd, "ep", split_axis=0, concat_axis=0, tiled=True)
    gathered = collect(places_fwd, back_fwd)
    mixture = (
        jnp.sum(gathered * fwd_gates[0][:, :, None, None], axis=1)
        .reshape(tok_count, -1)
        .astype(jnp.bfloat16)
    )
    grad_input = (
        jnp.sum(collect(places_bwd, back_bwd), axis=1).reshape(tok_count, -1).astype(jnp.bfloat16)
    )
    handed_forward = shifted(mixture[None], "pp", 1)
    handed_backward = shifted(grad_input[None], "pp", -1)
    return (handed_forward, handed_backward)


def solution(mesh):
    return jax.shard_map(
        on_device,
        mesh=mesh,
        in_specs=(
            P("pp", "ep", None),
            P("pp", "ep", None),
            P("pp", "ep", None),
            P("pp", "ep", None),
            P("pp", "ep", None),
            P("pp", "ep", None),
            P("pp", "ep", None),
            P("pp", "ep", None, None),
            P("pp", "ep", None, None),
            P("pp", "ep", None, None),
        ),
        out_specs=(P("pp", "ep", None), P("pp", "ep", None)),
        check_vma=False,
    )
```

profile of v0, /device:TPU:14, one launch (start us, length us, event | category | flops | bytes accessed | tf_op | source)
XLA Modules:
  0.0 461.1 jit_solution(14516132628490501383)
XLA Ops:
  6.6 6.2 %all-to-all-start.3 = ((bf16[16,48,1024]{2,1,0:T(8,128)(2,1)}), bf16[16,48,1024]{2,1,0:T(8,128)(2,1)}, u32[]{:S(2)}, u32[]{:S(2)}) async-start(bf16[16,48,1024]{2,1,0:T(8,128)(2,1)} %bitcast.30), calls=%async_computation.3 | async-start | bytes 3145728 | tf_op jit(solution)/shard_map/all_to_all | solution.py:139
  15.2 2.1 convolution_convert_fusion.2
  17.3 31.6 %all-to-all-done.3 = bf16[16,48,1024]{2,1,0:T(8,128)(2,1)} async-done(((bf16[16,48,1024]{2,1,0:T(8,128)(2,1)}), bf16[16,48,1024]{2,1,0:T(8,128)(2,1)}, u32[]{:S(2)}, u32[]{:S(2)}) %all-to-all-start.3) | async-done | bytes 1572896 | tf_op jit(solution)/shard_map/all_to_all | solution.py:139
  49.0 5.1 %all-to-all-start = ((bf16[16,48,1024]{2,1,0:T(8,128)(2,1)}), bf16[16,48,1024]{2,1,0:T(8,128)(2,1)}, u32[]{:S(2)}, u32[]{:S(2)}) async-start(bf16[16,48,1024]{2,1,0:T(8,128)(2,1)} %bitcast.5), calls=%async_computation | async-start | bytes 3145728 | tf_op jit(solution)/shard_map/all_to_all | solution.py:137
  54.0 3.3 fusion.25
  57.3 2.8 fusion.31
  62.2 2.6 reshape_squeeze.10
  65.2 3.4 multiply_convert_fusion
  68.6 21.6 %all-to-all-done = bf16[16,48,1024]{2,1,0:T(8,128)(2,1)} async-done(((bf16[16,48,1024]{2,1,0:T(8,128)(2,1)}), bf16[16,48,1024]{2,1,0:T(8,128)(2,1)}, u32[]{:S(2)}, u32[]{:S(2)}) %all-to-all-start) | async-done | bytes 1572896 | tf_op jit(solution)/shard_map/all_to_all | solution.py:137
  90.2 5.1 %all-to-all-start.2 = ((bf16[16,48,1024]{2,1,0:T(8,128)(2,1)}), bf16[16,48,1024]{2,1,0:T(8,128)(2,1)}, u32[]{:S(2)}, u32[]{:S(2)}) async-start(bf16[16,48,1024]{2,1,0:T(8,128)(2,1)} %bitcast.110), calls=%async_computation.2 | async-start | bytes 3145728 | tf_op jit(solution)/shard_map/all_to_all | solution.py:140
  95.2 4.8 %convert_add_fusion = f32[768,1536]{0,1:T(8,128)} fusion(bf16[768,1536]{0,1:T(8,128)(2,1)} %collective-permute-done.5, bf16[768,768]{0,1:T(8,128)(2,1)} %copy-done.2, bf16[768,768]{0,1:T(8,128)(2,1)S(1)} %fusion.25), kind=kLoop, calls=%fused_computation.2 | loop fusion | flops 7077888 | bytes 9437184 | tf_op jit(solution)/shard_map/add | solution.py:98
  100.6 2.9 fusion.22
  103.4 3.3 fusion.28
  108.5 22.9 %all-to-all-done.2 = bf16[16,48,1024]{2,1,0:T(8,128)(2,1)} async-done(((bf16[16,48,1024]{2,1,0:T(8,128)(2,1)}), bf16[16,48,1024]{2,1,0:T(8,128)(2,1)}, u32[]{:S(2)}, u32[]{:S(2)}) %all-to-all-start.2) | async-done | bytes 1572896 | tf_op jit(solution)/shard_map/all_to_all | solution.py:140
  131.5 3.3 fusion.34
  135.5 2.5 collective-permute-done.3
  138.3 4.5 convert_add_fusion.1
  144.7 70.8 %collective-permute-done.6 = f32[768,1536]{0,1:T(8,128)} collective-permute-done((f32[768,1536]{0,1:T(8,128)}, f32[768,1536]{0,1:T(8,128)}, u32[]{:S(2)}, u32[]{:S(2)}) %collective-permute-start.6) | collective-permute-done | bytes 4718624 | tf_op jit(solution)/shard_map/ppermute | solution.py:14
  215.5 3.7 fusion.80
  219.2 46.7 %collective-permute-done.4 = f32[768,768]{0,1:T(8,128)S(1)} collective-permute-done((f32[768,768]{0,1:T(8,128)S(1)}, f32[768,768]{0,1:T(8,128)S(1)}, u32[]{:S(2)}, u32[]{:S(2)}) %collective-permute-start.4) | collective-permute-done | bytes 2359328 | tf_op jit(solution)/shard_map/ppermute | solution.py:14
  267.9 3.6 add_convert_fusion
  271.4 6.2 %all-to-all-start.4 = ((bf16[16,48,1024]{2,1,0:T(8,128)(2,1)}), bf16[16,48,1024]{2,1,0:T(8,128)(2,1)}, u32[]{:S(2)}, u32[]{:S(2)}) async-start(bf16[16,48,1024]{2,1,0:T(8,128)(2,1)} %bitcast.111), calls=%async_computation.4 | async-start | bytes 3145728 | tf_op jit(solution)/shard_map/all_to_all | solution.py:157
  277.6 102.2 %collective-permute-done.1 = f32[768,1536]{0,1:T(8,128)} collective-permute-done((f32[768,1536]{0,1:T(8,128)}, f32[768,1536]{0,1:T(8,128)}, u32[]{:S(2)}, u32[]{:S(2)}) %collective-permute-start.1) | collective-permute-done | bytes 4718624 | tf_op jit(solution)/shard_map/ppermute | solution.py:14
  379.8 3.7 fusion.79
  383.5 2.6 convolution_convert_fusion.1
  386.2 6.1 %all-to-all-start.1 = ((bf16[16,48,1024]{2,1,0:T(8,128)(2,1)}), bf16[16,48,1024]{2,1,0:T(8,128)(2,1)S(1)}, u32[]{:S(2)}, u32[]{:S(2)}) async-start(bf16[16,48,1024]{2,1,0:T(8,128)(2,1)} %bitcast.10), calls=%async_computation.1 | async-start | bytes 3145728 | tf_op jit(solution)/shard_map/all_to_all | solution.py:156
  392.2 3.8 copy.47
  396.0 2.9 dot_general.60
  400.3 3.4 collective-permute-start.7
  403.7 24.6 %all-to-all-done.1 = bf16[16,48,1024]{2,1,0:T(8,128)(2,1)S(1)} async-done(((bf16[16,48,1024]{2,1,0:T(8,128)(2,1)}), bf16[16,48,1024]{2,1,0:T(8,128)(2,1)S(1)}, u32[]{:S(2)}, u32[]{:S(2)}) %all-to-all-start.1) | async-done | bytes 1572896 | tf_op jit(solution)/shard_map/all_to_all | solution.py:156
  431.4 26.1 %collective-permute-done.2 = bf16[1,128,4096]{1,2,0:T(8,128)(2,1)S(1)} collective-permute-done((bf16[1,128,4096]{1,2,0:T(8,128)(2,1)}, bf16[1,128,4096]{1,2,0:T(8,128)(2,1)S(1)}, u32[]{:S(2)}, u32[]{:S(2)}) %collective-permute-start.2) | collective-permute-done | bytes 1048608 | tf_op jit(solution)/shard_map/ppermute | solution.py:20
  458.8 2.3 copy.49
  (65 shorter events, 23.6 us)
Async XLA Ops:
  0.6 56.7 %copy-start = (bf16[1,1,1024,768]{3,2,1,0:T(8,128)(2,1)S(1)}, bf16[1,1,1024,768]{3,2,1,0:T(8,128)(2,1)}, u32[]{:S(2)}) copy-start(bf16[1,1,1024,768]{3,2,1,0:T(8,128)(2,1)} %param.18) | copy-start | bytes 4718596
  4.5 8.4 %copy-start.10 = (s32[1,128,1]{1,2,0:T(1,128)S(1)}, s32[1,128,1]{1,2,0:T(1,128)}, u32[]{:S(2)}) copy-start(s32[1,128,1]{1,2,0:T(1,128)} %param.11) | copy-start | bytes 1540
  6.6 42.4 %all-to-all-start.3 = ((bf16[16,48,1024]{2,1,0:T(8,128)(2,1)}), bf16[16,48,1024]{2,1,0:T(8,128)(2,1)}, u32[]{:S(2)}, u32[]{:S(2)}) async-start(bf16[16,48,1024]{2,1,0:T(8,128)(2,1)} %bitcast.30), calls=%async_computation.3 | async-start | bytes 3145728 | tf_op jit(solution)/shard_map/all_to_all | solution.py:139
  49.0 41.2 %all-to-all-start = ((bf16[16,48,1024]{2,1,0:T(8,128)(2,1)}), bf16[16,48,1024]{2,1,0:T(8,128)(2,1)}, u32[]{:S(2)}, u32[]{:S(2)}) async-start(bf16[16,48,1024]{2,1,0:T(8,128)(2,1)} %bitcast.5), calls=%async_computation | async-start | bytes 3145728 | tf_op jit(solution)/shard_map/all_to_all | solution.py:137
  60.2 1.8 copy-start.2
  60.2 4.6 copy-start.15
  62.0 33.2 %collective-permute-start.5 = (bf16[768,1536]{0,1:T(8,128)(2,1)}, bf16[768,1536]{0,1:T(8,128)(2,1)}, u32[]{:S(2)}, u32[]{:S(2)}) collective-permute-start(bf16[768,1536]{0,1:T(8,128)(2,1)} %pad_maximum_fusion.1), channel_id=1, source_target_pairs={{0,1},{1,0},{2,3},{3,2},{4,5},{5,4},{6,7},{7,6},{8,9},{9,8},{10,11... | collective-permute-start | bytes 7077896 | tf_op jit(solution)/shard_map/ppermute | solution.py:14
  90.2 41.3 %all-to-all-start.2 = ((bf16[16,48,1024]{2,1,0:T(8,128)(2,1)}), bf16[16,48,1024]{2,1,0:T(8,128)(2,1)}, u32[]{:S(2)}, u32[]{:S(2)}) async-start(bf16[16,48,1024]{2,1,0:T(8,128)(2,1)} %bitcast.110), calls=%async_computation.2 | async-start | bytes 3145728 | tf_op jit(solution)/shard_map/all_to_all | solution.py:140
  95.2 5.3 %copy-start.12 = (bf16[1,1,1024,768]{3,2,1,0:T(8,128)(2,1)S(1)}, bf16[1,1,1024,768]{3,2,1,0:T(8,128)(2,1)}, u32[]{:S(2)}) copy-start(bf16[1,1,1024,768]{3,2,1,0:T(8,128)(2,1)} %param.17) | copy-start | bytes 4718596
  100.0 115.5 %collective-permute-start.6 = (f32[768,1536]{0,1:T(8,128)}, f32[768,1536]{0,1:T(8,128)}, u32[]{:S(2)}, u32[]{:S(2)}) collective-permute-start(f32[768,1536]{0,1:T(8,128)} %convert_add_fusion), channel_id=1, source_target_pairs={{0,2},{2,0},{1,3},{3,1},{4,6},{6,4},{5,7},{7,5},{8,10},{10,8},{9,1... | collective-permute-start | bytes 14155784 | tf_op jit(solution)/shard_map/ppermute | solution.py:14
  103.4 3.3 copy-start.4
  106.7 1.8 copy-start.7
  108.5 29.8 %collective-permute-start = (bf16[768,1536]{0,1:T(8,128)(2,1)}, bf16[768,1536]{0,1:T(8,128)(2,1)}, u32[]{:S(2)}, u32[]{:S(2)}) collective-permute-start(bf16[768,1536]{0,1:T(8,128)(2,1)} %pad_maximum_fusion), channel_id=1, source_target_pairs={{0,1},{1,0},{2,3},{3,2},{4,5},{5,4},{6,7},{7,6},{8,9},{9,8},{10,11... | collective-permute-start | bytes 7077896 | tf_op jit(solution)/shard_map/ppermute | solution.py:14
  134.8 3.5 copy-start.5
  134.8 3.5 copy-start.8
  134.8 3.1 collective-permute-start.3
  138.2 77.3 %copy-start.3 = (bf16[768,768]{0,1:T(8,128)(2,1)S(1)}, bf16[768,768]{0,1:T(8,128)(2,1)}, u32[]{:S(2)}) copy-start(bf16[768,768]{0,1:T(8,128)(2,1)} %copy-done.2) | copy-start | bytes 3538948
  138.2 127.7 %collective-permute-start.4 = (f32[768,768]{0,1:T(8,128)S(1)}, f32[768,768]{0,1:T(8,128)S(1)}, u32[]{:S(2)}, u32[]{:S(2)}) collective-permute-start(f32[768,768]{0,1:T(8,128)S(1)} %convert_add_fusion.2), channel_id=1, source_target_pairs={{0,2},{2,0},{1,3},{3,1},{4,6},{6,4},{5,7},{7,5},{8,10},{10,8},{9,1... | collective-permute-start | bytes 7077896 | tf_op jit(solution)/shard_map/ppermute | solution.py:14
  142.8 237.0 %collective-permute-start.1 = (f32[768,1536]{0,1:T(8,128)}, f32[768,1536]{0,1:T(8,128)}, u32[]{:S(2)}, u32[]{:S(2)}) collective-permute-start(f32[768,1536]{0,1:T(8,128)} %convert_add_fusion.1), channel_id=1, source_target_pairs={{0,2},{2,0},{1,3},{3,1},{4,6},{6,4},{5,7},{7,5},{8,10},{10,8},{9,1... | collective-permute-start | bytes 14155784 | tf_op jit(solution)/shard_map/ppermute | solution.py:14
  219.2 48.6 %copy-start.13 = (bf16[1,1,1024,768]{3,2,1,0:T(8,128)(2,1)S(1)}, bf16[1,1,1024,768]{3,2,1,0:T(8,128)(2,1)}, u32[]{:S(2)}) copy-start(bf16[1,1,1024,768]{3,2,1,0:T(8,128)(2,1)} %param.17) | copy-start | bytes 4718596
  271.4 108.4 %copy-start.6 = (bf16[768,768]{0,1:T(8,128)(2,1)S(1)}, bf16[768,768]{0,1:T(8,128)(2,1)}, u32[]{:S(2)}) copy-start(bf16[768,768]{0,1:T(8,128)(2,1)} %copy-done.4) | copy-start | bytes 3538948
  271.4 108.4 %copy-start.9 = (bf16[768,768]{0,1:T(8,128)(2,1)S(1)}, bf16[768,768]{0,1:T(8,128)(2,1)}, u32[]{:S(2)}) copy-start(bf16[768,768]{0,1:T(8,128)(2,1)} %copy-done.7) | copy-start | bytes 3538948
  271.4 114.8 %all-to-all-start.4 = ((bf16[16,48,1024]{2,1,0:T(8,128)(2,1)}), bf16[16,48,1024]{2,1,0:T(8,128)(2,1)}, u32[]{:S(2)}, u32[]{:S(2)}) async-start(bf16[16,48,1024]{2,1,0:T(8,128)(2,1)} %bitcast.111), calls=%async_computation.4 | async-start | bytes 3145728 | tf_op jit(solution)/shard_map/all_to_all | solution.py:157
  277.6 106.0 %copy-start.14 = (bf16[1,1,768,1024]{3,2,1,0:T(8,128)(2,1)S(1)}, bf16[1,1,768,1024]{3,2,1,0:T(8,128)(2,1)}, u32[]{:S(2)}) copy-start(bf16[1,1,768,1024]{3,2,1,0:T(8,128)(2,1)} %param.19) | copy-start | bytes 4718596
  386.2 42.1 %all-to-all-start.1 = ((bf16[16,48,1024]{2,1,0:T(8,128)(2,1)}), bf16[16,48,1024]{2,1,0:T(8,128)(2,1)S(1)}, u32[]{:S(2)}, u32[]{:S(2)}) async-start(bf16[16,48,1024]{2,1,0:T(8,128)(2,1)} %bitcast.10), calls=%async_computation.1 | async-start | bytes 3145728 | tf_op jit(solution)/shard_map/all_to_all | solution.py:156
  396.0 32.3 %copy-start.11 = (f32[1,128,1]{1,2,0:T(1,128)S(1)}, f32[1,128,1]{1,2,0:T(1,128)}, u32[]{:S(2)}) copy-start(f32[1,128,1]{1,2,0:T(1,128)} %param.12) | copy-start | bytes 1540
  400.3 31.1 %collective-permute-start.7 = (bf16[1,128,4096]{2,1,0:T(8,128)(2,1)}, bf16[1,128,4096]{2,1,0:T(8,128)(2,1)}, u32[]{:S(2)}, u32[]{:S(2)}) collective-permute-start(bf16[1,128,4096]{2,1,0:T(8,128)(2,1)} %fusion.1), channel_id=1, source_target_pairs={{16,0},{17,1},{18,2},{19,3},{20,4},{21,5},{22,6},{23,7},{24,8},{25... | collective-permute-start | bytes 3145736 | tf_op jit(solution)/shard_map/ppermute | solution.py:20
  428.8 32.4 %copy-start.1 = (bf16[1,1,1024,768]{3,2,1,0:T(8,128)(2,1)S(1)}, bf16[1,1,1024,768]{3,2,1,0:T(8,128)(2,1)}, u32[]{:S(2)}) copy-start(bf16[1,1,1024,768]{3,2,1,0:T(8,128)(2,1)} %param.18) | copy-start | bytes 4718596
  430.1 27.4 %collective-permute-start.2 = (bf16[1,128,4096]{1,2,0:T(8,128)(2,1)}, bf16[1,128,4096]{1,2,0:T(8,128)(2,1)S(1)}, u32[]{:S(2)}, u32[]{:S(2)}) collective-permute-start(bf16[1,128,4096]{1,2,0:T(8,128)(2,1)} %bitcast.112), channel_id=1, source_target_pairs={{0,16},{1,17},{2,18},{3,19},{4,20},{5,21},{6,22},{7,23},{8,24},{9,... | collective-permute-start | bytes 3145736 | tf_op jit(solution)/shard_map/ppermute | solution.py:20
where the time goes:
time: 462 us; the launch traced here: 461 us
  waiting for transfers between devices  349 us (76%)
  starting transfers between devices  36.6 us (8%)
  matrix products  33.6 us (7%)
  other arithmetic  22.6 us (5%)
  local copies, waits for them, and re-layouts  18.3 us (4%)
    ppermute x6, waiting for transfers between devices, partner(): return lax.ppermute(block, axis, route)  222 us
    all_to_all x1, waiting for transfers between devices, on_device(): lax.all_to_all(send_rows, 'ep', split_axis=0, concat_axis=0, tiled=True)  31.6 us
    ppermute x2, waiting for transfers between devices, shifted(): return lax.ppermute(shard, axis, pairs)  26.2 us
    all_to_all x1, waiting for transfers between devices, on_device(): lax.all_to_all(out_fwd, 'ep', split_axis=0, concat_axis=0, tiled=True)  24.6 us
    all_to_all x1, waiting for transfers between devices, on_device(): lax.all_to_all(send_grads, 'ep', split_axis=0, concat_axis=0, tiled=True)  22.9 us
    all_to_all x1, waiting for transfers between devices, on_device(): lax.all_to_all(send_fwd, 'ep', split_axis=0, concat_axis=0, tiled=True)  21.6 us
  transfers between devices with their start and end apart: 13, of which 9 were waited for; matrix products, arithmetic and copies ran while one was open for 14% of the time, Pallas kernels for 0%

commit v1 on v0

v1 whole, which is shorter than its diff:
```python
import functools

import jax
import jax.numpy as jnp
from jax import lax
from jax.experimental import pallas as pl
from jax.experimental.pallas import tpu as pltpu
from jax.sharding import PartitionSpec as P

QUARTERS = 4


def paired(block, distance):
    count = lax.axis_size("ep")
    return lax.ppermute(block, "ep", [(i, i ^ distance) for i in range(count)])


def handed(block, by, distance):
    sections, count = lax.axis_size("pp"), lax.axis_size("ep")
    route = [
        (s * count + i, (s + by) * count + (i ^ distance))
        for s in range(sections)
        if 0 <= s + by < sections
        for i in range(count)
    ]
    return lax.ppermute(block, ("pp", "ep"), route)


def quarters_of(weight):
    across = paired(weight, 2)
    return [weight, paired(weight, 1), across, paired(across, 1)]


def slot_rows(route_row, expert, slot_cap):
    count = route_row.shape[1]
    named = route_row == expert
    low = lax.broadcasted_iota(jnp.int32, (count, count), 0)
    high = lax.broadcasted_iota(jnp.int32, (count, count), 1)
    earlier = jnp.where(low < high, 1.0, 0.0).astype(jnp.bfloat16)
    hits = jnp.broadcast_to(jnp.where(named, 1.0, 0.0), (8, count)).astype(jnp.bfloat16)
    place = jnp.dot(hits, earlier, preferred_element_type=jnp.float32)[:1]
    slots = lax.broadcasted_iota(jnp.int32, (slot_cap, count), 0)
    taken = (slots == place.astype(jnp.int32)) & named
    return jnp.where(taken, 1.0, 0.0).astype(jnp.bfloat16)


def spread_kernel(slot_cap, experts, scaled, where_ref, route_ref, *refs):
    if scaled:
        gate_ref, refs = refs[0], refs[1:]
    value_ref, out_refs = refs[0], refs[1:]
    values = value_ref[...]
    if scaled:
        values = (values.astype(jnp.float32) * gate_ref[...]).astype(jnp.bfloat16)
    for distance in range(experts):
        chosen = slot_rows(route_ref[...], where_ref[0] ^ distance, slot_cap)
        out_refs[distance][...] = jnp.dot(
            chosen, values, preferred_element_type=jnp.float32
        ).astype(jnp.bfloat16)


def spread(where, route_row, values, slot_cap, experts, gates=None):
    tokens, width = values.shape
    quarter = width // QUARTERS
    whole = lambda *shape: pl.BlockSpec(shape, lambda j, where: (0, 0))
    in_specs = [whole(1, tokens)]
    args = [route_row]
    if gates is not None:
        in_specs.append(whole(tokens, 1))
        args.append(gates)
    in_specs.append(pl.BlockSpec((tokens, quarter), lambda j, where: (0, where[1] ^ j)))
    args.append(values)
    return pl.pallas_call(
        functools.partial(spread_kernel, slot_cap, experts, gates is not None),
        grid_spec=pltpu.PrefetchScalarGridSpec(
            num_scalar_prefetch=1,
            grid=(QUARTERS,),
            in_specs=in_specs,
            out_specs=[pl.BlockSpec((slot_cap, quarter), lambda j, where: (0, j))] * experts,
        ),
        out_shape=[jax.ShapeDtypeStruct((slot_cap, width), jnp.bfloat16)] * experts,
        cost_estimate=pl.CostEstimate(
            flops=2 * experts * slot_cap * tokens * width,
            bytes_accessed=2 * width * (tokens + experts * slot_cap),
            transcendentals=0,
        ),
    )(where, *args)


def collect_kernel(slot_cap, experts, scaled, where_ref, route_ref, *refs):
    if scaled:
        gate_ref, refs = refs[0], refs[1:]
    block_refs, out_ref = refs[:-1], refs[-1]
    total = None
    for distance in range(experts):
        chosen = slot_rows(route_ref[...], where_ref[0] ^ distance, slot_cap)
        part = lax.dot_general(
            chosen,
            block_refs[distance][...],
            (((0,), (0,)), ((), ())),
            preferred_element_type=jnp.float32,
        )
        total = part if total is None else total + part
    if scaled:
        total = total * gate_ref[...]
    out_ref[...] = total.astype(jnp.bfloat16)


def collect(where, route_row, blocks, gates=None):
    tokens = route_row.shape[1]
    experts = len(blocks)
    slot_cap, width = blocks[0].shape
    quarter = width // QUARTERS
    whole = lambda *shape: pl.BlockSpec(shape, lambda j, where: (0, 0))
    in_specs = [whole(1, tokens)]
    args = [route_row]
    if gates is not None:
        in_specs.append(whole(tokens, 1))
        args.append(gates)
    in_specs += [pl.BlockSpec((slot_cap, quarter), lambda j, where: (0, j))] * experts
    return pl.pallas_call(
        functools.partial(collect_kernel, slot_cap, experts, gates is not None),
        grid_spec=pltpu.PrefetchScalarGridSpec(
            num_scalar_prefetch=1,
            grid=(QUARTERS,),
            in_specs=in_specs,
            out_specs=pl.BlockSpec((tokens, quarter), lambda j, where: (0, where[1] ^ j)),
        ),
        out_shape=jax.ShapeDtypeStruct((tokens, width), jnp.bfloat16),
        cost_estimate=pl.CostEstimate(
            flops=2 * experts * slot_cap * tokens * width,
            bytes_accessed=2 * width * (tokens + experts * slot_cap),
            transcendentals=0,
        ),
    )(where, *args, *blocks)


def rows_times(rows, mats):
    quarter = mats[0].shape[0]
    total = None
    for j, mat in enumerate(mats):
        part = jnp.dot(
            rows[:, j * quarter : (j + 1) * quarter], mat, preferred_element_type=jnp.float32
        )
        total = part if total is None else total + part
    return total


def contract_cols(left, right):
    return lax.dot_general(
        left, right, (((1,), (1,)), ((), ())), preferred_element_type=jnp.float32
    )


def on_device(
    fwd_tokens,
    fwd_routes,
    fwd_gates,
    bwd_tokens,
    bwd_grads,
    bwd_routes,
    bwd_gates,
    gate_proj,
    up_proj,
    down_proj,
):
    experts = lax.axis_size("ep") // QUARTERS
    tokens = fwd_tokens.shape[1]
    slot_cap = 3 * tokens // (2 * experts)
    me = lax.axis_index("ep")
    where = jnp.stack([me // QUARTERS, me % QUARTERS]).astype(jnp.int32)
    fwd_row = fwd_routes[0].reshape(1, tokens)
    bwd_row = bwd_routes[0].reshape(1, tokens)

    gate_mats = quarters_of(gate_proj[0, 0])
    up_mats = quarters_of(up_proj[0, 0])
    down_mats = quarters_of(down_proj[0, 0])

    def exchanged(blocks):
        return [blocks[0]] + [
            paired(blocks[distance], QUARTERS * distance) for distance in range(1, experts)
        ]

    fwd_blocks = exchanged(spread(where, fwd_row, fwd_tokens[0], slot_cap, experts))
    bwd_blocks = exchanged(spread(where, bwd_row, bwd_tokens[0], slot_cap, experts))
    grad_blocks = exchanged(
        spread(where, bwd_row, bwd_grads[0], slot_cap, experts, gates=bwd_gates[0])
    )

    fwd_meta = handed(
        jnp.concatenate([fwd_row.astype(jnp.float32), fwd_gates[0].reshape(1, tokens)]), 1, 0
    )
    bwd_meta = handed(bwd_row.astype(jnp.float32), -1, 0)

    rows = jnp.concatenate(fwd_blocks)
    gate_value, up_value = rows_times(rows, gate_mats), rows_times(rows, up_mats)
    hidden = (jax.nn.silu(gate_value) * up_value).astype(jnp.bfloat16)
    fwd_out = jnp.concatenate(
        [
            jnp.dot(hidden, mat, preferred_element_type=jnp.float32).astype(jnp.bfloat16)
            for mat in down_mats
        ],
        axis=1,
    )

    rows = jnp.concatenate(bwd_blocks)
    gate_value, up_value = rows_times(rows, gate_mats), rows_times(rows, up_mats)
    grads = jnp.concatenate(grad_blocks)
    quarter = down_mats[0].shape[1]
    grad_hidden = sum(
        contract_cols(grads[:, j * quarter : (j + 1) * quarter], mat)
        for j, mat in enumerate(down_mats)
    )
    sigmoid_value = jax.nn.sigmoid(gate_value)
    grad_gate = (
        grad_hidden * up_value * sigmoid_value * (1.0 + gate_value * (1.0 - sigmoid_value))
    ).astype(jnp.bfloat16)
    grad_up = (grad_hidden * gate_value * sigmoid_value).astype(jnp.bfloat16)
    bwd_out = jnp.concatenate(
        [
            (contract_cols(grad_gate, g) + contract_cols(grad_up, u)).astype(jnp.bfloat16)
            for g, u in zip(gate_mats, up_mats)
        ],
        axis=1,
    )

    def returned(out, by):
        return [
            handed(out[d * slot_cap : (d + 1) * slot_cap], by, QUARTERS * d)
            for d in range(experts)
        ]

    fwd_back = returned(fwd_out, 1)
    bwd_back = returned(bwd_out, -1)
    handed_forward = collect(
        where,
        fwd_meta[:1].astype(jnp.int32),
        fwd_back,
        gates=fwd_meta[1:].reshape(tokens, 1),
    )
    handed_backward = collect(where, bwd_meta.astype(jnp.int32), bwd_back)
    return handed_forward[None], handed_backward[None]


def solution(mesh):
    return jax.shard_map(
        on_device,
        mesh=mesh,
        in_specs=(P("pp", "ep", None),) * 7 + (P("pp", "ep", None, None),) * 3,
        out_specs=(P("pp", "ep", None), P("pp", "ep", None)),
        check_vma=False,
    )
```

time: 462 us -> 284 us (0.61)
  waiting for transfers between devices: 349 us -> 180 us
  Pallas kernels: 0 us -> 30.4 us
  other arithmetic: 22.6 us -> 3.23 us
  starting transfers between devices: 36.6 us -> 29 us
  matrix products: 33.6 us -> 26.5 us
  local copies, waits for them, and re-layouts: 18.3 us -> 12.2 us
    all_to_all x5 -> x0, waiting for transfers between devices: 101 us -> none  [the longest x1 31.6 us: on_device(): lax.all_to_all(send_rows, 'ep', split_axis=0, concat_axis=0, tiled=True)]
    ppermute x8 -> x28, waiting for transfers between devices: 248 us -> 180 us  [the longest x18 139 us: paired(): return lax.ppermute(block, 'ep', [(i, i ^ distance) for i in range(count)])]
    pallas_call x0 -> x5, Pallas kernels: none -> 30.4 us  [the longest x3 17.2 us: spread(): pl.pallas_call(functools.partial(spread_kernel, slot_cap, experts, gates...]
    all_to_all x5 -> x0, starting transfers between devices: 28.6 us -> none  [the longest x1 6.24 us: on_device(): lax.all_to_all(send_rows, 'ep', split_axis=0, concat_axis=0, tiled=True)]
    ppermute x8 -> x28, starting transfers between devices: 8.05 us -> 29 us  [the longest x10 17.9 us: handed(): return lax.ppermute(block, ('pp', 'ep'), route)]
    add x5 -> x0, other arithmetic: 16.9 us -> none  [the longest x1 4.76 us: backward_expert(): pair_sum = partials.astype(jnp.float32) + partner_part.astype(jnp.float32)]
    dot_general x11 -> x20, matrix products: 24.9 us -> 15.6 us  [the longest x16 13.7 us: rows_times(): jnp.dot(rows[:, j * quarter:(j + 1) * quarter], mat, preferred_element_ty...]
    another operation x3 -> x0, local copies, waits for them, and re-layouts: 6.37 us -> none  [spread_rows(): values.reshape(tok_count, 4, quarter_width)]
  transfers between devices with their start and end apart: 13 -> 28, of which waited for: 9 -> 13; matrix products, arithmetic and copies ran while one was open for 14% -> 14% of each run, Pallas kernels for 0% -> 8%
where the time goes in v1:
time: 284 us; the launch traced here: 282 us
  waiting for transfers between devices  180 us (63%)
  Pallas kernels  30.4 us (11%)
  starting transfers between devices  29 us (10%)
  matrix products  26.5 us (9%)
  local copies, waits for them, and re-layouts  12.2 us (4%)
  other arithmetic  3.23 us (1%)
    ppermute x18, waiting for transfers between devices, paired(): return lax.ppermute(block, 'ep', [(i, i ^ distance) for i in range(count)])  139 us
    ppermute x10, waiting for transfers between devices, handed(): return lax.ppermute(block, ('pp', 'ep'), route)  40.4 us
    ppermute x10, starting transfers between devices, handed(): return lax.ppermute(block, ('pp', 'ep'), route)  17.9 us
    pallas_call x3, Pallas kernels, spread(): pl.pallas_call(functools.partial(spread_kernel, slot_cap, experts, gates...  17.2 us
    dot_general x16, matrix products, rows_times(): jnp.dot(rows[:, j * quarter:(j + 1) * quarter], mat, preferred_element_ty...  13.7 us
    pallas_call x2, Pallas kernels, collect(): pl.pallas_call(functools.partial(collect_kernel, slot_cap, experts, gates...  13.1 us
    ppermute x18, starting transfers between devices, paired(): return lax.ppermute(block, 'ep', [(i, i ^ distance) for i in range(count)])  11.1 us
    dot_general x12, matrix products, contract_cols(): lax.dot_general(left, right, (((1,), (1,)), ((), ())), preferred_element_...  10.9 us
  transfers between devices with their start and end apart: 28, of which 13 were waited for; matrix products, arithmetic and copies ran while one was open for 14% of the time, Pallas kernels for 8%

profile of v1, /device:TPU:14, one launch (start us, length us, event | category | flops | bytes accessed | tf_op | source)
XLA Modules:
  0.0 282.1 jit_solution(6728885887252061206)
XLA Ops:
  4.9 5.7 %shard_map.115 = (bf16[48,4096]{1,0:T(8,128)(2,1)}, bf16[48,4096]{1,0:T(8,128)(2,1)}, bf16[48,4096]{1,0:T(8,128)(2,1)}, bf16[48,4096]{1,0:T(8,128)(2,1)}) custom-call(s32[2]{0:T(128)} %pad_add_fusion.where_ref, s32[1,128]{1,0:T(1,128)} %bitcast.81, f32[128,1]{1,0:T(8,128)} %copy.13.refs_0_, bf16[128,4096]{1,0:T(8,128)(2,1)} %bitcast.78), custom_call_target="tpu_custom_call" | custom-call | flops 201326592 | bytes 2621440 | tf_op jit(solution)/shard_map/pallas_call | solution.py:72
  12.4 1.8 constant_dynamic-update-slice_fusion.7
  14.2 5.8 %shard_map.113 = (bf16[48,4096]{1,0:T(8,128)(2,1)}, bf16[48,4096]{1,0:T(8,128)(2,1)}, bf16[48,4096]{1,0:T(8,128)(2,1)}, bf16[48,4096]{1,0:T(8,128)(2,1)}) custom-call(s32[2]{0:T(128)} %pad_add_fusion.where_ref, s32[1,128]{1,0:T(1,128)} %bitcast.83, bf16[128,4096]{1,0:T(8,128)(2,1)} %bitcast.79), custom_call_target="tpu_custom_call" | custom-call | flops 201326592 | bytes 2621440 | tf_op jit(solution)/shard_map/pallas_call | solution.py:72
  21.8 5.7 %shard_map.116 = (bf16[48,4096]{1,0:T(8,128)(2,1)}, bf16[48,4096]{1,0:T(8,128)(2,1)}, bf16[48,4096]{1,0:T(8,128)(2,1)}, bf16[48,4096]{1,0:T(8,128)(2,1)}) custom-call(s32[2]{0:T(128)} %pad_add_fusion.where_ref, s32[1,128]{1,0:T(1,128)} %bitcast.82, bf16[128,4096]{1,0:T(8,128)(2,1)} %bitcast.80), custom_call_target="tpu_custom_call" | custom-call | flops 201326592 | bytes 2621440 | tf_op jit(solution)/shard_map/pallas_call | solution.py:72
  28.8 2.6 collective-permute-start.19
  32.2 16.3 %collective-permute-done.19 = bf16[48,4096]{1,0:T(8,128)(2,1)S(1)} collective-permute-done((bf16[48,4096]{1,0:T(8,128)(2,1)}, bf16[48,4096]{1,0:T(8,128)(2,1)S(1)}, u32[]{:S(2)}, u32[]{:S(2)}) %collective-permute-start.19) | collective-permute-done | bytes 393248 | tf_op jit(solution)/shard_map/ppermute | solution.py:15
  49.6 17.3 %collective-permute-done.20 = bf16[48,4096]{1,0:T(8,128)(2,1)S(1)} collective-permute-done((bf16[48,4096]{1,0:T(8,128)(2,1)S(1)}, bf16[48,4096]{1,0:T(8,128)(2,1)S(1)}, u32[]{:S(2)}, u32[]{:S(2)}) %collective-permute-start.20) | collective-permute-done | bytes 393248 | tf_op jit(solution)/shard_map/ppermute | solution.py:15
  67.7 8.4 %collective-permute-done.1 = bf16[48,4096]{1,0:T(8,128)(2,1)S(1)} collective-permute-done((bf16[48,4096]{1,0:T(8,128)(2,1)S(1)}, bf16[48,4096]{1,0:T(8,128)(2,1)S(1)}, u32[]{:S(2)}, u32[]{:S(2)}) %collective-permute-start.1) | collective-permute-done | bytes 393248 | tf_op jit(solution)/shard_map/ppermute | solution.py:15
  76.1 2.2 collective-permute-start.2
  78.3 15.6 %collective-permute-done.2 = bf16[48,4096]{1,0:T(8,128)(2,1)S(1)} collective-permute-done((bf16[48,4096]{1,0:T(8,128)(2,1)S(1)}, bf16[48,4096]{1,0:T(8,128)(2,1)S(1)}, u32[]{:S(2)}, u32[]{:S(2)}) %collective-permute-start.2) | collective-permute-done | bytes 393248 | tf_op jit(solution)/shard_map/ppermute | solution.py:15
  94.2 18.2 %collective-permute-done.3 = bf16[48,4096]{1,0:T(8,128)(2,1)S(1)} collective-permute-done((bf16[48,4096]{1,0:T(8,128)(2,1)S(1)}, bf16[48,4096]{1,0:T(8,128)(2,1)S(1)}, u32[]{:S(2)}, u32[]{:S(2)}) %collective-permute-start.3) | collective-permute-done | bytes 393248 | tf_op jit(solution)/shard_map/ppermute | solution.py:15
  112.4 9.1 %collective-permute-done.21 = bf16[48,4096]{1,0:T(8,128)(2,1)S(1)} collective-permute-done((bf16[48,4096]{1,0:T(8,128)(2,1)S(1)}, bf16[48,4096]{1,0:T(8,128)(2,1)S(1)}, u32[]{:S(2)}, u32[]{:S(2)}) %collective-permute-start.21) | collective-permute-done | bytes 393248 | tf_op jit(solution)/shard_map/ppermute | solution.py:15
  123.1 15.4 %collective-permute-done.22 = bf16[48,4096]{1,0:T(8,128)(2,1)S(1)} collective-permute-done((bf16[48,4096]{1,0:T(8,128)(2,1)S(1)}, bf16[48,4096]{1,0:T(8,128)(2,1)S(1)}, u32[]{:S(2)}, u32[]{:S(2)}) %collective-permute-start.22) | collective-permute-done | bytes 393248 | tf_op jit(solution)/shard_map/ppermute | solution.py:15
  138.6 18.2 %collective-permute-done.23 = bf16[48,4096]{1,0:T(8,128)(2,1)S(1)} collective-permute-done((bf16[48,4096]{1,0:T(8,128)(2,1)S(1)}, bf16[48,4096]{1,0:T(8,128)(2,1)S(1)}, u32[]{:S(2)}, u32[]{:S(2)}) %collective-permute-start.23) | collective-permute-done | bytes 393248 | tf_op jit(solution)/shard_map/ppermute | solution.py:15
  158.4 2.4 collective-permute-start.17
  160.8 1.9 fusion.23
  162.7 1.9 fusion.35
  168.5 1.9 fusion.21
  171.0 2.0 fusion.37
  173.0 20.7 %collective-permute-done.11 = bf16[768,1024]{1,0:T(8,128)(2,1)S(1)} collective-permute-done((bf16[768,1024]{1,0:T(8,128)(2,1)S(1)}, bf16[768,1024]{1,0:T(8,128)(2,1)S(1)}, u32[]{:S(2)}, u32[]{:S(2)}) %collective-permute-start.11) | collective-permute-done | bytes 1572896 | tf_op jit(solution)/shard_map/ppermute | solution.py:15
  202.1 2.1 fusion.57
  205.5 2.1 fusion.2
  209.2 2.7 collective-permute-start.27
  211.9 2.1 collective-permute-start.26
  214.0 2.0 collective-permute-start.25
  217.7 2.1 collective-permute-start.24
  222.0 20.8 %collective-permute-done.27.refs_3_ = bf16[48,4096]{1,0:T(8,128)(2,1)S(1)} collective-permute-done((bf16[48,4096]{1,0:T(8,128)(2,1)S(1)}, bf16[48,4096]{1,0:T(8,128)(2,1)S(1)}, u32[]{:S(2)}, u32[]{:S(2)}) %collective-permute-start.27) | collective-permute-done | bytes 393248 | tf_op jit(solution)/shard_map/ppermute | solution.py:26
  244.1 7.1 %collective-permute-done.26.refs_2_ = bf16[48,4096]{1,0:T(8,128)(2,1)} collective-permute-done((bf16[48,4096]{1,0:T(8,128)(2,1)S(1)}, bf16[48,4096]{1,0:T(8,128)(2,1)}, u32[]{:S(2)}, u32[]{:S(2)}) %collective-permute-start.26) | collective-permute-done | bytes 393248 | tf_op jit(solution)/shard_map/ppermute | solution.py:26
  255.6 6.5 %shard_map.117 = bf16[128,4096]{1,0:T(8,128)(2,1)} custom-call(s32[2]{0:T(128)} %pad_add_fusion.where_ref, s32[1,128]{1,0:T(1,128)} %convert_element_type.69.route_ref, bf16[48,4096]{1,0:T(8,128)(2,1)} %collective-permute-done.24.refs_0_, bf16[48,4096]{1,0:T(8,128)(2,1)} %collective-permute-done.25.refs_1_, ...), custom_call_target="tpu_custom_call" | custom-call | flops 201326592 | bytes 2621440 | tf_op jit(solution)/shard_map/pallas_call | solution.py:120
  262.2 4.2 %collective-permute-done.14.refs_2_ = bf16[48,4096]{1,0:T(8,128)(2,1)S(1)} collective-permute-done((bf16[48,4096]{1,0:T(8,128)(2,1)S(1)}, bf16[48,4096]{1,0:T(8,128)(2,1)S(1)}, u32[]{:S(2)}, u32[]{:S(2)}) %collective-permute-start.14) | collective-permute-done | bytes 393248 | tf_op jit(solution)/shard_map/ppermute | solution.py:26
  266.4 8.3 %collective-permute-done.13.refs_1_ = bf16[48,4096]{1,0:T(8,128)(2,1)S(1)} collective-permute-done((bf16[48,4096]{1,0:T(8,128)(2,1)S(1)}, bf16[48,4096]{1,0:T(8,128)(2,1)S(1)}, u32[]{:S(2)}, u32[]{:S(2)}) %collective-permute-start.13) | collective-permute-done | bytes 393248 | tf_op jit(solution)/shard_map/ppermute | solution.py:26
  275.5 6.6 %shard_map.114 = bf16[128,4096]{1,0:T(8,128)(2,1)} custom-call(s32[2]{0:T(128)} %pad_add_fusion.where_ref, s32[1,128]{1,0:T(1,128)} %get-tuple-element.35.route_ref, f32[128,1]{1,0:T(8,128)} %copy.12.refs_0_, bf16[48,4096]{1,0:T(8,128)(2,1)} %copy-done.9, bf16[48,4096]{1,0:T(8,128)(2,1)} %copy-done.8, bf16[48,4096]{1,0:T(8,128)(2,1)} %copy-done.7, ...), custom_call_target="tpu_custom_call" | custom-call | flops 201326592 | bytes 2621440 | tf_op jit(solution)/shard_map/pallas_call | solution.py:120
  (121 shorter events, 41.2 us)
Async XLA Ops:
  0.6 156.2 %collective-permute-start.7 = (bf16[1024,768]{1,0:T(8,128)(2,1)}, bf16[1024,768]{1,0:T(8,128)(2,1)S(1)}, u32[]{:S(2)}, u32[]{:S(2)}) collective-permute-start(bf16[1024,768]{1,0:T(8,128)(2,1)} %bitcast.70), channel_id=1, source_target_pairs={{0,1},{1,0},{2,3},{3,2},{4,5},{5,4},{6,7},{7,6},{8,9},{9,8},{10,11... | collective-permute-start | bytes 4718600 | tf_op jit(solution)/shard_map/ppermute | solution.py:15
  0.7 157.7 %collective-permute-start.8 = (bf16[1024,768]{1,0:T(8,128)(2,1)}, bf16[1024,768]{1,0:T(8,128)(2,1)}, u32[]{:S(2)}, u32[]{:S(2)}) collective-permute-start(bf16[1024,768]{1,0:T(8,128)(2,1)} %bitcast.71), channel_id=1, source_target_pairs={{0,2},{1,3},{2,0},{3,1},{4,6},{5,7},{6,4},{7,5},{8,10},{9,11},{10,... | collective-permute-start | bytes 4718600 | tf_op jit(solution)/shard_map/ppermute | solution.py:15
  1.3 163.3 %collective-permute-start.4 = (bf16[1024,768]{1,0:T(8,128)(2,1)}, bf16[1024,768]{1,0:T(8,128)(2,1)S(1)}, u32[]{:S(2)}, u32[]{:S(2)}) collective-permute-start(bf16[1024,768]{1,0:T(8,128)(2,1)} %bitcast.72), channel_id=1, source_target_pairs={{0,1},{1,0},{2,3},{3,2},{4,5},{5,4},{6,7},{7,6},{8,9},{9,8},{10,11... | collective-permute-start | bytes 4718600 | tf_op jit(solution)/shard_map/ppermute | solution.py:15
  1.5 167.0 %collective-permute-start.5 = (bf16[1024,768]{1,0:T(8,128)(2,1)}, bf16[1024,768]{1,0:T(8,128)(2,1)}, u32[]{:S(2)}, u32[]{:S(2)}) collective-permute-start(bf16[1024,768]{1,0:T(8,128)(2,1)} %bitcast.73), channel_id=1, source_target_pairs={{0,2},{1,3},{2,0},{3,1},{4,6},{5,7},{6,4},{7,5},{8,10},{9,11},{10,... | collective-permute-start | bytes 4718600 | tf_op jit(solution)/shard_map/ppermute | solution.py:15
  10.7 18.1 %collective-permute-start.18 = (bf16[48,4096]{1,0:T(8,128)(2,1)}, bf16[48,4096]{1,0:T(8,128)(2,1)S(1)}, u32[]{:S(2)}, u32[]{:S(2)}) collective-permute-start(bf16[48,4096]{1,0:T(8,128)(2,1)} %get-tuple-element.19), channel_id=1, source_target_pairs={{0,4},{1,5},{2,6},{3,7},{4,0},{5,1},{6,2},{7,3},{8,12},{9,13},{10,... | collective-permute-start | bytes 1179656 | tf_op jit(solution)/shard_map/ppermute | solution.py:15
  28.7 65.1 %copy-start.14 = (bf16[48,4096]{1,0:T(8,128)(2,1)S(1)}, bf16[48,4096]{1,0:T(8,128)(2,1)}, u32[]{:S(2)}) copy-start(bf16[48,4096]{1,0:T(8,128)(2,1)} %get-tuple-element.17) | copy-start | bytes 1179652
  28.8 19.7 %collective-permute-start.19 = (bf16[48,4096]{1,0:T(8,128)(2,1)}, bf16[48,4096]{1,0:T(8,128)(2,1)S(1)}, u32[]{:S(2)}, u32[]{:S(2)}) collective-permute-start(bf16[48,4096]{1,0:T(8,128)(2,1)} %get-tuple-element.20), channel_id=1, source_target_pairs={{0,8},{1,9},{2,10},{3,11},{4,12},{5,13},{6,14},{7,15},{8,0},{9,1},... | collective-permute-start | bytes 1179656 | tf_op jit(solution)/shard_map/ppermute | solution.py:15
  48.5 63.9 %copy-start.13 = (bf16[48,4096]{1,0:T(8,128)(2,1)S(1)}, bf16[48,4096]{1,0:T(8,128)(2,1)}, u32[]{:S(2)}) copy-start(bf16[48,4096]{1,0:T(8,128)(2,1)} %get-tuple-element.23) | copy-start | bytes 1179652
  48.5 18.4 %collective-permute-start.20 = (bf16[48,4096]{1,0:T(8,128)(2,1)S(1)}, bf16[48,4096]{1,0:T(8,128)(2,1)S(1)}, u32[]{:S(2)}, u32[]{:S(2)}) collective-permute-start(bf16[48,4096]{1,0:T(8,128)(2,1)S(1)} %copy-done.16), channel_id=1, source_target_pairs={{0,12},{1,13},{2,14},{3,15},{4,8},{5,9},{6,10},{7,11},{8,4},{9,5},... | collective-permute-start | bytes 1179656 | tf_op jit(solution)/shard_map/ppermute | solution.py:15
  66.9 9.2 %collective-permute-start.1 = (bf16[48,4096]{1,0:T(8,128)(2,1)S(1)}, bf16[48,4096]{1,0:T(8,128)(2,1)S(1)}, u32[]{:S(2)}, u32[]{:S(2)}) collective-permute-start(bf16[48,4096]{1,0:T(8,128)(2,1)S(1)} %copy-done.17), channel_id=1, source_target_pairs={{0,4},{1,5},{2,6},{3,7},{4,0},{5,1},{6,2},{7,3},{8,12},{9,13},{10,... | collective-permute-start | bytes 1179656 | tf_op jit(solution)/shard_map/ppermute | solution.py:15
  76.1 62.4 %copy-start.11 = (bf16[48,4096]{1,0:T(8,128)(2,1)S(1)}, bf16[48,4096]{1,0:T(8,128)(2,1)}, u32[]{:S(2)}) copy-start(bf16[48,4096]{1,0:T(8,128)(2,1)} %get-tuple-element.25) | copy-start | bytes 1179652
  76.1 17.8 %collective-permute-start.2 = (bf16[48,4096]{1,0:T(8,128)(2,1)S(1)}, bf16[48,4096]{1,0:T(8,128)(2,1)S(1)}, u32[]{:S(2)}, u32[]{:S(2)}) collective-permute-start(bf16[48,4096]{1,0:T(8,128)(2,1)S(1)} %copy-done.15), channel_id=1, source_target_pairs={{0,8},{1,9},{2,10},{3,11},{4,12},{5,13},{6,14},{7,15},{8,0},{9,1},... | collective-permute-start | bytes 1179656 | tf_op jit(solution)/shard_map/ppermute | solution.py:15
  93.9 62.9 %copy-start.3 = (bf16[1,1,768,1024]{3,2,1,0:T(8,128)(2,1)S(1)}, bf16[1,1,768,1024]{3,2,1,0:T(8,128)(2,1)}, u32[]{:S(2)}) copy-start(bf16[1,1,768,1024]{3,2,1,0:T(8,128)(2,1)} %param.19) | copy-start | bytes 4718596
  93.9 18.5 %collective-permute-start.3 = (bf16[48,4096]{1,0:T(8,128)(2,1)S(1)}, bf16[48,4096]{1,0:T(8,128)(2,1)S(1)}, u32[]{:S(2)}, u32[]{:S(2)}) collective-permute-start(bf16[48,4096]{1,0:T(8,128)(2,1)S(1)} %copy-done.14), channel_id=1, source_target_pairs={{0,12},{1,13},{2,14},{3,15},{4,8},{5,9},{6,10},{7,11},{8,4},{9,5},... | collective-permute-start | bytes 1179656 | tf_op jit(solution)/shard_map/ppermute | solution.py:15
  112.4 9.2 %collective-permute-start.21 = (bf16[48,4096]{1,0:T(8,128)(2,1)S(1)}, bf16[48,4096]{1,0:T(8,128)(2,1)S(1)}, u32[]{:S(2)}, u32[]{:S(2)}) collective-permute-start(bf16[48,4096]{1,0:T(8,128)(2,1)S(1)} %copy-done.13), channel_id=1, source_target_pairs={{0,4},{1,5},{2,6},{3,7},{4,0},{5,1},{6,2},{7,3},{8,12},{9,13},{10,... | collective-permute-start | bytes 1179656 | tf_op jit(solution)/shard_map/ppermute | solution.py:15
  121.6 16.9 %collective-permute-start.22 = (bf16[48,4096]{1,0:T(8,128)(2,1)S(1)}, bf16[48,4096]{1,0:T(8,128)(2,1)S(1)}, u32[]{:S(2)}, u32[]{:S(2)}) collective-permute-start(bf16[48,4096]{1,0:T(8,128)(2,1)S(1)} %copy-done.12), channel_id=1, source_target_pairs={{0,8},{1,9},{2,10},{3,11},{4,12},{5,13},{6,14},{7,15},{8,0},{9,1},... | collective-permute-start | bytes 1179656 | tf_op jit(solution)/shard_map/ppermute | solution.py:15
  138.5 18.3 %collective-permute-start.23 = (bf16[48,4096]{1,0:T(8,128)(2,1)S(1)}, bf16[48,4096]{1,0:T(8,128)(2,1)S(1)}, u32[]{:S(2)}, u32[]{:S(2)}) collective-permute-start(bf16[48,4096]{1,0:T(8,128)(2,1)S(1)} %copy-done.11), channel_id=1, source_target_pairs={{0,12},{1,13},{2,14},{3,15},{4,8},{5,9},{6,10},{7,11},{8,4},{9,5},... | collective-permute-start | bytes 1179656 | tf_op jit(solution)/shard_map/ppermute | solution.py:15
  156.8 38.6 %collective-permute-start.10 = (bf16[768,1024]{1,0:T(8,128)(2,1)S(1)}, bf16[768,1024]{1,0:T(8,128)(2,1)S(1)}, u32[]{:S(2)}, u32[]{:S(2)}) collective-permute-start(bf16[768,1024]{1,0:T(8,128)(2,1)S(1)} %bitcast.74), channel_id=1, source_target_pairs={{0,1},{1,0},{2,3},{3,2},{4,5},{5,4},{6,7},{7,6},{8,9},{9,8},{10,11... | collective-permute-start | bytes 4718600 | tf_op jit(solution)/shard_map/ppermute | solution.py:15
  156.8 36.9 %collective-permute-start.11 = (bf16[768,1024]{1,0:T(8,128)(2,1)S(1)}, bf16[768,1024]{1,0:T(8,128)(2,1)S(1)}, u32[]{:S(2)}, u32[]{:S(2)}) collective-permute-start(bf16[768,1024]{1,0:T(8,128)(2,1)S(1)} %bitcast.75), channel_id=1, source_target_pairs={{0,2},{1,3},{2,0},{3,1},{4,6},{5,7},{6,4},{7,5},{8,10},{9,11},{10,... | collective-permute-start | bytes 4718600 | tf_op jit(solution)/shard_map/ppermute | solution.py:15
  158.4 59.2 %collective-permute-start.17 = (f32[1,128]{1,0:T(1,128)S(1)}, f32[1,128]{1,0:T(1,128)S(1)}, u32[]{:S(2)}, u32[]{:S(2)}) collective-permute-start(f32[1,128]{1,0:T(1,128)S(1)} %bitcast_convert_fusion), channel_id=1, source_target_pairs={{16,0},{17,1},{18,2},{19,3},{20,4},{21,5},{22,6},{23,7},{24,8},{25... | collective-permute-start | bytes 1544 | tf_op jit(solution)/shard_map/ppermute | solution.py:26
  164.6 56.1 %collective-permute-start = (f32[2,128]{1,0:T(2,128)S(1)}, f32[2,128]{1,0:T(2,128)S(1)}, u32[]{:S(2)}, u32[]{:S(2)}) collective-permute-start(f32[2,128]{1,0:T(2,128)S(1)} %pad_maximum_fusion.2), channel_id=1, source_target_pairs={{0,16},{1,17},{2,18},{3,19},{4,20},{5,21},{6,22},{7,23},{8,24},{9,... | collective-permute-start | bytes 3080 | tf_op jit(solution)/shard_map/ppermute | solution.py:26
  170.4 27.0 %collective-permute-start.6 = (bf16[1024,768]{1,0:T(8,128)(2,1)}, bf16[1024,768]{1,0:T(8,128)(2,1)S(1)}, u32[]{:S(2)}, u32[]{:S(2)}) collective-permute-start(bf16[1024,768]{1,0:T(8,128)(2,1)} %collective-permute-done.5), channel_id=1, source_target_pairs={{0,1},{1,0},{2,3},{3,2},{4,5},{5,4},{6,7},{7,6},{8,9},{9,8},{10,11... | collective-permute-start | bytes 4718600 | tf_op jit(solution)/shard_map/ppermute | solution.py:15
  193.7 4.2 %collective-permute-start.9 = (bf16[1024,768]{1,0:T(8,128)(2,1)}, bf16[1024,768]{1,0:T(8,128)(2,1)S(1)}, u32[]{:S(2)}, u32[]{:S(2)}) collective-permute-start(bf16[1024,768]{1,0:T(8,128)(2,1)} %collective-permute-done.8), channel_id=1, source_target_pairs={{0,1},{1,0},{2,3},{3,2},{4,5},{5,4},{6,7},{7,6},{8,9},{9,8},{10,11... | collective-permute-start | bytes 4718600 | tf_op jit(solution)/shard_map/ppermute | solution.py:15
  195.4 4.0 %collective-permute-start.12 = (bf16[768,1024]{1,0:T(8,128)(2,1)S(1)}, bf16[768,1024]{1,0:T(8,128)(2,1)S(1)}, u32[]{:S(2)}, u32[]{:S(2)}) collective-permute-start(bf16[768,1024]{1,0:T(8,128)(2,1)S(1)} %collective-permute-done.11), channel_id=1, source_target_pairs={{0,1},{1,0},{2,3},{3,2},{4,5},{5,4},{6,7},{7,6},{8,9},{9,8},{10,11... | collective-permute-start | bytes 4718600 | tf_op jit(solution)/shard_map/ppermute | solution.py:15
  209.2 33.6 %collective-permute-start.27 = (bf16[48,4096]{1,0:T(8,128)(2,1)S(1)}, bf16[48,4096]{1,0:T(8,128)(2,1)S(1)}, u32[]{:S(2)}, u32[]{:S(2)}) collective-permute-start(bf16[48,4096]{1,0:T(8,128)(2,1)S(1)} %get-tuple-element.26), channel_id=1, source_target_pairs={{16,12},{17,13},{18,14},{19,15},{20,8},{21,9},{22,10},{23,11},{24,... | collective-permute-start | bytes 1179656 | tf_op jit(solution)/shard_map/ppermute | solution.py:26
  211.9 39.2 %collective-permute-start.26 = (bf16[48,4096]{1,0:T(8,128)(2,1)S(1)}, bf16[48,4096]{1,0:T(8,128)(2,1)}, u32[]{:S(2)}, u32[]{:S(2)}) collective-permute-start(bf16[48,4096]{1,0:T(8,128)(2,1)S(1)} %get-tuple-element.27), channel_id=1, source_target_pairs={{16,8},{17,9},{18,10},{19,11},{20,12},{21,13},{22,14},{23,15},{24,... | collective-permute-start | bytes 1179656 | tf_op jit(solution)/shard_map/ppermute | solution.py:26
  214.0 38.4 %collective-permute-start.25 = (bf16[48,4096]{1,0:T(8,128)(2,1)S(1)}, bf16[48,4096]{1,0:T(8,128)(2,1)}, u32[]{:S(2)}, u32[]{:S(2)}) collective-permute-start(bf16[48,4096]{1,0:T(8,128)(2,1)S(1)} %get-tuple-element.28), channel_id=1, source_target_pairs={{16,4},{17,5},{18,6},{19,7},{20,0},{21,1},{22,2},{23,3},{24,12},{2... | collective-permute-start | bytes 1179656 | tf_op jit(solution)/shard_map/ppermute | solution.py:26
  217.7 37.9 %collective-permute-start.24 = (bf16[48,4096]{1,0:T(8,128)(2,1)S(1)}, bf16[48,4096]{1,0:T(8,128)(2,1)}, u32[]{:S(2)}, u32[]{:S(2)}) collective-permute-start(bf16[48,4096]{1,0:T(8,128)(2,1)S(1)} %get-tuple-element.29), channel_id=1, source_target_pairs={{16,0},{17,1},{18,2},{19,3},{20,4},{21,5},{22,6},{23,7},{24,8},{25... | collective-permute-start | bytes 1179656 | tf_op jit(solution)/shard_map/ppermute | solution.py:26
  220.7 41.4 %collective-permute-start.16 = (bf16[48,4096]{1,0:T(8,128)(2,1)}, bf16[48,4096]{1,0:T(8,128)(2,1)S(1)}, u32[]{:S(2)}, u32[]{:S(2)}) collective-permute-start(bf16[48,4096]{1,0:T(8,128)(2,1)} %get-tuple-element.30), channel_id=1, source_target_pairs={{0,28},{1,29},{2,30},{3,31},{4,24},{5,25},{6,26},{7,27},{8,20},{9,... | collective-permute-start | bytes 1179656 | tf_op jit(solution)/shard_map/ppermute | solution.py:26
  242.8 19.3 %collective-permute-start.15 = (bf16[48,4096]{1,0:T(8,128)(2,1)}, bf16[48,4096]{1,0:T(8,128)(2,1)S(1)}, u32[]{:S(2)}, u32[]{:S(2)}) collective-permute-start(bf16[48,4096]{1,0:T(8,128)(2,1)} %get-tuple-element.31), channel_id=1, source_target_pairs={{0,24},{1,25},{2,26},{3,27},{4,28},{5,29},{6,30},{7,31},{8,16},{9,... | collective-permute-start | bytes 1179656 | tf_op jit(solution)/shard_map/ppermute | solution.py:26
  251.2 15.2 %collective-permute-start.14 = (bf16[48,4096]{1,0:T(8,128)(2,1)S(1)}, bf16[48,4096]{1,0:T(8,128)(2,1)S(1)}, u32[]{:S(2)}, u32[]{:S(2)}) collective-permute-start(bf16[48,4096]{1,0:T(8,128)(2,1)S(1)} %get-tuple-element.32), channel_id=1, source_target_pairs={{0,20},{1,21},{2,22},{3,23},{4,16},{5,17},{6,18},{7,19},{8,28},{9,... | collective-permute-start | bytes 1179656 | tf_op jit(solution)/shard_map/ppermute | solution.py:26
  252.5 22.2 %collective-permute-start.13 = (bf16[48,4096]{1,0:T(8,128)(2,1)S(1)}, bf16[48,4096]{1,0:T(8,128)(2,1)S(1)}, u32[]{:S(2)}, u32[]{:S(2)}) collective-permute-start(bf16[48,4096]{1,0:T(8,128)(2,1)S(1)} %get-tuple-element.33), channel_id=1, source_target_pairs={{0,16},{1,17},{2,18},{3,19},{4,20},{5,21},{6,22},{7,23},{8,24},{9,... | collective-permute-start | bytes 1179656 | tf_op jit(solution)/shard_map/ppermute | solution.py:26
  (14 other events, 320.0 us)

commit v2 on v1

v2 whole, which is shorter than its diff:
```python
import functools

import jax
import jax.numpy as jnp
from jax import lax
from jax.experimental import pallas as pl
from jax.experimental.pallas import tpu as pltpu
from jax.sharding import PartitionSpec as P

QUARTERS = 4


def after(block, *done):
    return lax.optimization_barrier((block, *done))[0] if done else block


def paired(block, distance, *done):
    block = after(block, *done)
    count = lax.axis_size("ep")
    return lax.ppermute(block, "ep", [(i, i ^ distance) for i in range(count)])


def handed(block, steps, distance):
    sections, count = lax.axis_size("pp"), lax.axis_size("ep")
    route = [
        (s * count + i, (s + by) * count + (i ^ distance))
        for s in range(sections)
        for by in steps
        if 0 <= s + by < sections
        for i in range(count)
    ]
    return lax.ppermute(block, ("pp", "ep"), route)


def slot_matrix(route, expert_of, slot_cap, experts):
    count = route.shape[1]
    named = [route == expert_of(distance) for distance in range(experts)]
    hits = [jnp.where(one, 1.0, 0.0) for one in named]
    hits += [jnp.zeros_like(hits[0])] * (-experts % 8)
    low = lax.broadcasted_iota(jnp.int32, (count, count), 0)
    high = lax.broadcasted_iota(jnp.int32, (count, count), 1)
    earlier = jnp.where(low < high, 1.0, 0.0).astype(jnp.bfloat16)
    place = jnp.dot(
        jnp.concatenate(hits).astype(jnp.bfloat16), earlier, preferred_element_type=jnp.float32
    ).astype(jnp.int32)
    slots = lax.broadcasted_iota(jnp.int32, (slot_cap, count), 0)
    return jnp.concatenate(
        [jnp.where((slots == place[d : d + 1]) & named[d], 1.0, 0.0) for d in range(experts)]
    )


def spread_kernel(slot_cap, experts, where_ref, fwd_ref, bwd_ref, gate_ref, *refs):
    value_refs, out_refs = refs[:3], refs[3:]
    quarter = value_refs[0].shape[1] // QUARTERS
    fwd_slots, bwd_slots = [
        slot_matrix(ref[...], lambda d: where_ref[0] ^ d, slot_cap, experts)
        for ref in (fwd_ref, bwd_ref)
    ]
    slot_gate = jnp.sum(bwd_slots * gate_ref[...], axis=1, keepdims=True)
    fwd_slots, bwd_slots = fwd_slots.astype(jnp.bfloat16), bwd_slots.astype(jnp.bfloat16)
    for at, chosen in enumerate((fwd_slots, bwd_slots, bwd_slots)):
        for j in range(QUARTERS):
            start = pl.multiple_of((where_ref[1] ^ j) * quarter, quarter)
            values = value_refs[at][:, pl.ds(start, quarter)]
            rows = jnp.dot(chosen, values, preferred_element_type=jnp.float32)
            if at == 2:
                rows = rows * slot_gate
            for d in range(experts):
                out_refs[at * experts + d][:, j * quarter : (j + 1) * quarter] = rows[
                    d * slot_cap : (d + 1) * slot_cap
                ].astype(jnp.bfloat16)


def spread(where, fwd_routes, bwd_routes, gates, values, slot_cap, experts):
    tokens, width = values[0].shape
    args = [*(row.reshape(1, tokens) for row in (fwd_routes, bwd_routes, gates)), *values]
    out_count = experts * len(values)
    vmem = pl.BlockSpec(memory_space=pltpu.VMEM)
    out = pl.pallas_call(
        functools.partial(spread_kernel, slot_cap, experts),
        in_specs=[pl.BlockSpec(memory_space=pltpu.SMEM)] + [vmem] * len(args),
        out_specs=[vmem] * out_count,
        out_shape=[jax.ShapeDtypeStruct((slot_cap, width), jnp.bfloat16)] * out_count,
        cost_estimate=pl.CostEstimate(
            flops=2 * out_count * slot_cap * tokens * width,
            bytes_accessed=2 * width * (tokens * len(values) + out_count * slot_cap),
            transcendentals=0,
        ),
    )(where, *args)
    return [out[at * experts : (at + 1) * experts] for at in range(len(values))]


def collect_kernel(slot_cap, experts, where_ref, meta_ref, *refs):
    block_refs, out_refs = refs[:experts], refs[experts:]
    tokens = meta_ref.shape[1]
    quarter = out_refs[0].shape[1] // QUARTERS
    low = lax.broadcasted_iota(jnp.int32, (tokens, tokens), 1)
    high = lax.broadcasted_iota(jnp.int32, (tokens, tokens), 0)
    route, gate = [
        jnp.sum(jnp.where(low == high, meta_ref[at : at + 1], 0.0), axis=1, keepdims=True)
        for at in range(2)
    ]
    relative = where_ref[0] ^ lax.broadcasted_iota(jnp.int32, (1, 128), 1)
    hits = jnp.where(route == relative.astype(jnp.float32), 1.0, 0.0)
    earlier = jnp.where(low < high, 1.0, 0.0).astype(jnp.bfloat16)
    place = jnp.dot(earlier, hits.astype(jnp.bfloat16), preferred_element_type=jnp.float32)
    slots = lax.broadcasted_iota(jnp.int32, (tokens, slot_cap), 1).astype(jnp.float32)
    chosen = jnp.concatenate(
        [
            jnp.where((slots == place[:, d : d + 1]) & (hits[:, d : d + 1] > 0.0), 1.0, 0.0)
            for d in range(experts)
        ],
        axis=1,
    ).astype(jnp.bfloat16)
    for j in range(QUARTERS):
        part = slice(j * quarter, (j + 1) * quarter)
        rows = jnp.concatenate([ref[:, part] for ref in block_refs])
        total = jnp.dot(chosen, rows, preferred_element_type=jnp.float32) * gate
        start = pl.multiple_of((where_ref[1] ^ j) * quarter, quarter)
        if len(out_refs) == 1:
            out_refs[0][:, pl.ds(start, quarter)] = total.astype(jnp.bfloat16)
        else:
            first = where_ref[2] == 0
            fwd, bwd = jnp.where(first, 0.0, total), jnp.where(first, total, 0.0)
            out_refs[0][:, pl.ds(start, quarter)] = fwd.astype(jnp.bfloat16)
            out_refs[1][:, pl.ds(start, quarter)] = bwd.astype(jnp.bfloat16)


def collect(where, meta, blocks, outputs):
    tokens = meta.shape[1]
    experts = len(blocks)
    slot_cap, width = blocks[0].shape
    vmem = pl.BlockSpec(memory_space=pltpu.VMEM)
    return pl.pallas_call(
        functools.partial(collect_kernel, slot_cap, experts),
        in_specs=[pl.BlockSpec(memory_space=pltpu.SMEM)] + [vmem] * (1 + experts),
        out_specs=[vmem] * outputs,
        out_shape=[jax.ShapeDtypeStruct((tokens, width), jnp.bfloat16)] * outputs,
        cost_estimate=pl.CostEstimate(
            flops=2 * experts * slot_cap * tokens * width,
            bytes_accessed=2 * width * (tokens * outputs + experts * slot_cap),
            transcendentals=0,
        ),
    )(where, meta, *blocks)


def rows_times(rows, mats):
    quarter = mats[0].shape[0]
    total = None
    for j, mat in enumerate(mats):
        part = jnp.dot(
            rows[:, j * quarter : (j + 1) * quarter], mat, preferred_element_type=jnp.float32
        )
        total = part if total is None else total + part
    return total


def contract_cols(left, right):
    return lax.dot_general(
        left, right, (((1,), (1,)), ((), ())), preferred_element_type=jnp.float32
    )


def on_device(
    fwd_tokens,
    fwd_routes,
    fwd_gates,
    bwd_tokens,
    bwd_grads,
    bwd_routes,
    bwd_gates,
    gate_proj,
    up_proj,
    down_proj,
):
    experts = lax.axis_size("ep") // QUARTERS
    tokens = fwd_tokens.shape[1]
    slot_cap = 3 * tokens // (2 * experts)
    me = lax.axis_index("ep")
    section = lax.axis_index("pp")
    where = jnp.stack([me // QUARTERS, me % QUARTERS, section]).astype(jnp.int32)

    fwd_meta = jnp.concatenate(
        [fwd_routes[0].reshape(1, tokens).astype(jnp.float32), fwd_gates[0].reshape(1, tokens)]
    )
    bwd_meta = bwd_routes[0].reshape(1, tokens).astype(jnp.float32)
    bwd_meta = jnp.concatenate([bwd_meta, jnp.ones_like(bwd_meta)])
    merged = lax.axis_size("pp") == 2
    first = section == 0
    if merged:
        metas = [handed(jnp.where(first, fwd_meta, bwd_meta), (1, -1), 0)]
    else:
        metas = [handed(fwd_meta, (1,), 0), handed(bwd_meta, (-1,), 0)]

    gate, up, down = gate_proj[0, 0], up_proj[0, 0], down_proj[0, 0]
    gate_across = paired(gate, 2)
    up_across = paired(up, 2)
    gate_beside = paired(gate, 1)
    up_beside = paired(up, 1)
    down_beside = paired(down, 1)
    fwd_spread, row_spread, grad_spread = spread(
        after(where, gate_beside),
        fwd_routes[0],
        bwd_routes[0],
        bwd_gates[0],
        (fwd_tokens[0], bwd_tokens[0], bwd_grads[0]),
        slot_cap,
        experts,
    )
    order = sorted(range(1, experts), reverse=True)
    last = order[-1]
    fwd_blocks, bwd_blocks, grad_blocks = {}, {}, {}
    for d in order:
        before = (up_beside, down_beside) if d == last else ()
        fwd_blocks[d] = paired(fwd_spread[d], QUARTERS * d, *before)
    for d in order:
        before = metas if d == last else ()
        bwd_blocks[d] = paired(row_spread[d], QUARTERS * d, fwd_blocks[d], *before)
    down_across = paired(down, 2, gate_across)
    gate_diagonal = paired(gate_across, 1, bwd_blocks[last])
    up_diagonal = paired(up_across, 1, bwd_blocks[last])
    for d in order:
        before = (gate_diagonal, up_diagonal) if d == last else (up_across,)
        grad_blocks[d] = paired(grad_spread[d], QUARTERS * d, bwd_blocks[d], *before)
    down_diagonal = paired(down_across, 1, grad_blocks[last])
    gate_mats = [gate, gate_beside, gate_across, gate_diagonal]
    up_mats = [up, up_beside, up_across, up_diagonal]
    down_mats = [down, down_beside, down_across, down_diagonal]
    fwd_blocks = [fwd_spread[0]] + [fwd_blocks[d] for d in range(1, experts)]
    bwd_blocks = [row_spread[0]] + [bwd_blocks[d] for d in range(1, experts)]
    grad_blocks = [grad_spread[0]] + [grad_blocks[d] for d in range(1, experts)]

    rows = jnp.concatenate(fwd_blocks)
    gate_value, up_value = rows_times(rows, gate_mats), rows_times(rows, up_mats)
    hidden = (jax.nn.silu(gate_value) * up_value).astype(jnp.bfloat16)
    fwd_out = jnp.concatenate(
        [
            jnp.dot(hidden, mat, preferred_element_type=jnp.float32).astype(jnp.bfloat16)
            for mat in down_mats
        ],
        axis=1,
    )

    rows = jnp.concatenate(bwd_blocks)
    gate_value, up_value = rows_times(rows, gate_mats), rows_times(rows, up_mats)
    grads = jnp.concatenate(grad_blocks)
    quarter = down_mats[0].shape[1]
    grad_hidden = sum(
        contract_cols(grads[:, j * quarter : (j + 1) * quarter], mat)
        for j, mat in enumerate(down_mats)
    )
    sigmoid_value = jax.nn.sigmoid(gate_value)
    grad_gate = (
        grad_hidden * up_value * sigmoid_value * (1.0 + gate_value * (1.0 - sigmoid_value))
    ).astype(jnp.bfloat16)
    grad_up = (grad_hidden * gate_value * sigmoid_value).astype(jnp.bfloat16)
    bwd_out = jnp.concatenate(
        [
            (contract_cols(grad_gate, g) + contract_cols(grad_up, u)).astype(jnp.bfloat16)
            for g, u in zip(gate_mats, up_mats)
        ],
        axis=1,
    )

    def returned(out, steps):
        parts = [out[d * slot_cap : (d + 1) * slot_cap] for d in range(experts)]
        back = {d: handed(parts[d], steps, QUARTERS * d) for d in reversed(range(experts))}
        return [back[d] for d in range(experts)]

    if merged:
        back = returned(jnp.where(first, fwd_out, bwd_out), (1, -1))
        handed_forward, handed_backward = collect(where, metas[0], back, 2)
    else:
        (handed_forward,) = collect(where, metas[0], returned(fwd_out, (1,)), 1)
        (handed_backward,) = collect(where, metas[1], returned(bwd_out, (-1,)), 1)
    return handed_forward[None], handed_backward[None]


def solution(mesh):
    return jax.shard_map(
        on_device,
        mesh=mesh,
        in_specs=(P("pp", "ep", None),) * 7 + (P("pp", "ep", None, None),) * 3,
        out_specs=(P("pp", "ep", None), P("pp", "ep", None)),
        check_vma=False,
    )
```

time: 284 us -> 175 us (0.62)
  waiting for transfers between devices: 180 us -> 105 us
  Pallas kernels: 30.4 us -> 8.55 us
  local copies, waits for them, and re-layouts: 12.2 us -> 5.94 us
  starting transfers between devices: 29 us -> 24.2 us
    ppermute x18, waiting for transfers between devices: 139 us -> 71.8 us  [paired(): return lax.ppermute(block, 'ep', [(i, i ^ distance) for i in range(count)])]
    pallas_call x5 -> x2, Pallas kernels: 30.4 us -> 8.55 us  [the longest x1 4.96 us: spread(): pl.pallas_call(functools.partial(spread_kernel, slot_cap, experts), in_sp...]
    ppermute x10 -> x5, starting transfers between devices: 17.9 us -> 6.42 us  [handed(): return lax.ppermute(block, ('pp', 'ep'), route)]
    ppermute x10 -> x5, waiting for transfers between devices: 40.4 us -> 33.4 us  [handed(): return lax.ppermute(block, ('pp', 'ep'), route)]
    ppermute x18, starting transfers between devices: 11.1 us -> 17.8 us  [paired(): return lax.ppermute(block, 'ep', [(i, i ^ distance) for i in range(count)])]
    dot_general x16, matrix products: 13.7 us -> 10.8 us  [rows_times(): jnp.dot(rows[:, j * quarter:(j + 1) * quarter], mat, preferred_element_ty...]
    unnamed x45 -> x35, local copies, waits for them, and re-layouts: 8.12 us -> 5.72 us
  transfers between devices with their start and end apart: 28 -> 23, of which waited for: 13 -> 10; matrix products, arithmetic and copies ran while one was open for 14% -> 12% of each run, Pallas kernels for 8% -> 3%
where the time goes in v2:
time: 175 us; the launch traced here: 173 us
  waiting for transfers between devices  105 us (60%)
  matrix products  25.3 us (14%)
  starting transfers between devices  24.2 us (14%)
  Pallas kernels  8.55 us (5%)
  local copies, waits for them, and re-layouts  5.94 us (3%)
  other arithmetic  2.37 us (1%)
    ppermute x18, waiting for transfers between devices, paired(): return lax.ppermute(block, 'ep', [(i, i ^ distance) for i in range(count)])  71.8 us
    ppermute x5, waiting for transfers between devices, handed(): return lax.ppermute(block, ('pp', 'ep'), route)  33.4 us
    ppermute x18, starting transfers between devices, paired(): return lax.ppermute(block, 'ep', [(i, i ^ distance) for i in range(count)])  17.8 us
    dot_general x12, matrix products, contract_cols(): lax.dot_general(left, right, (((1,), (1,)), ((), ())), preferred_element_...  11.1 us
    dot_general x16, matrix products, rows_times(): jnp.dot(rows[:, j * quarter:(j + 1) * quarter], mat, preferred_element_ty...  10.8 us
    ppermute x5, starting transfers between devices, handed(): return lax.ppermute(block, ('pp', 'ep'), route)  6.42 us
    unnamed x35, local copies, waits for them, and re-layouts  5.72 us
    pallas_call x1, Pallas kernels, spread(): pl.pallas_call(functools.partial(spread_kernel, slot_cap, experts), in_sp...  4.96 us
  transfers between devices with their start and end apart: 23, of which 10 were waited for; matrix products, arithmetic and copies ran while one was open for 12% of the time, Pallas kernels for 3%

profile of v2, /device:TPU:14, one launch (start us, length us, event | category | flops | bytes accessed | tf_op | source)
XLA Modules:
  0.0 172.7 jit_solution(4958598517873555111)
XLA Ops:
  4.3 1.5 collective-permute-done.1
  5.8 5.0 %shard_map.113 = (bf16[48,4096]{1,0:T(8,128)(2,1)}, bf16[48,4096]{1,0:T(8,128)(2,1)}, bf16[48,4096]{1,0:T(8,128)(2,1)}, bf16[48,4096]{1,0:T(8,128)(2,1)}, bf16[4...) custom-call(s32[3]{0:T(128)} %pad_add_fusion.where_ref, ...), custom_call_target="tpu_custom_call" | custom-call | flops 603979776 | bytes 7864320 | tf_op jit(solution)/shard_map/pallas_call | solution.py:79
  11.3 2.6 %collective-permute-start.5 = (bf16[48,4096]{1,0:T(8,128)(2,1)}, bf16[48,4096]{1,0:T(8,128)(2,1)S(1)}, u32[]{:S(2)}, u32[]{:S(2)}) collective-permute-start(bf16[48,4096]{1,0:T(8,128)(2,1)} %get-tuple-element.32), channel_id=1, source_target_pairs={{0,8},{1,9},{2,10},{3,11},{4,12},{5,13},{6,14},{7,15},{8,0},{9,1},... | collective-permute-start | bytes 1179656 | tf_op jit(solution)/shard_map/ppermute | solution.py:20
  14.3 1.0 constant_dynamic-update-slice_fusion.11
  15.3 1.0 constant_dynamic-update-slice_fusion.7
  16.4 1.0 constant_dynamic-update-slice_fusion.3
  17.4 20.9 %collective-permute-done.7 = bf16[1024,768]{1,0:T(8,128)(2,1)S(1)} collective-permute-done((bf16[1024,768]{1,0:T(8,128)(2,1)}, bf16[1024,768]{1,0:T(8,128)(2,1)S(1)}, u32[]{:S(2)}, u32[]{:S(2)}) %collective-permute-start.7) | collective-permute-done | bytes 1572896 | tf_op jit(solution)/shard_map/ppermute | solution.py:20
  38.8 1.6 collective-permute-start.12
  40.8 3.0 %collective-permute-start.15 = (bf16[48,4096]{1,0:T(8,128)(2,1)S(1)}, bf16[48,4096]{1,0:T(8,128)(2,1)S(1)}, u32[]{:S(2)}, u32[]{:S(2)}) collective-permute-start(bf16[48,4096]{1,0:T(8,128)(2,1)S(1)} %copy-done.12), channel_id=1, source_target_pairs={{0,8},{1,9},{2,10},{3,11},{4,12},{5,13},{6,14},{7,15},{8,0},{9,1},... | collective-permute-start | bytes 1179656 | tf_op jit(solution)/shard_map/ppermute | solution.py:20
  43.8 6.0 %collective-permute-done.6 = bf16[48,4096]{1,0:T(8,128)(2,1)S(1)} collective-permute-done((bf16[48,4096]{1,0:T(8,128)(2,1)}, bf16[48,4096]{1,0:T(8,128)(2,1)S(1)}, u32[]{:S(2)}, u32[]{:S(2)}) %collective-permute-start.6) | collective-permute-done | bytes 393248 | tf_op jit(solution)/shard_map/ppermute | solution.py:20
  49.8 2.7 %collective-permute-start.17 = (bf16[48,4096]{1,0:T(8,128)(2,1)S(1)}, bf16[48,4096]{1,0:T(8,128)(2,1)S(1)}, u32[]{:S(2)}, u32[]{:S(2)}) collective-permute-start(bf16[48,4096]{1,0:T(8,128)(2,1)S(1)} %copy-done.11), channel_id=1, source_target_pairs={{0,12},{1,13},{2,14},{3,15},{4,8},{5,9},{6,10},{7,11},{8,4},{9,5},... | collective-permute-start | bytes 1179656 | tf_op jit(solution)/shard_map/ppermute | solution.py:20
  53.6 1.9 %fusion.47 = f32[192,768]{1,0:T(8,128)S(1)} fusion(bf16[1024,768]{1,0:T(8,128)(2,1)} %collective-permute-done.2, bf16[192,4096]{1,0:T(8,128)(2,1)S(1)} %constant_dynamic-update-slice_fusion), kind=kOutput, calls=%fused_computation.64 | convolution fusion | flops 301989888 | bytes 2555904 | tf_op jit(solution)/shard_map/dot_general | solution.py:151
  55.5 20.3 %collective-permute-done.10 = bf16[1024,768]{1,0:T(8,128)(2,1)S(1)} collective-permute-done((bf16[1024,768]{1,0:T(8,128)(2,1)}, bf16[1024,768]{1,0:T(8,128)(2,1)S(1)}, u32[]{:S(2)}, u32[]{:S(2)}) %collective-permute-start.10) | collective-permute-done | bytes 1572896 | tf_op jit(solution)/shard_map/ppermute | solution.py:20
  76.8 2.6 %collective-permute-start.16 = (bf16[48,4096]{1,0:T(8,128)(2,1)S(1)}, bf16[48,4096]{1,0:T(8,128)(2,1)S(1)}, u32[]{:S(2)}, u32[]{:S(2)}) collective-permute-start(bf16[48,4096]{1,0:T(8,128)(2,1)S(1)} %copy-done.9), channel_id=1, source_target_pairs={{0,8},{1,9},{2,10},{3,11},{4,12},{5,13},{6,14},{7,15},{8,0},{9,1},... | collective-permute-start | bytes 1179656 | tf_op jit(solution)/shard_map/ppermute | solution.py:20
  79.4 20.9 %collective-permute-done.17 = bf16[48,4096]{1,0:T(8,128)(2,1)S(1)} collective-permute-done((bf16[48,4096]{1,0:T(8,128)(2,1)S(1)}, bf16[48,4096]{1,0:T(8,128)(2,1)S(1)}, u32[]{:S(2)}, u32[]{:S(2)}) %collective-permute-start.17) | collective-permute-done | bytes 393248 | tf_op jit(solution)/shard_map/ppermute | solution.py:20
  100.3 1.6 collective-permute-start.18
  103.5 1.9 %fusion.35 = f32[192,768]{1,0:T(8,128)S(1)} fusion(bf16[1024,768]{1,0:T(8,128)(2,1)} %collective-permute-done.2, bf16[192,4096]{1,0:T(8,128)(2,1)S(1)} %constant_dynamic-update-slice_fusion.8), kind=kOutput, calls=%fused_computation.52 | convolution fusion | flops 301989888 | bytes 2555904 | tf_op jit(solution)/shard_map/dot_general | solution.py:151
  106.0 0.8 copy-done
  107.9 0.9 copy-done.2
  109.8 1.9 %convolution_convert_fusion.2 = bf16[192,1024]{1,0:T(8,128)(2,1)S(1)} fusion(bf16[192,768]{1,0:T(8,128)(2,1)S(1)} %multiply_convert_fusion.1, bf16[768,1024]{1,0:T(8,128)(2,1)} %collective-permute-done.3), kind=kOutput, calls=%fused_computation.21 | convolution fusion | flops 302186496 | bytes 2260992 | tf_op jit(solution)/shard_map/dot_general | solution.py:238
  113.7 1.4 collective-permute-done.13
  115.2 1.0 collective-permute-done.18
  116.2 2.1 %fusion.22 = f32[192,768]{1,0:T(8,128)S(1)} fusion(bf16[768,1024]{1,0:T(8,128)(2,1)} %collective-permute-done.3, bf16[192,4096]{1,0:T(8,128)(2,1)S(1)} %constant_dynamic-update-slice_fusion.4), kind=kOutput, calls=%fused_computation.39 | convolution fusion | flops 301989888 | bytes 2555904 | tf_op jit(solution)/shard_map/dot_general | solution.py:159
  121.1 0.8 fusion.60
  122.6 2.1 %fusion.65 = f32[192,1024]{1,0:T(8,128)S(1)} fusion(bf16[192,768]{1,0:T(8,128)(2,1)S(1)} %get-tuple-element.58, bf16[1024,768]{1,0:T(8,128)(2,1)} %collective-permute-done.2), kind=kOutput, calls=%fused_computation.96 | convolution fusion | flops 301989888 | bytes 2654208 | tf_op jit(solution)/shard_map/dot_general | solution.py:159
  129.6 3.0 %collective-permute-start.20 = (bf16[48,4096]{1,0:T(8,128)(2,1)S(1)}, bf16[48,4096]{1,0:T(8,128)(2,1)S(1)}, u32[]{:S(2)}, u32[]{:S(2)}) collective-permute-start(bf16[48,4096]{1,0:T(8,128)(2,1)S(1)} %get-tuple-element.56), channel_id=1, source_target_pairs={{0,20},{1,21},{2,22},{3,23},{4,16},{5,17},{6,18},{7,19},{8,28},{9,... | collective-permute-start | bytes 1179656 | tf_op jit(solution)/shard_map/ppermute | solution.py:32
  132.6 1.0 collective-permute-start.21
  133.6 1.4 collective-permute-start.22
  135.0 22.5 %collective-permute-done.19.refs_0_ = bf16[48,4096]{1,0:T(8,128)(2,1)S(1)} collective-permute-done((bf16[48,4096]{1,0:T(8,128)(2,1)S(1)}, bf16[48,4096]{1,0:T(8,128)(2,1)S(1)}, u32[]{:S(2)}, u32[]{:S(2)}) %collective-permute-start.19) | collective-permute-done | bytes 393248 | tf_op jit(solution)/shard_map/ppermute | solution.py:32
  157.5 2.5 %collective-permute-done.21.refs_2_ = bf16[48,4096]{1,0:T(8,128)(2,1)S(1)} collective-permute-done((bf16[48,4096]{1,0:T(8,128)(2,1)S(1)}, bf16[48,4096]{1,0:T(8,128)(2,1)S(1)}, u32[]{:S(2)}, u32[]{:S(2)}) %collective-permute-start.21) | collective-permute-done | bytes 393248 | tf_op jit(solution)/shard_map/ppermute | solution.py:32
  159.9 8.4 %collective-permute-done.22.refs_3_ = bf16[48,4096]{1,0:T(8,128)(2,1)S(1)} collective-permute-done((bf16[48,4096]{1,0:T(8,128)(2,1)S(1)}, bf16[48,4096]{1,0:T(8,128)(2,1)S(1)}, u32[]{:S(2)}, u32[]{:S(2)}) %collective-permute-start.22) | collective-permute-done | bytes 393248 | tf_op jit(solution)/shard_map/ppermute | solution.py:32
  169.1 3.6 %shard_map.114 = (bf16[128,4096]{1,0:T(8,128)(2,1)}, bf16[128,4096]{1,0:T(8,128)(2,1)}) custom-call(s32[3]{0:T(128)} %pad_add_fusion.where_ref, f32[2,128]{1,0:T(2,128)} %copy-done.7, bf16[48,4096]{1,0:T(8,128)(2,1)} %copy-done.3, bf16[48,4096]{1,0:T(8,128)(2,1)} %copy-done.4, bf16[48,4096]{1,0:T(8,128)(2,1)} %copy-done.5, bf16[48,4096]{1,0:T(8,128)(2,1)} %copy-done.6), custom_call_target="tpu_custom_call" | custom-call | flops 201326592 | bytes 3670016 | tf_op jit(solution)/shard_map/pallas_call | solution.py:134
  (91 shorter events, 23.0 us)
Async XLA Ops:
  0.6 5.1 %collective-permute-start.1 = (bf16[1024,768]{1,0:T(8,128)(2,1)}, bf16[1024,768]{1,0:T(8,128)(2,1)S(1)}, u32[]{:S(2)}, u32[]{:S(2)}) collective-permute-start(bf16[1024,768]{1,0:T(8,128)(2,1)} %bitcast.71), channel_id=1, source_target_pairs={{0,1},{1,0},{2,3},{3,2},{4,5},{5,4},{6,7},{7,6},{8,9},{9,8},{10,11... | collective-permute-start | bytes 4718600 | tf_op jit(solution)/shard_map/ppermute | solution.py:20
  0.7 10.0 %collective-permute-start.2 = (bf16[1024,768]{1,0:T(8,128)(2,1)}, bf16[1024,768]{1,0:T(8,128)(2,1)}, u32[]{:S(2)}, u32[]{:S(2)}) collective-permute-start(bf16[1024,768]{1,0:T(8,128)(2,1)} %bitcast.75), channel_id=1, source_target_pairs={{0,1},{1,0},{2,3},{3,2},{4,5},{5,4},{6,7},{7,6},{8,9},{9,8},{10,11... | collective-permute-start | bytes 4718600 | tf_op jit(solution)/shard_map/ppermute | solution.py:20
  1.2 9.5 %collective-permute-start.3 = (bf16[768,1024]{1,0:T(8,128)(2,1)}, bf16[768,1024]{1,0:T(8,128)(2,1)}, u32[]{:S(2)}, u32[]{:S(2)}) collective-permute-start(bf16[768,1024]{1,0:T(8,128)(2,1)} %bitcast.73), channel_id=1, source_target_pairs={{0,1},{1,0},{2,3},{3,2},{4,5},{5,4},{6,7},{7,6},{8,9},{9,8},{10,11... | collective-permute-start | bytes 4718600 | tf_op jit(solution)/shard_map/ppermute | solution.py:20
  1.3 37.0 %collective-permute-start.7 = (bf16[1024,768]{1,0:T(8,128)(2,1)}, bf16[1024,768]{1,0:T(8,128)(2,1)S(1)}, u32[]{:S(2)}, u32[]{:S(2)}) collective-permute-start(bf16[1024,768]{1,0:T(8,128)(2,1)} %bitcast.72), channel_id=1, source_target_pairs={{0,2},{1,3},{2,0},{3,1},{4,6},{5,7},{6,4},{7,5},{8,10},{9,11},{10,... | collective-permute-start | bytes 4718600 | tf_op jit(solution)/shard_map/ppermute | solution.py:20
  3.2 35.6 %collective-permute-start = (f32[2,128]{1,0:T(2,128)S(1)}, f32[2,128]{1,0:T(2,128)S(1)}, u32[]{:S(2)}, u32[]{:S(2)}) collective-permute-start(f32[2,128]{1,0:T(2,128)S(1)} %maximum_select_fusion.1), channel_id=1, source_target_pairs={{0,16},{1,17},{2,18},{3,19},{4,20},{5,21},{6,22},{7,23},{8,24},{9,... | collective-permute-start | bytes 3080 | tf_op jit(solution)/shard_map/ppermute | solution.py:32
  10.7 28.1 %copy-start.1 = (bf16[1,1,768,1024]{3,2,1,0:T(8,128)(2,1)S(1)}, bf16[1,1,768,1024]{3,2,1,0:T(8,128)(2,1)}, u32[]{:S(2)}) copy-start(bf16[1,1,768,1024]{3,2,1,0:T(8,128)(2,1)} %param.19) | copy-start | bytes 4718596
  10.7 30.1 %copy-start.12 = (bf16[48,4096]{1,0:T(8,128)(2,1)S(1)}, bf16[48,4096]{1,0:T(8,128)(2,1)}, u32[]{:S(2)}) copy-start(bf16[48,4096]{1,0:T(8,128)(2,1)} %get-tuple-element.45) | copy-start | bytes 1179652
  10.7 39.1 %copy-start.11 = (bf16[48,4096]{1,0:T(8,128)(2,1)S(1)}, bf16[48,4096]{1,0:T(8,128)(2,1)}, u32[]{:S(2)}) copy-start(bf16[48,4096]{1,0:T(8,128)(2,1)} %get-tuple-element.49) | copy-start | bytes 1179652
  10.8 29.6 %collective-permute-start.4 = (bf16[48,4096]{1,0:T(8,128)(2,1)}, bf16[48,4096]{1,0:T(8,128)(2,1)S(1)}, u32[]{:S(2)}, u32[]{:S(2)}) collective-permute-start(bf16[48,4096]{1,0:T(8,128)(2,1)} %get-tuple-element.31), channel_id=1, source_target_pairs={{0,4},{1,5},{2,6},{3,7},{4,0},{5,1},{6,2},{7,3},{8,12},{9,13},{10,... | collective-permute-start | bytes 1179656 | tf_op jit(solution)/shard_map/ppermute | solution.py:20
  11.3 29.5 %collective-permute-start.5 = (bf16[48,4096]{1,0:T(8,128)(2,1)}, bf16[48,4096]{1,0:T(8,128)(2,1)S(1)}, u32[]{:S(2)}, u32[]{:S(2)}) collective-permute-start(bf16[48,4096]{1,0:T(8,128)(2,1)} %get-tuple-element.32), channel_id=1, source_target_pairs={{0,8},{1,9},{2,10},{3,11},{4,12},{5,13},{6,14},{7,15},{8,0},{9,1},... | collective-permute-start | bytes 1179656 | tf_op jit(solution)/shard_map/ppermute | solution.py:20
  13.9 35.9 %collective-permute-start.6 = (bf16[48,4096]{1,0:T(8,128)(2,1)}, bf16[48,4096]{1,0:T(8,128)(2,1)S(1)}, u32[]{:S(2)}, u32[]{:S(2)}) collective-permute-start(bf16[48,4096]{1,0:T(8,128)(2,1)} %get-tuple-element.33), channel_id=1, source_target_pairs={{0,12},{1,13},{2,14},{3,15},{4,8},{5,9},{6,10},{7,11},{8,4},{9,5},... | collective-permute-start | bytes 1179656 | tf_op jit(solution)/shard_map/ppermute | solution.py:20
  38.2 37.5 %collective-permute-start.10 = (bf16[1024,768]{1,0:T(8,128)(2,1)}, bf16[1024,768]{1,0:T(8,128)(2,1)S(1)}, u32[]{:S(2)}, u32[]{:S(2)}) collective-permute-start(bf16[1024,768]{1,0:T(8,128)(2,1)} %bitcast.76), channel_id=1, source_target_pairs={{0,2},{1,3},{2,0},{3,1},{4,6},{5,7},{6,4},{7,5},{8,10},{9,11},{10,... | collective-permute-start | bytes 4718600 | tf_op jit(solution)/shard_map/ppermute | solution.py:20
  38.8 14.3 %copy-start.7 = (f32[2,128]{1,0:T(2,128)}, f32[2,128]{1,0:T(2,128)S(1)}, u32[]{:S(2)}) copy-start(f32[2,128]{1,0:T(2,128)S(1)} %collective-permute-done.meta_ref) | copy-start | bytes 3076
  38.8 73.9 %collective-permute-start.12 = (bf16[768,1024]{1,0:T(8,128)(2,1)S(1)}, bf16[768,1024]{1,0:T(8,128)(2,1)S(1)}, u32[]{:S(2)}, u32[]{:S(2)}) collective-permute-start(bf16[768,1024]{1,0:T(8,128)(2,1)S(1)} %bitcast.74), channel_id=1, source_target_pairs={{0,2},{1,3},{2,0},{3,1},{4,6},{5,7},{6,4},{7,5},{8,10},{9,11},{10,... | collective-permute-start | bytes 4718600 | tf_op jit(solution)/shard_map/ppermute | solution.py:20
  40.3 35.9 %collective-permute-start.8 = (bf16[48,4096]{1,0:T(8,128)(2,1)}, bf16[48,4096]{1,0:T(8,128)(2,1)S(1)}, u32[]{:S(2)}, u32[]{:S(2)}) collective-permute-start(bf16[48,4096]{1,0:T(8,128)(2,1)} %get-tuple-element.35), channel_id=1, source_target_pairs={{0,4},{1,5},{2,6},{3,7},{4,0},{5,1},{6,2},{7,3},{8,12},{9,13},{10,... | collective-permute-start | bytes 1179656 | tf_op jit(solution)/shard_map/ppermute | solution.py:20
  40.8 36.1 %collective-permute-start.15 = (bf16[48,4096]{1,0:T(8,128)(2,1)S(1)}, bf16[48,4096]{1,0:T(8,128)(2,1)S(1)}, u32[]{:S(2)}, u32[]{:S(2)}) collective-permute-start(bf16[48,4096]{1,0:T(8,128)(2,1)S(1)} %copy-done.12), channel_id=1, source_target_pairs={{0,8},{1,9},{2,10},{3,11},{4,12},{5,13},{6,14},{7,15},{8,0},{9,1},... | collective-permute-start | bytes 1179656 | tf_op jit(solution)/shard_map/ppermute | solution.py:20
  49.8 50.5 %collective-permute-start.17 = (bf16[48,4096]{1,0:T(8,128)(2,1)S(1)}, bf16[48,4096]{1,0:T(8,128)(2,1)S(1)}, u32[]{:S(2)}, u32[]{:S(2)}) collective-permute-start(bf16[48,4096]{1,0:T(8,128)(2,1)S(1)} %copy-done.11), channel_id=1, source_target_pairs={{0,12},{1,13},{2,14},{3,15},{4,8},{5,9},{6,10},{7,11},{8,4},{9,5},... | collective-permute-start | bytes 1179656 | tf_op jit(solution)/shard_map/ppermute | solution.py:20
  55.5 21.4 %copy-start.9 = (bf16[48,4096]{1,0:T(8,128)(2,1)S(1)}, bf16[48,4096]{1,0:T(8,128)(2,1)}, u32[]{:S(2)}) copy-start(bf16[48,4096]{1,0:T(8,128)(2,1)} %get-tuple-element.46) | copy-start | bytes 1179652
  55.5 44.9 %copy-start.8 = (bf16[48,4096]{1,0:T(8,128)(2,1)S(1)}, bf16[48,4096]{1,0:T(8,128)(2,1)}, u32[]{:S(2)}) copy-start(bf16[48,4096]{1,0:T(8,128)(2,1)} %get-tuple-element.50) | copy-start | bytes 1179652
  76.3 29.2 %collective-permute-start.11 = (bf16[1024,768]{1,0:T(8,128)(2,1)S(1)}, bf16[1024,768]{1,0:T(8,128)(2,1)S(1)}, u32[]{:S(2)}, u32[]{:S(2)}) collective-permute-start(bf16[1024,768]{1,0:T(8,128)(2,1)S(1)} %collective-permute-done.10), channel_id=1, source_target_pairs={{0,1},{1,0},{2,3},{3,2},{4,5},{5,4},{6,7},{7,6},{8,9},{9,8},{10,11... | collective-permute-start | bytes 4718600 | tf_op jit(solution)/shard_map/ppermute | solution.py:20
  76.3 29.1 %collective-permute-start.9 = (bf16[1024,768]{1,0:T(8,128)(2,1)S(1)}, bf16[1024,768]{1,0:T(8,128)(2,1)S(1)}, u32[]{:S(2)}, u32[]{:S(2)}) collective-permute-start(bf16[1024,768]{1,0:T(8,128)(2,1)S(1)} %collective-permute-done.7), channel_id=1, source_target_pairs={{0,1},{1,0},{2,3},{3,2},{4,5},{5,4},{6,7},{7,6},{8,9},{9,8},{10,11... | collective-permute-start | bytes 4718600 | tf_op jit(solution)/shard_map/ppermute | solution.py:20
  76.8 38.3 %collective-permute-start.16 = (bf16[48,4096]{1,0:T(8,128)(2,1)S(1)}, bf16[48,4096]{1,0:T(8,128)(2,1)S(1)}, u32[]{:S(2)}, u32[]{:S(2)}) collective-permute-start(bf16[48,4096]{1,0:T(8,128)(2,1)S(1)} %copy-done.9), channel_id=1, source_target_pairs={{0,8},{1,9},{2,10},{3,11},{4,12},{5,13},{6,14},{7,15},{8,0},{9,1},... | collective-permute-start | bytes 1179656 | tf_op jit(solution)/shard_map/ppermute | solution.py:20
  100.3 15.8 %collective-permute-start.18 = (bf16[48,4096]{1,0:T(8,128)(2,1)S(1)}, bf16[48,4096]{1,0:T(8,128)(2,1)S(1)}, u32[]{:S(2)}, u32[]{:S(2)}) collective-permute-start(bf16[48,4096]{1,0:T(8,128)(2,1)S(1)} %copy-done.8), channel_id=1, source_target_pairs={{0,12},{1,13},{2,14},{3,15},{4,8},{5,9},{6,10},{7,11},{8,4},{9,5},... | collective-permute-start | bytes 1179656 | tf_op jit(solution)/shard_map/ppermute | solution.py:20
  105.5 9.6 %collective-permute-start.13 = (bf16[48,4096]{1,0:T(8,128)(2,1)S(1)}, bf16[48,4096]{1,0:T(8,128)(2,1)S(1)}, u32[]{:S(2)}, u32[]{:S(2)}) collective-permute-start(bf16[48,4096]{1,0:T(8,128)(2,1)S(1)} %copy-done.10), channel_id=1, source_target_pairs={{0,4},{1,5},{2,6},{3,7},{4,0},{5,1},{6,2},{7,3},{8,12},{9,13},{10,... | collective-permute-start | bytes 1179656 | tf_op jit(solution)/shard_map/ppermute | solution.py:20
  115.1 3.9 %collective-permute-start.14 = (bf16[768,1024]{1,0:T(8,128)(2,1)S(1)}, bf16[768,1024]{1,0:T(8,128)(2,1)S(1)}, u32[]{:S(2)}, u32[]{:S(2)}) collective-permute-start(bf16[768,1024]{1,0:T(8,128)(2,1)S(1)} %collective-permute-done.12), channel_id=1, source_target_pairs={{0,1},{1,0},{2,3},{3,2},{4,5},{5,4},{6,7},{7,6},{8,9},{9,8},{10,11... | collective-permute-start | bytes 4718600 | tf_op jit(solution)/shard_map/ppermute | solution.py:20
  129.0 28.4 %collective-permute-start.19 = (bf16[48,4096]{1,0:T(8,128)(2,1)S(1)}, bf16[48,4096]{1,0:T(8,128)(2,1)S(1)}, u32[]{:S(2)}, u32[]{:S(2)}) collective-permute-start(bf16[48,4096]{1,0:T(8,128)(2,1)S(1)} %get-tuple-element.57), channel_id=1, source_target_pairs={{0,16},{1,17},{2,18},{3,19},{4,20},{5,21},{6,22},{7,23},{8,24},{9,... | collective-permute-start | bytes 1179656 | tf_op jit(solution)/shard_map/ppermute | solution.py:32
  129.6 27.9 %collective-permute-start.20 = (bf16[48,4096]{1,0:T(8,128)(2,1)S(1)}, bf16[48,4096]{1,0:T(8,128)(2,1)S(1)}, u32[]{:S(2)}, u32[]{:S(2)}) collective-permute-start(bf16[48,4096]{1,0:T(8,128)(2,1)S(1)} %get-tuple-element.56), channel_id=1, source_target_pairs={{0,20},{1,21},{2,22},{3,23},{4,16},{5,17},{6,18},{7,19},{8,28},{9,... | collective-permute-start | bytes 1179656 | tf_op jit(solution)/shard_map/ppermute | solution.py:32
  132.6 27.4 %collective-permute-start.21 = (bf16[48,4096]{1,0:T(8,128)(2,1)S(1)}, bf16[48,4096]{1,0:T(8,128)(2,1)S(1)}, u32[]{:S(2)}, u32[]{:S(2)}) collective-permute-start(bf16[48,4096]{1,0:T(8,128)(2,1)S(1)} %get-tuple-element.55), channel_id=1, source_target_pairs={{0,24},{1,25},{2,26},{3,27},{4,28},{5,29},{6,30},{7,31},{8,16},{9,... | collective-permute-start | bytes 1179656 | tf_op jit(solution)/shard_map/ppermute | solution.py:32
  133.6 34.8 %collective-permute-start.22 = (bf16[48,4096]{1,0:T(8,128)(2,1)S(1)}, bf16[48,4096]{1,0:T(8,128)(2,1)S(1)}, u32[]{:S(2)}, u32[]{:S(2)}) collective-permute-start(bf16[48,4096]{1,0:T(8,128)(2,1)S(1)} %get-tuple-element.54), channel_id=1, source_target_pairs={{0,28},{1,29},{2,30},{3,31},{4,24},{5,25},{6,26},{7,27},{8,20},{9,... | collective-permute-start | bytes 1179656 | tf_op jit(solution)/shard_map/ppermute | solution.py:32
  157.5 10.9 %copy-start.3 = (bf16[48,4096]{1,0:T(8,128)(2,1)}, bf16[48,4096]{1,0:T(8,128)(2,1)S(1)}, u32[]{:S(2)}) copy-start(bf16[48,4096]{1,0:T(8,128)(2,1)S(1)} %collective-permute-done.19.refs_0_) | copy-start | bytes 1179652
  157.5 10.9 %copy-start.4 = (bf16[48,4096]{1,0:T(8,128)(2,1)}, bf16[48,4096]{1,0:T(8,128)(2,1)S(1)}, u32[]{:S(2)}) copy-start(bf16[48,4096]{1,0:T(8,128)(2,1)S(1)} %collective-permute-done.20.refs_1_) | copy-start | bytes 1179652
  159.9 8.4 %copy-start.5 = (bf16[48,4096]{1,0:T(8,128)(2,1)}, bf16[48,4096]{1,0:T(8,128)(2,1)S(1)}, u32[]{:S(2)}) copy-start(bf16[48,4096]{1,0:T(8,128)(2,1)S(1)} %collective-permute-done.21.refs_2_) | copy-start | bytes 1179652
  (4 other events, 5.6 us)

commit v3 on v2

--- a/solution.py
+++ b/solution.py
@@ -86,7 +86,8 @@
             bytes_accessed=2 * width * (tokens * len(values) + out_count * slot_cap),
             transcendentals=0,
         ),
-    )(where, *args)
+        compiler_params=pltpu.CompilerParams(vmem_limit_bytes=20 << 20),
+    )(where, *[pltpu.with_memory_space_constraint(arg, pltpu.HBM) for arg in args])
     return [out[at * experts : (at + 1) * experts] for at in range(len(values))]
 
 
@@ -141,7 +142,37 @@
             bytes_accessed=2 * width * (tokens * outputs + experts * slot_cap),
             transcendentals=0,
         ),
+        compiler_params=pltpu.CompilerParams(vmem_limit_bytes=16 << 20),
     )(where, meta, *blocks)
+
+
+def stage_kernel(*refs):
+    count = len(refs) // 2
+    arrived = refs[-1]
+    copies = [
+        pltpu.make_async_copy(refs[at], refs[count + at], arrived.at[at]) for at in range(count)
+    ]
+    for copy in copies:
+        copy.start()
+    for copy in copies:
+        copy.wait()
+
+
+def staged(weights):
+    count = len(weights)
+    return pl.pallas_call(
+        stage_kernel,
+        in_specs=[pl.BlockSpec(memory_space=pl.ANY)] * count,
+        out_specs=[pl.BlockSpec(memory_space=pltpu.VMEM)] * count,
+        out_shape=[jax.ShapeDtypeStruct(weight.shape, weight.dtype) for weight in weights],
+        scratch_shapes=[pltpu.SemaphoreType.DMA((count,))],
+        cost_estimate=pl.CostEstimate(
+            flops=0,
+            bytes_accessed=sum(2 * weight.size * weight.dtype.itemsize for weight in weights),
+            transcendentals=0,
+        ),
+        compiler_params=pltpu.CompilerParams(vmem_limit_bytes=16 << 20),
+    )(*[pltpu.with_memory_space_constraint(weight, pltpu.HBM) for weight in weights])
 
 
 def rows_times(rows, mats):
@@ -180,18 +211,6 @@
     section = lax.axis_index("pp")
     where = jnp.stack([me // QUARTERS, me % QUARTERS, section]).astype(jnp.int32)
 
-    fwd_meta = jnp.concatenate(
-        [fwd_routes[0].reshape(1, tokens).astype(jnp.float32), fwd_gates[0].reshape(1, tokens)]
-    )
-    bwd_meta = bwd_routes[0].reshape(1, tokens).astype(jnp.float32)
-    bwd_meta = jnp.concatenate([bwd_meta, jnp.ones_like(bwd_meta)])
-    merged = lax.axis_size("pp") == 2
-    first = section == 0
-    if merged:
-        metas = [handed(jnp.where(first, fwd_meta, bwd_meta), (1, -1), 0)]
-    else:
-        metas = [handed(fwd_meta, (1,), 0), handed(bwd_meta, (-1,), 0)]
-
     gate, up, down = gate_proj[0, 0], up_proj[0, 0], down_proj[0, 0]
     gate_across = paired(gate, 2)
     up_across = paired(up, 2)
@@ -214,15 +233,18 @@
         before = (up_beside, down_beside) if d == last else ()
         fwd_blocks[d] = paired(fwd_spread[d], QUARTERS * d, *before)
     for d in order:
-        before = metas if d == last else ()
-        bwd_blocks[d] = paired(row_spread[d], QUARTERS * d, fwd_blocks[d], *before)
+        bwd_blocks[d] = paired(row_spread[d], QUARTERS * d, fwd_blocks[d])
     down_across = paired(down, 2, gate_across)
     gate_diagonal = paired(gate_across, 1, bwd_blocks[last])
     up_diagonal = paired(up_across, 1, bwd_blocks[last])
     for d in order:
         before = (gate_diagonal, up_diagonal) if d == last else (up_across,)
         grad_blocks[d] = paired(grad_spread[d], QUARTERS * d, bwd_blocks[d], *before)
-    down_diagonal = paired(down_across, 1, grad_blocks[last])
+    down_diagonal = paired(down_across, 1, up_diagonal)
+    near = lax.optimization_barrier((gate_across, down_beside, fwd_blocks[last]))
+    gate_across, down_beside = staged(near[:2])
+    near = lax.optimization_barrier((up_across, bwd_blocks[last]))
+    (up_across,) = staged(near[:1])
     gate_mats = [gate, gate_beside, gate_across, gate_diagonal]
     up_mats = [up, up_beside, up_across, up_diagonal]
     down_mats = [down, down_beside, down_across, down_diagonal]
@@ -233,46 +255,54 @@
     rows = jnp.concatenate(fwd_blocks)
     gate_value, up_value = rows_times(rows, gate_mats), rows_times(rows, up_mats)
     hidden = (jax.nn.silu(gate_value) * up_value).astype(jnp.bfloat16)
-    fwd_out = jnp.concatenate(
-        [
-            jnp.dot(hidden, mat, preferred_element_type=jnp.float32).astype(jnp.bfloat16)
-            for mat in down_mats
-        ],
-        axis=1,
-    )
+    fwd_parts = [
+        jnp.dot(hidden, mat, preferred_element_type=jnp.float32).astype(jnp.bfloat16)
+        for mat in down_mats
+    ]
 
     rows = jnp.concatenate(bwd_blocks)
     gate_value, up_value = rows_times(rows, gate_mats), rows_times(rows, up_mats)
-    grads = jnp.concatenate(grad_blocks)
-    quarter = down_mats[0].shape[1]
+    sigmoid_value = jax.nn.sigmoid(gate_value)
+    gate_factor = up_value * sigmoid_value * (1.0 + gate_value * (1.0 - sigmoid_value))
+    up_factor = gate_value * sigmoid_value
+
+    landed = lax.optimization_barrier((*grad_blocks[1:], gate_factor, up_factor, *fwd_parts))
+    grads = jnp.concatenate([grad_blocks[0], *landed[: experts - 1]])
+    quarter = down.shape[1]
     grad_hidden = sum(
         contract_cols(grads[:, j * quarter : (j + 1) * quarter], mat)
         for j, mat in enumerate(down_mats)
     )
-    sigmoid_value = jax.nn.sigmoid(gate_value)
-    grad_gate = (
-        grad_hidden * up_value * sigmoid_value * (1.0 + gate_value * (1.0 - sigmoid_value))
-    ).astype(jnp.bfloat16)
-    grad_up = (grad_hidden * gate_value * sigmoid_value).astype(jnp.bfloat16)
-    bwd_out = jnp.concatenate(
-        [
-            (contract_cols(grad_gate, g) + contract_cols(grad_up, u)).astype(jnp.bfloat16)
-            for g, u in zip(gate_mats, up_mats)
-        ],
-        axis=1,
-    )
-
-    def returned(out, steps):
-        parts = [out[d * slot_cap : (d + 1) * slot_cap] for d in range(experts)]
-        back = {d: handed(parts[d], steps, QUARTERS * d) for d in reversed(range(experts))}
-        return [back[d] for d in range(experts)]
+    grad_gate = (grad_hidden * landed[experts - 1]).astype(jnp.bfloat16)
+    grad_up = (grad_hidden * landed[experts]).astype(jnp.bfloat16)
+    bwd_parts = [
+        (contract_cols(grad_gate, g) + contract_cols(grad_up, u)).astype(jnp.bfloat16)
+        for g, u in zip(gate_mats, up_mats)
+    ]
+    fwd_parts = landed[experts + 1 :]
+    merged = lax.axis_size("pp") == 2
+
+    done = tuple(grad_blocks[1:])
+    fwd_meta = jnp.concatenate(
+        [fwd_routes[0].reshape(1, tokens).astype(jnp.float32), fwd_gates[0].reshape(1, tokens)]
+    )
+    bwd_meta = bwd_routes[0].reshape(1, tokens).astype(jnp.float32)
+    bwd_meta = jnp.concatenate([bwd_meta, jnp.ones_like(bwd_meta)])
+
+    def returned(parts, steps):
+        out = jnp.concatenate(parts, axis=1)
+        blocks = [out[d * slot_cap : (d + 1) * slot_cap] for d in range(experts)]
+        return [handed(blocks[d], steps, QUARTERS * d) for d in range(experts)]
 
     if merged:
-        back = returned(jnp.where(first, fwd_out, bwd_out), (1, -1))
-        handed_forward, handed_backward = collect(where, metas[0], back, 2)
+        first = section == 0
+        meta = handed(after(jnp.where(first, fwd_meta, bwd_meta), *done), (1, -1), 0)
+        parts = [jnp.where(first, fwd, bwd) for fwd, bwd in zip(fwd_parts, bwd_parts)]
+        handed_forward, handed_backward = collect(where, meta, returned(parts, (1, -1)), 2)
     else:
-        (handed_forward,) = collect(where, metas[0], returned(fwd_out, (1,)), 1)
-        (handed_backward,) = collect(where, metas[1], returned(bwd_out, (-1,)), 1)
+        metas = [handed(after(m, *done), (by,), 0) for m, by in ((fwd_meta, 1), (bwd_meta, -1))]
+        (handed_forward,) = collect(where, metas[0], returned(fwd_parts, (1,)), 1)
+        (handed_backward,) = collect(where, metas[1], returned(bwd_parts, (-1,)), 1)
     return handed_forward[None], handed_backward[None]
 
 

time: 175 us -> 166 us (0.949)
  matrix products: 25.3 us -> 18.2 us
  waiting for transfers between devices: 105 us -> 110 us
  local copies, waits for them, and re-layouts: 5.94 us -> 2.24 us
  other arithmetic: 2.37 us -> 0.48 us
    ppermute x18, waiting for transfers between devices: 71.8 us -> 77.5 us  [paired(): return lax.ppermute(block, 'ep', [(i, i ^ distance) for i in range(count)])]
    unnamed x35 -> x21, local copies, waits for them, and re-layouts: 5.72 us -> 2.06 us
    pallas_call x0 -> x2, Pallas kernels: none -> 3.31 us  [staged(): pl.pallas_call(stage_kernel, in_specs=[pl.BlockSpec(memory_space=pl.ANY)]...]
    dot_general x12, matrix products: 11.1 us -> 8.21 us  [contract_cols(): lax.dot_general(left, right, (((1,), (1,)), ((), ())), preferred_element_...]
    dot_general x16, matrix products: 10.8 us -> 8.08 us  [rows_times(): jnp.dot(rows[:, j * quarter:(j + 1) * quarter], mat, preferred_element_ty...]
  transfers between devices with their start and end apart: 23 -> 23, of which waited for: 10 -> 12; matrix products, arithmetic and copies ran while one was open for 12% -> 6% of each run, Pallas kernels for 3% -> 4%
where the time goes in v3:
time: 166 us; the launch traced here: 165 us
  waiting for transfers between devices  110 us (66%)
  starting transfers between devices  23.3 us (14%)
  matrix products  18.2 us (11%)
  Pallas kernels  9.51 us (6%)
  local copies, waits for them, and re-layouts  2.24 us (1%)
    ppermute x18, waiting for transfers between devices, paired(): return lax.ppermute(block, 'ep', [(i, i ^ distance) for i in range(count)])  77.5 us
    ppermute x5, waiting for transfers between devices, handed(): return lax.ppermute(block, ('pp', 'ep'), route)  32.5 us
    ppermute x18, starting transfers between devices, paired(): return lax.ppermute(block, 'ep', [(i, i ^ distance) for i in range(count)])  16.8 us
    dot_general x12, matrix products, contract_cols(): lax.dot_general(left, right, (((1,), (1,)), ((), ())), preferred_element_...  8.21 us
    dot_general x16, matrix products, rows_times(): jnp.dot(rows[:, j * quarter:(j + 1) * quarter], mat, preferred_element_ty...  8.08 us
    ppermute x5, starting transfers between devices, handed(): return lax.ppermute(block, ('pp', 'ep'), route)  6.5 us
    pallas_call x1, Pallas kernels, spread(): pl.pallas_call(functools.partial(spread_kernel, slot_cap, experts), in_sp...  3.42 us
  transfers between devices with their start and end apart: 23, of which 12 were waited for; matrix products, arithmetic and copies ran while one was open for 6% of the time, Pallas kernels for 4%

profile of v3, /device:TPU:14, one launch (start us, length us, event | category | flops | bytes accessed | tf_op | source)
XLA Modules:
  0.0 164.8 jit_solution(12229907606609695224)
XLA Ops:
  1.8 1.5 collective-permute-start.7
  3.4 0.9 collective-permute-done
  4.3 3.4 %shard_map.113 = (bf16[48,4096]{1,0:T(8,128)(2,1)S(1)}, bf16[48,4096]{1,0:T(8,128)(2,1)S(1)}, bf16[48,4096]{1,0:T(8,128)(2,1)S(1)}, bf16[48,4096]{1,0:T(8,128)(2...) custom-call(s32[3]{0:T(128)S(1)} %pad_add_fusion.where_ref, ...), custom_call_target="tpu_custom_call" | custom-call | flops 603979776 | bytes 7864320 | tf_op jit(solution)/shard_map/pallas_call | solution.py:79
  7.8 1.1 collective-permute-done.1
  9.4 2.6 %collective-permute-start.10 = (bf16[48,4096]{1,0:T(8,128)(2,1)S(1)}, bf16[48,4096]{1,0:T(8,128)(2,1)S(1)}, u32[]{:S(2)}, u32[]{:S(2)}) collective-permute-start(bf16[48,4096]{1,0:T(8,128)(2,1)S(1)} %get-tuple-element.53), channel_id=1, source_target_pairs={{0,8},{1,9},{2,10},{3,11},{4,12},{5,13},{6,14},{7,15},{8,0},{9,1},... | collective-permute-start | bytes 1179656 | tf_op jit(solution)/shard_map/ppermute | solution.py:20
  12.5 26.3 %collective-permute-done.5.refs_0_ = bf16[1024,768]{1,0:T(8,128)(2,1)} collective-permute-done((bf16[1024,768]{1,0:T(8,128)(2,1)}, bf16[1024,768]{1,0:T(8,128)(2,1)}, u32[]{:S(2)}, u32[]{:S(2)}) %collective-permute-start.5) | collective-permute-done | bytes 1572896 | tf_op jit(solution)/shard_map/ppermute | solution.py:20
  39.9 2.6 %collective-permute-start.11 = (bf16[48,4096]{1,0:T(8,128)(2,1)S(1)}, bf16[48,4096]{1,0:T(8,128)(2,1)S(1)}, u32[]{:S(2)}, u32[]{:S(2)}) collective-permute-start(bf16[48,4096]{1,0:T(8,128)(2,1)S(1)} %get-tuple-element.54), channel_id=1, source_target_pairs={{0,8},{1,9},{2,10},{3,11},{4,12},{5,13},{6,14},{7,15},{8,0},{9,1},... | collective-permute-start | bytes 1179656 | tf_op jit(solution)/shard_map/ppermute | solution.py:20
  42.5 5.2 %collective-permute-done.13 = bf16[48,4096]{1,0:T(8,128)(2,1)S(1)} collective-permute-done((bf16[48,4096]{1,0:T(8,128)(2,1)S(1)}, bf16[48,4096]{1,0:T(8,128)(2,1)S(1)}, u32[]{:S(2)}, u32[]{:S(2)}) %collective-permute-start.13) | collective-permute-done | bytes 393248 | tf_op jit(solution)/shard_map/ppermute | solution.py:20
  47.7 2.1 %collective-permute-start.14 = (bf16[48,4096]{1,0:T(8,128)(2,1)S(1)}, bf16[48,4096]{1,0:T(8,128)(2,1)S(1)}, u32[]{:S(2)}, u32[]{:S(2)}) collective-permute-start(bf16[48,4096]{1,0:T(8,128)(2,1)S(1)} %get-tuple-element.59), channel_id=1, source_target_pairs={{0,12},{1,13},{2,14},{3,15},{4,8},{5,9},{6,10},{7,11},{8,4},{9,5},... | collective-permute-start | bytes 1179656 | tf_op jit(solution)/shard_map/ppermute | solution.py:20
  49.8 1.9 %shard_map.115 = (bf16[1024,768]{1,0:T(8,128)(2,1)S(1)}, bf16[768,1024]{1,0:T(8,128)(2,1)S(1)}) custom-call(bf16[1024,768]{1,0:T(8,128)(2,1)} %collective-permute-done.5.refs_0_, bf16[768,1024]{1,0:T(8,128)(2,1)} %collective-permute-done.2.refs_1_), custom_call_target="tpu_custom_call" | custom-call | bytes 6291456 | tf_op jit(solution)/shard_map/pallas_call | solution.py:163
  53.3 19.2 %collective-permute-done.7.refs_0_ = bf16[1024,768]{1,0:T(8,128)(2,1)} collective-permute-done((bf16[1024,768]{1,0:T(8,128)(2,1)}, bf16[1024,768]{1,0:T(8,128)(2,1)}, u32[]{:S(2)}, u32[]{:S(2)}) %collective-permute-start.7) | collective-permute-done | bytes 1572896 | tf_op jit(solution)/shard_map/ppermute | solution.py:20
  72.5 1.4 shard_map.114
  74.5 2.6 %collective-permute-start.12 = (bf16[48,4096]{1,0:T(8,128)(2,1)S(1)}, bf16[48,4096]{1,0:T(8,128)(2,1)S(1)}, u32[]{:S(2)}, u32[]{:S(2)}) collective-permute-start(bf16[48,4096]{1,0:T(8,128)(2,1)S(1)} %get-tuple-element.55), channel_id=1, source_target_pairs={{0,8},{1,9},{2,10},{3,11},{4,12},{5,13},{6,14},{7,15},{8,0},{9,1},... | collective-permute-start | bytes 1179656 | tf_op jit(solution)/shard_map/ppermute | solution.py:20
  77.1 21.1 %collective-permute-done.14 = bf16[48,4096]{1,0:T(8,128)(2,1)S(1)} collective-permute-done((bf16[48,4096]{1,0:T(8,128)(2,1)S(1)}, bf16[48,4096]{1,0:T(8,128)(2,1)S(1)}, u32[]{:S(2)}, u32[]{:S(2)}) %collective-permute-start.14) | collective-permute-done | bytes 393248 | tf_op jit(solution)/shard_map/ppermute | solution.py:20
  98.2 1.6 collective-permute-start.15
  103.5 0.9 copy-done.1
  104.9 0.9 copy-done.2
  110.1 0.7 collective-permute-done.18
  111.3 2.8 %collective-permute-done.15 = bf16[48,4096]{1,0:T(8,128)(2,1)S(1)} collective-permute-done((bf16[48,4096]{1,0:T(8,128)(2,1)S(1)}, bf16[48,4096]{1,0:T(8,128)(2,1)S(1)}, u32[]{:S(2)}, u32[]{:S(2)}) %collective-permute-start.15) | collective-permute-done | bytes 393248 | tf_op jit(solution)/shard_map/ppermute | solution.py:20
  114.2 0.7 fusion.20
  114.9 0.7 convolution_add_fusion.5
  116.2 0.7 multiply_convert_fusion.1
  116.9 0.8 fusion.63
  119.1 0.7 fusion
  121.9 0.7 fusion.1
  123.6 2.4 %collective-permute-start.20 = (bf16[48,4096]{1,0:T(8,128)(2,1)S(1)}, bf16[48,4096]{1,0:T(8,128)(2,1)S(1)}, u32[]{:S(2)}, u32[]{:S(2)}) collective-permute-start(bf16[48,4096]{1,0:T(8,128)(2,1)S(1)} %get-tuple-element.84), channel_id=1, source_target_pairs={{0,20},{1,21},{2,22},{3,23},{4,16},{5,17},{6,18},{7,19},{8,28},{9,... | collective-permute-start | bytes 1179656 | tf_op jit(solution)/shard_map/ppermute | solution.py:32
  126.0 1.6 collective-permute-start.21
  127.5 1.4 collective-permute-start.22
  129.5 21.5 %collective-permute-done.16.meta_ref = f32[2,128]{1,0:T(2,128)S(1)} collective-permute-done((f32[2,128]{1,0:T(2,128)S(1)}, f32[2,128]{1,0:T(2,128)S(1)}, u32[]{:S(2)}, u32[]{:S(2)}) %collective-permute-start.16) | collective-permute-done | bytes 1056 | tf_op jit(solution)/shard_map/ppermute | solution.py:32
  151.0 2.9 %collective-permute-done.21.refs_2_ = bf16[48,4096]{1,0:T(8,128)(2,1)S(1)} collective-permute-done((bf16[48,4096]{1,0:T(8,128)(2,1)S(1)}, bf16[48,4096]{1,0:T(8,128)(2,1)S(1)}, u32[]{:S(2)}, u32[]{:S(2)}) %collective-permute-start.21) | collective-permute-done | bytes 393248 | tf_op jit(solution)/shard_map/ppermute | solution.py:32
  153.9 8.1 %collective-permute-done.22.refs_3_ = bf16[48,4096]{1,0:T(8,128)(2,1)S(1)} collective-permute-done((bf16[48,4096]{1,0:T(8,128)(2,1)S(1)}, bf16[48,4096]{1,0:T(8,128)(2,1)S(1)}, u32[]{:S(2)}, u32[]{:S(2)}) %collective-permute-start.22) | collective-permute-done | bytes 393248 | tf_op jit(solution)/shard_map/ppermute | solution.py:32
  162.0 2.8 %shard_map.116 = (bf16[128,4096]{1,0:T(8,128)(2,1)}, bf16[128,4096]{1,0:T(8,128)(2,1)}) custom-call(s32[3]{0:T(128)S(1)} %pad_add_fusion.where_ref, f32[2,128]{1,0:T(2,128)S(1)} %collective-permute-done.16.meta_ref, bf16[48,4096]{1,0:T(8,128)(2,1)S(1)} %collective-permute-done.19.refs_0_, bf16[48,4096]{1,0:T(8,128)(2,1)S(1)} %collective-permute-done.20.refs_1_, ...), custom_call_target="tpu_custom_call" | custom-call | flops 201326592 | bytes 3670016 | tf_op jit(solution)/shard_map/pallas_call | solution.py:135
  (81 shorter events, 20.1 us)
Async XLA Ops:
  0.6 3.7 %collective-permute-start = (bf16[1024,768]{1,0:T(8,128)(2,1)}, bf16[1024,768]{1,0:T(8,128)(2,1)S(1)}, u32[]{:S(2)}, u32[]{:S(2)}) collective-permute-start(bf16[1024,768]{1,0:T(8,128)(2,1)} %bitcast.73), channel_id=1, source_target_pairs={{0,1},{1,0},{2,3},{3,2},{4,5},{5,4},{6,7},{7,6},{8,9},{9,8},{10,11... | collective-permute-start | bytes 4718600 | tf_op jit(solution)/shard_map/ppermute | solution.py:20
  0.7 8.1 %collective-permute-start.1 = (bf16[1024,768]{1,0:T(8,128)(2,1)}, bf16[1024,768]{1,0:T(8,128)(2,1)S(1)}, u32[]{:S(2)}, u32[]{:S(2)}) collective-permute-start(bf16[1024,768]{1,0:T(8,128)(2,1)} %bitcast.75), channel_id=1, source_target_pairs={{0,1},{1,0},{2,3},{3,2},{4,5},{5,4},{6,7},{7,6},{8,9},{9,8},{10,11... | collective-permute-start | bytes 4718600 | tf_op jit(solution)/shard_map/ppermute | solution.py:20
  1.2 7.7 %collective-permute-start.2 = (bf16[768,1024]{1,0:T(8,128)(2,1)}, bf16[768,1024]{1,0:T(8,128)(2,1)}, u32[]{:S(2)}, u32[]{:S(2)}) collective-permute-start(bf16[768,1024]{1,0:T(8,128)(2,1)} %bitcast.71), channel_id=1, source_target_pairs={{0,1},{1,0},{2,3},{3,2},{4,5},{5,4},{6,7},{7,6},{8,9},{9,8},{10,11... | collective-permute-start | bytes 4718600 | tf_op jit(solution)/shard_map/ppermute | solution.py:20
  1.3 37.5 %collective-permute-start.5 = (bf16[1024,768]{1,0:T(8,128)(2,1)}, bf16[1024,768]{1,0:T(8,128)(2,1)}, u32[]{:S(2)}, u32[]{:S(2)}) collective-permute-start(bf16[1024,768]{1,0:T(8,128)(2,1)} %bitcast.74), channel_id=1, source_target_pairs={{0,2},{1,3},{2,0},{3,1},{4,6},{5,7},{6,4},{7,5},{8,10},{9,11},{10,... | collective-permute-start | bytes 4718600 | tf_op jit(solution)/shard_map/ppermute | solution.py:20
  1.8 70.7 %collective-permute-start.7 = (bf16[1024,768]{1,0:T(8,128)(2,1)}, bf16[1024,768]{1,0:T(8,128)(2,1)}, u32[]{:S(2)}, u32[]{:S(2)}) collective-permute-start(bf16[1024,768]{1,0:T(8,128)(2,1)} %bitcast.76), channel_id=1, source_target_pairs={{0,2},{1,3},{2,0},{3,1},{4,6},{5,7},{6,4},{7,5},{8,10},{9,11},{10,... | collective-permute-start | bytes 4718600 | tf_op jit(solution)/shard_map/ppermute | solution.py:20
  7.7 31.1 %copy-start = (bf16[1,1,768,1024]{3,2,1,0:T(8,128)(2,1)S(1)}, bf16[1,1,768,1024]{3,2,1,0:T(8,128)(2,1)}, u32[]{:S(2)}) copy-start(bf16[1,1,768,1024]{3,2,1,0:T(8,128)(2,1)} %param.19) | copy-start | bytes 4718596
  8.9 30.4 %collective-permute-start.3 = (bf16[48,4096]{1,0:T(8,128)(2,1)S(1)}, bf16[48,4096]{1,0:T(8,128)(2,1)S(1)}, u32[]{:S(2)}, u32[]{:S(2)}) collective-permute-start(bf16[48,4096]{1,0:T(8,128)(2,1)S(1)} %get-tuple-element.46), channel_id=1, source_target_pairs={{0,4},{1,5},{2,6},{3,7},{4,0},{5,1},{6,2},{7,3},{8,12},{9,13},{10,... | collective-permute-start | bytes 1179656 | tf_op jit(solution)/shard_map/ppermute | solution.py:20
  9.4 30.5 %collective-permute-start.10 = (bf16[48,4096]{1,0:T(8,128)(2,1)S(1)}, bf16[48,4096]{1,0:T(8,128)(2,1)S(1)}, u32[]{:S(2)}, u32[]{:S(2)}) collective-permute-start(bf16[48,4096]{1,0:T(8,128)(2,1)S(1)} %get-tuple-element.53), channel_id=1, source_target_pairs={{0,8},{1,9},{2,10},{3,11},{4,12},{5,13},{6,14},{7,15},{8,0},{9,1},... | collective-permute-start | bytes 1179656 | tf_op jit(solution)/shard_map/ppermute | solution.py:20
  12.0 35.7 %collective-permute-start.13 = (bf16[48,4096]{1,0:T(8,128)(2,1)S(1)}, bf16[48,4096]{1,0:T(8,128)(2,1)S(1)}, u32[]{:S(2)}, u32[]{:S(2)}) collective-permute-start(bf16[48,4096]{1,0:T(8,128)(2,1)S(1)} %get-tuple-element.58), channel_id=1, source_target_pairs={{0,12},{1,13},{2,14},{3,15},{4,8},{5,9},{6,10},{7,11},{8,4},{9,5},... | collective-permute-start | bytes 1179656 | tf_op jit(solution)/shard_map/ppermute | solution.py:20
  38.8 68.5 %collective-permute-start.17 = (bf16[768,1024]{1,0:T(8,128)(2,1)S(1)}, bf16[768,1024]{1,0:T(8,128)(2,1)S(1)}, u32[]{:S(2)}, u32[]{:S(2)}) collective-permute-start(bf16[768,1024]{1,0:T(8,128)(2,1)S(1)} %bitcast.72), channel_id=1, source_target_pairs={{0,2},{1,3},{2,0},{3,1},{4,6},{5,7},{6,4},{7,5},{8,10},{9,11},{10,... | collective-permute-start | bytes 4718600 | tf_op jit(solution)/shard_map/ppermute | solution.py:20
  39.4 33.1 %collective-permute-start.4 = (bf16[48,4096]{1,0:T(8,128)(2,1)S(1)}, bf16[48,4096]{1,0:T(8,128)(2,1)S(1)}, u32[]{:S(2)}, u32[]{:S(2)}) collective-permute-start(bf16[48,4096]{1,0:T(8,128)(2,1)S(1)} %get-tuple-element.47), channel_id=1, source_target_pairs={{0,4},{1,5},{2,6},{3,7},{4,0},{5,1},{6,2},{7,3},{8,12},{9,13},{10,... | collective-permute-start | bytes 1179656 | tf_op jit(solution)/shard_map/ppermute | solution.py:20
  39.9 34.6 %collective-permute-start.11 = (bf16[48,4096]{1,0:T(8,128)(2,1)S(1)}, bf16[48,4096]{1,0:T(8,128)(2,1)S(1)}, u32[]{:S(2)}, u32[]{:S(2)}) collective-permute-start(bf16[48,4096]{1,0:T(8,128)(2,1)S(1)} %get-tuple-element.54), channel_id=1, source_target_pairs={{0,8},{1,9},{2,10},{3,11},{4,12},{5,13},{6,14},{7,15},{8,0},{9,1},... | collective-permute-start | bytes 1179656 | tf_op jit(solution)/shard_map/ppermute | solution.py:20
  47.7 50.6 %collective-permute-start.14 = (bf16[48,4096]{1,0:T(8,128)(2,1)S(1)}, bf16[48,4096]{1,0:T(8,128)(2,1)S(1)}, u32[]{:S(2)}, u32[]{:S(2)}) collective-permute-start(bf16[48,4096]{1,0:T(8,128)(2,1)S(1)} %get-tuple-element.59), channel_id=1, source_target_pairs={{0,12},{1,13},{2,14},{3,15},{4,8},{5,9},{6,10},{7,11},{8,4},{9,5},... | collective-permute-start | bytes 1179656 | tf_op jit(solution)/shard_map/ppermute | solution.py:20
  72.5 29.9 %collective-permute-start.8 = (bf16[1024,768]{1,0:T(8,128)(2,1)}, bf16[1024,768]{1,0:T(8,128)(2,1)S(1)}, u32[]{:S(2)}, u32[]{:S(2)}) collective-permute-start(bf16[1024,768]{1,0:T(8,128)(2,1)} %collective-permute-done.7.refs_0_), channel_id=1, source_target_pairs={{0,1},{1,0},{2,3},{3,2},{4,5},{5,4},{6,7},{7,6},{8,9},{9,8},{10,11... | collective-permute-start | bytes 4718600 | tf_op jit(solution)/shard_map/ppermute | solution.py:20
  73.9 28.5 %collective-permute-start.6 = (bf16[1024,768]{1,0:T(8,128)(2,1)}, bf16[1024,768]{1,0:T(8,128)(2,1)S(1)}, u32[]{:S(2)}, u32[]{:S(2)}) collective-permute-start(bf16[1024,768]{1,0:T(8,128)(2,1)} %collective-permute-done.5.refs_0_), channel_id=1, source_target_pairs={{0,1},{1,0},{2,3},{3,2},{4,5},{5,4},{6,7},{7,6},{8,9},{9,8},{10,11... | collective-permute-start | bytes 4718600 | tf_op jit(solution)/shard_map/ppermute | solution.py:20
  74.5 36.8 %collective-permute-start.12 = (bf16[48,4096]{1,0:T(8,128)(2,1)S(1)}, bf16[48,4096]{1,0:T(8,128)(2,1)S(1)}, u32[]{:S(2)}, u32[]{:S(2)}) collective-permute-start(bf16[48,4096]{1,0:T(8,128)(2,1)S(1)} %get-tuple-element.55), channel_id=1, source_target_pairs={{0,8},{1,9},{2,10},{3,11},{4,12},{5,13},{6,14},{7,15},{8,0},{9,1},... | collective-permute-start | bytes 1179656 | tf_op jit(solution)/shard_map/ppermute | solution.py:20
  98.2 15.8 %collective-permute-start.15 = (bf16[48,4096]{1,0:T(8,128)(2,1)S(1)}, bf16[48,4096]{1,0:T(8,128)(2,1)S(1)}, u32[]{:S(2)}, u32[]{:S(2)}) collective-permute-start(bf16[48,4096]{1,0:T(8,128)(2,1)S(1)} %get-tuple-element.60), channel_id=1, source_target_pairs={{0,12},{1,13},{2,14},{3,15},{4,8},{5,9},{6,10},{7,11},{8,4},{9,5},... | collective-permute-start | bytes 1179656 | tf_op jit(solution)/shard_map/ppermute | solution.py:20
  102.4 11.7 %collective-permute-start.9 = (bf16[48,4096]{1,0:T(8,128)(2,1)S(1)}, bf16[48,4096]{1,0:T(8,128)(2,1)S(1)}, u32[]{:S(2)}, u32[]{:S(2)}) collective-permute-start(bf16[48,4096]{1,0:T(8,128)(2,1)S(1)} %get-tuple-element.50), channel_id=1, source_target_pairs={{0,4},{1,5},{2,6},{3,7},{4,0},{5,1},{6,2},{7,3},{8,12},{9,13},{10,... | collective-permute-start | bytes 1179656 | tf_op jit(solution)/shard_map/ppermute | solution.py:20
  103.0 1.4 copy-start.1
  104.4 1.4 copy-start.2
  107.3 3.5 %collective-permute-start.18 = (bf16[768,1024]{1,0:T(8,128)(2,1)S(1)}, bf16[768,1024]{1,0:T(8,128)(2,1)S(1)}, u32[]{:S(2)}, u32[]{:S(2)}) collective-permute-start(bf16[768,1024]{1,0:T(8,128)(2,1)S(1)} %collective-permute-done.17), channel_id=1, source_target_pairs={{0,1},{1,0},{2,3},{3,2},{4,5},{5,4},{6,7},{7,6},{8,9},{9,8},{10,11... | collective-permute-start | bytes 4718600 | tf_op jit(solution)/shard_map/ppermute | solution.py:20
  122.9 6.1 %copy-start.3 = (s32[1,128,1]{1,2,0:T(1,128)S(1)}, s32[1,128,1]{1,2,0:T(1,128)}, u32[]{:S(2)}) copy-start(s32[1,128,1]{1,2,0:T(1,128)} %param.15) | copy-start | bytes 1540
  122.9 6.1 %copy-start.4 = (s32[1,128,1]{1,2,0:T(1,128)S(1)}, s32[1,128,1]{1,2,0:T(1,128)}, u32[]{:S(2)}) copy-start(s32[1,128,1]{1,2,0:T(1,128)} %param.11) | copy-start | bytes 1540
  122.9 6.1 %copy-start.5 = (f32[1,128,1]{1,2,0:T(1,128)S(1)}, f32[1,128,1]{1,2,0:T(1,128)}, u32[]{:S(2)}) copy-start(f32[1,128,1]{1,2,0:T(1,128)} %param.12) | copy-start | bytes 1540
  123.0 28.0 %collective-permute-start.19 = (bf16[48,4096]{1,0:T(8,128)(2,1)S(1)}, bf16[48,4096]{1,0:T(8,128)(2,1)S(1)}, u32[]{:S(2)}, u32[]{:S(2)}) collective-permute-start(bf16[48,4096]{1,0:T(8,128)(2,1)S(1)} %get-tuple-element.85), channel_id=1, source_target_pairs={{0,16},{1,17},{2,18},{3,19},{4,20},{5,21},{6,22},{7,23},{8,24},{9,... | collective-permute-start | bytes 1179656 | tf_op jit(solution)/shard_map/ppermute | solution.py:32
  123.6 27.4 %collective-permute-start.20 = (bf16[48,4096]{1,0:T(8,128)(2,1)S(1)}, bf16[48,4096]{1,0:T(8,128)(2,1)S(1)}, u32[]{:S(2)}, u32[]{:S(2)}) collective-permute-start(bf16[48,4096]{1,0:T(8,128)(2,1)S(1)} %get-tuple-element.84), channel_id=1, source_target_pairs={{0,20},{1,21},{2,22},{3,23},{4,16},{5,17},{6,18},{7,19},{8,28},{9,... | collective-permute-start | bytes 1179656 | tf_op jit(solution)/shard_map/ppermute | solution.py:32
  126.0 28.0 %collective-permute-start.21 = (bf16[48,4096]{1,0:T(8,128)(2,1)S(1)}, bf16[48,4096]{1,0:T(8,128)(2,1)S(1)}, u32[]{:S(2)}, u32[]{:S(2)}) collective-permute-start(bf16[48,4096]{1,0:T(8,128)(2,1)S(1)} %get-tuple-element.83), channel_id=1, source_target_pairs={{0,24},{1,25},{2,26},{3,27},{4,28},{5,29},{6,30},{7,31},{8,16},{9,... | collective-permute-start | bytes 1179656 | tf_op jit(solution)/shard_map/ppermute | solution.py:32
  127.5 34.5 %collective-permute-start.22 = (bf16[48,4096]{1,0:T(8,128)(2,1)S(1)}, bf16[48,4096]{1,0:T(8,128)(2,1)S(1)}, u32[]{:S(2)}, u32[]{:S(2)}) collective-permute-start(bf16[48,4096]{1,0:T(8,128)(2,1)S(1)} %get-tuple-element.82), channel_id=1, source_target_pairs={{0,28},{1,29},{2,30},{3,31},{4,24},{5,25},{6,26},{7,27},{8,20},{9,... | collective-permute-start | bytes 1179656 | tf_op jit(solution)/shard_map/ppermute | solution.py:32
  129.0 22.1 %collective-permute-start.16 = (f32[2,128]{1,0:T(2,128)S(1)}, f32[2,128]{1,0:T(2,128)S(1)}, u32[]{:S(2)}, u32[]{:S(2)}) collective-permute-start(f32[2,128]{1,0:T(2,128)S(1)} %maximum_select_fusion), channel_id=1, source_target_pairs={{0,16},{1,17},{2,18},{3,19},{4,20},{5,21},{6,22},{7,23},{8,24},{9,... | collective-permute-start | bytes 3080 | tf_op jit(solution)/shard_map/ppermute | solution.py:32

commit v4 on v3

--- a/solution.py
+++ b/solution.py
@@ -10,6 +10,37 @@
 QUARTERS = 4
 
 
+def is_inner(place):
+    return (place ^ (place >> 1)) & 1
+
+
+def sent_distances(experts):
+    if experts == 4:
+        return ((0, 0), (2, 1), (1, 2), (3, 3))
+    return tuple((d, d) for d in range(experts))
+
+
+def handed_distances(experts):
+    if experts == 4:
+        return ((3, 0), (2, 1), (1, 2), (0, 3))
+    return tuple((d, d) for d in range(experts))
+
+
+def landed_distances(experts):
+    if experts == 4:
+        return ((3, 0), (1, 2), (2, 1), (0, 3))
+    return tuple((d, d) for d in range(experts))
+
+
+def expert_at(where_ref, distance):
+    outer, inner = distance
+    return where_ref[0] ^ (outer + where_ref[3] * (inner - outer))
+
+
+def target(index, distance):
+    return index ^ (QUARTERS * distance[is_inner(index // QUARTERS)])
+
+
 def after(block, *done):
     return lax.optimization_barrier((block, *done))[0] if done else block
 
@@ -20,10 +51,16 @@
     return lax.ppermute(block, "ep", [(i, i ^ distance) for i in range(count)])
 
 
+def sent(block, distance, *done):
+    block = after(block, *done)
+    count = lax.axis_size("ep")
+    return lax.ppermute(block, "ep", [(i, target(i, distance)) for i in range(count)])
+
+
 def handed(block, steps, distance):
     sections, count = lax.axis_size("pp"), lax.axis_size("ep")
     route = [
-        (s * count + i, (s + by) * count + (i ^ distance))
+        (s * count + i, (s + by) * count + target(i, distance))
         for s in range(sections)
         for by in steps
         if 0 <= s + by < sections
@@ -53,7 +90,7 @@
     value_refs, out_refs = refs[:3], refs[3:]
     quarter = value_refs[0].shape[1] // QUARTERS
     fwd_slots, bwd_slots = [
-        slot_matrix(ref[...], lambda d: where_ref[0] ^ d, slot_cap, experts)
+        slot_matrix(ref[...], lambda d: expert_at(where_ref, sent_distances(experts)[d]), slot_cap, experts)
         for ref in (fwd_ref, bwd_ref)
     ]
     slot_gate = jnp.sum(bwd_slots * gate_ref[...], axis=1, keepdims=True)
@@ -101,7 +138,10 @@
         jnp.sum(jnp.where(low == high, meta_ref[at : at + 1], 0.0), axis=1, keepdims=True)
         for at in range(2)
     ]
-    relative = where_ref[0] ^ lax.broadcasted_iota(jnp.int32, (1, 128), 1)
+    lane = lax.broadcasted_iota(jnp.int32, (1, 128), 1)
+    relative = jnp.full((1, 128), -1, jnp.int32)
+    for d, distance in enumerate(landed_distances(experts)):
+        relative = jnp.where(lane == d, expert_at(where_ref, distance), relative)
     hits = jnp.where(route == relative.astype(jnp.float32), 1.0, 0.0)
     earlier = jnp.where(low < high, 1.0, 0.0).astype(jnp.bfloat16)
     place = jnp.dot(earlier, hits.astype(jnp.bfloat16), preferred_element_type=jnp.float32)
@@ -209,7 +249,9 @@
     slot_cap = 3 * tokens // (2 * experts)
     me = lax.axis_index("ep")
     section = lax.axis_index("pp")
-    where = jnp.stack([me // QUARTERS, me % QUARTERS, section]).astype(jnp.int32)
+    place = me // QUARTERS
+    inner = is_inner(place) if experts == 4 else jnp.zeros_like(place)
+    where = jnp.stack([place, me % QUARTERS, section, inner]).astype(jnp.int32)
 
     gate, up, down = gate_proj[0, 0], up_proj[0, 0], down_proj[0, 0]
     gate_across = paired(gate, 2)
@@ -227,46 +269,46 @@
         experts,
     )
     order = sorted(range(1, experts), reverse=True)
+    distances = sent_distances(experts)
     last = order[-1]
     fwd_blocks, bwd_blocks, grad_blocks = {}, {}, {}
     for d in order:
         before = (up_beside, down_beside) if d == last else ()
-        fwd_blocks[d] = paired(fwd_spread[d], QUARTERS * d, *before)
+        fwd_blocks[d] = sent(fwd_spread[d], distances[d], *before)
     for d in order:
-        bwd_blocks[d] = paired(row_spread[d], QUARTERS * d, fwd_blocks[d])
+        bwd_blocks[d] = sent(row_spread[d], distances[d], fwd_blocks[d])
     down_across = paired(down, 2, gate_across)
     gate_diagonal = paired(gate_across, 1, bwd_blocks[last])
     up_diagonal = paired(up_across, 1, bwd_blocks[last])
-    for d in order:
-        before = (gate_diagonal, up_diagonal) if d == last else (up_across,)
-        grad_blocks[d] = paired(grad_spread[d], QUARTERS * d, bwd_blocks[d], *before)
-    down_diagonal = paired(down_across, 1, up_diagonal)
     near = lax.optimization_barrier((gate_across, down_beside, fwd_blocks[last]))
     gate_across, down_beside = staged(near[:2])
     near = lax.optimization_barrier((up_across, bwd_blocks[last]))
     (up_across,) = staged(near[:1])
     gate_mats = [gate, gate_beside, gate_across, gate_diagonal]
     up_mats = [up, up_beside, up_across, up_diagonal]
-    down_mats = [down, down_beside, down_across, down_diagonal]
     fwd_blocks = [fwd_spread[0]] + [fwd_blocks[d] for d in range(1, experts)]
-    bwd_blocks = [row_spread[0]] + [bwd_blocks[d] for d in range(1, experts)]
-    grad_blocks = [grad_spread[0]] + [grad_blocks[d] for d in range(1, experts)]
 
     rows = jnp.concatenate(fwd_blocks)
     gate_value, up_value = rows_times(rows, gate_mats), rows_times(rows, up_mats)
     hidden = (jax.nn.silu(gate_value) * up_value).astype(jnp.bfloat16)
-    fwd_parts = [
-        jnp.dot(hidden, mat, preferred_element_type=jnp.float32).astype(jnp.bfloat16)
-        for mat in down_mats
-    ]
-
-    rows = jnp.concatenate(bwd_blocks)
+    for d in order:
+        before = () if d == last else (hidden,) if d == order[0] else ()
+        grad_blocks[d] = sent(grad_spread[d], distances[d], bwd_blocks[d], *before)
+    bwd_blocks = [row_spread[0]] + [bwd_blocks[d] for d in range(1, experts)]
+    grad_blocks = [grad_spread[0]] + [grad_blocks[d] for d in range(1, experts)]
+    rows = jnp.concatenate(lax.optimization_barrier((*bwd_blocks, hidden))[:experts])
     gate_value, up_value = rows_times(rows, gate_mats), rows_times(rows, up_mats)
     sigmoid_value = jax.nn.sigmoid(gate_value)
     gate_factor = up_value * sigmoid_value * (1.0 + gate_value * (1.0 - sigmoid_value))
     up_factor = gate_value * sigmoid_value
 
-    landed = lax.optimization_barrier((*grad_blocks[1:], gate_factor, up_factor, *fwd_parts))
+    near_parts = [
+        jnp.dot(hidden, mat, preferred_element_type=jnp.float32).astype(jnp.bfloat16)
+        for mat in (down, down_beside)
+    ]
+    landed = lax.optimization_barrier((*grad_blocks[1:], gate_factor, up_factor, *near_parts))
+    down_across = after(down_across, landed[0])
+    down_mats = [down, down_beside, down_across, paired(down_across, 1)]
     grads = jnp.concatenate([grad_blocks[0], *landed[: experts - 1]])
     quarter = down.shape[1]
     grad_hidden = sum(
@@ -279,7 +321,11 @@
         (contract_cols(grad_gate, g) + contract_cols(grad_up, u)).astype(jnp.bfloat16)
         for g, u in zip(gate_mats, up_mats)
     ]
-    fwd_parts = landed[experts + 1 :]
+    far_parts = [
+        jnp.dot(hidden, mat, preferred_element_type=jnp.float32).astype(jnp.bfloat16)
+        for mat in down_mats[2:]
+    ]
+    fwd_parts = [*landed[experts + 1 :], *far_parts]
     merged = lax.axis_size("pp") == 2
 
     done = tuple(grad_blocks[1:])
@@ -292,15 +338,19 @@
     def returned(parts, steps):
         out = jnp.concatenate(parts, axis=1)
         blocks = [out[d * slot_cap : (d + 1) * slot_cap] for d in range(experts)]
-        return [handed(blocks[d], steps, QUARTERS * d) for d in range(experts)]
+        if experts == 4:
+            edge = jnp.where(inner == 1, blocks[0], blocks[3])
+            core = jnp.where(inner == 1, blocks[3], blocks[0])
+            blocks = [edge, blocks[2], blocks[1], core]
+        return [handed(b, steps, d) for b, d in zip(blocks, handed_distances(experts))]
 
     if merged:
         first = section == 0
-        meta = handed(after(jnp.where(first, fwd_meta, bwd_meta), *done), (1, -1), 0)
+        meta = handed(after(jnp.where(first, fwd_meta, bwd_meta), *done), (1, -1), (0, 0))
         parts = [jnp.where(first, fwd, bwd) for fwd, bwd in zip(fwd_parts, bwd_parts)]
         handed_forward, handed_backward = collect(where, meta, returned(parts, (1, -1)), 2)
     else:
-        metas = [handed(after(m, *done), (by,), 0) for m, by in ((fwd_meta, 1), (bwd_meta, -1))]
+        metas = [handed(after(m, *done), (by,), (0, 0)) for m, by in ((fwd_meta, 1), (bwd_meta, -1))]
         (handed_forward,) = collect(where, metas[0], returned(fwd_parts, (1,)), 1)
         (handed_backward,) = collect(where, metas[1], returned(bwd_parts, (-1,)), 1)
     return handed_forward[None], handed_backward[None]

time: 166 us -> 165 us (level)
    ppermute x0 -> x9, waiting for transfers between devices: none -> 37.1 us  [sent(): lax.ppermute(block, 'ep', [(i, target(i, distance)) for i in range(count)])]
    ppermute x18 -> x9, waiting for transfers between devices: 77.5 us -> 43.3 us  [paired(): return lax.ppermute(block, 'ep', [(i, i ^ distance) for i in range(count)])]
    ppermute x0 -> x9, starting transfers between devices: none -> 13.9 us  [sent(): lax.ppermute(block, 'ep', [(i, target(i, distance)) for i in range(count)])]
    ppermute x18 -> x9, starting transfers between devices: 16.8 us -> 3.3 us  [paired(): return lax.ppermute(block, 'ep', [(i, i ^ distance) for i in range(count)])]
    ppermute x5, waiting for transfers between devices: 32.5 us -> 29 us  [handed(): return lax.ppermute(block, ('pp', 'ep'), route)]
  transfers between devices with their start and end apart: 23 -> 23, of which waited for: 12 -> 11; matrix products, arithmetic and copies ran while one was open for 6% -> 7% of each run, Pallas kernels for 4% -> 4%
where the time goes in v4:
time: 165 us
  waiting for transfers between devices  109 us (66%)
  starting transfers between devices  24.7 us (15%)
  matrix products  18 us (11%)
  Pallas kernels  9.63 us (6%)
    ppermute x9, waiting for transfers between devices, paired(): return lax.ppermute(block, 'ep', [(i, i ^ distance) for i in range(count)])  43.3 us
    ppermute x9, waiting for transfers between devices, sent(): lax.ppermute(block, 'ep', [(i, target(i, distance)) for i in range(count)])  37.1 us
    ppermute x5, waiting for transfers between devices, handed(): return lax.ppermute(block, ('pp', 'ep'), route)  29 us
    ppermute x9, starting transfers between devices, sent(): lax.ppermute(block, 'ep', [(i, target(i, distance)) for i in range(count)])  13.9 us
    dot_general x16, matrix products, rows_times(): jnp.dot(rows[:, j * quarter:(j + 1) * quarter], mat, preferred_element_ty...  8.09 us
    dot_general x12, matrix products, contract_cols(): lax.dot_general(left, right, (((1,), (1,)), ((), ())), preferred_element_...  8.02 us
    ppermute x5, starting transfers between devices, handed(): return lax.ppermute(block, ('pp', 'ep'), route)  7.5 us
    pallas_call x1, Pallas kernels, spread(): pl.pallas_call(functools.partial(spread_kernel, slot_cap, experts), in_sp...  3.54 us
  transfers between devices with their start and end apart: 23, of which 11 were waited for; matrix products, arithmetic and copies ran while one was open for 7% of the time, Pallas kernels for 4%

profile of v4, /device:TPU:14, one launch (start us, length us, event | category | flops | bytes accessed | tf_op | source)
XLA Modules:
  0.0 164.5 jit_solution(18362131308151542517)
XLA Ops:
  1.8 1.5 collective-permute-start.13
  3.4 0.9 collective-permute-done
  4.3 3.5 %shard_map.113 = (bf16[48,4096]{1,0:T(8,128)(2,1)S(1)}, bf16[48,4096]{1,0:T(8,128)(2,1)S(1)}, bf16[48,4096]{1,0:T(8,128)(2,1)S(1)}, bf16[48,4096]{1,0:T(8,128)(2...) custom-call(s32[4]{0:T(128)S(1)} %pad_add_fusion.where_ref, ...), custom_call_target="tpu_custom_call" | custom-call | flops 603979776 | bytes 7864320 | tf_op jit(solution)/shard_map/pallas_call | solution.py:116
  7.9 1.0 collective-permute-done.1
  9.4 2.5 %collective-permute-start.6 = (bf16[48,4096]{1,0:T(8,128)(2,1)S(1)}, bf16[48,4096]{1,0:T(8,128)(2,1)S(1)}, u32[]{:S(2)}, u32[]{:S(2)}) collective-permute-start(bf16[48,4096]{1,0:T(8,128)(2,1)S(1)} %get-tuple-element.53), channel_id=1, source_target_pairs={{0,4},{1,5},{2,6},{3,7},{4,12},{5,13},{6,14},{7,15},{8,0},{9,1},{1... | collective-permute-start | bytes 1179656 | tf_op jit(solution)/shard_map/ppermute | solution.py:57
  11.9 1.6 collective-permute-start.9
  13.5 25.3 %collective-permute-done.11.refs_0_ = bf16[1024,768]{1,0:T(8,128)(2,1)} collective-permute-done((bf16[1024,768]{1,0:T(8,128)(2,1)}, bf16[1024,768]{1,0:T(8,128)(2,1)}, u32[]{:S(2)}, u32[]{:S(2)}) %collective-permute-start.11) | collective-permute-done | bytes 1572896 | tf_op jit(solution)/shard_map/ppermute | solution.py:51
  39.9 2.5 %collective-permute-start.7 = (bf16[48,4096]{1,0:T(8,128)(2,1)S(1)}, bf16[48,4096]{1,0:T(8,128)(2,1)S(1)}, u32[]{:S(2)}, u32[]{:S(2)}) collective-permute-start(bf16[48,4096]{1,0:T(8,128)(2,1)S(1)} %get-tuple-element.54), channel_id=1, source_target_pairs={{0,4},{1,5},{2,6},{3,7},{4,12},{5,13},{6,14},{7,15},{8,0},{9,1},{1... | collective-permute-start | bytes 1179656 | tf_op jit(solution)/shard_map/ppermute | solution.py:57
  42.4 12.4 %collective-permute-done.9 = bf16[48,4096]{1,0:T(8,128)(2,1)S(1)} collective-permute-done((bf16[48,4096]{1,0:T(8,128)(2,1)S(1)}, bf16[48,4096]{1,0:T(8,128)(2,1)S(1)}, u32[]{:S(2)}, u32[]{:S(2)}) %collective-permute-start.9) | collective-permute-done | bytes 393248 | tf_op jit(solution)/shard_map/ppermute | solution.py:57
  54.8 1.6 collective-permute-start.10
  56.4 1.9 %shard_map.114 = (bf16[1024,768]{1,0:T(8,128)(2,1)S(1)}, bf16[768,1024]{1,0:T(8,128)(2,1)S(1)}) custom-call(bf16[1024,768]{1,0:T(8,128)(2,1)} %collective-permute-done.11.refs_0_, bf16[768,1024]{1,0:T(8,128)(2,1)} %collective-permute-done.2.refs_1_), custom_call_target="tpu_custom_call" | custom-call | bytes 6291456 | tf_op jit(solution)/shard_map/pallas_call | solution.py:203
  58.5 14.0 %collective-permute-done.13.refs_0_ = bf16[1024,768]{1,0:T(8,128)(2,1)} collective-permute-done((bf16[1024,768]{1,0:T(8,128)(2,1)}, bf16[1024,768]{1,0:T(8,128)(2,1)}, u32[]{:S(2)}, u32[]{:S(2)}) %collective-permute-start.13) | collective-permute-done | bytes 1572896 | tf_op jit(solution)/shard_map/ppermute | solution.py:51
  74.0 1.4 shard_map.115
  76.4 2.7 %collective-permute-start.8 = (bf16[48,4096]{1,0:T(8,128)(2,1)S(1)}, bf16[48,4096]{1,0:T(8,128)(2,1)S(1)}, u32[]{:S(2)}, u32[]{:S(2)}) collective-permute-start(bf16[48,4096]{1,0:T(8,128)(2,1)S(1)} %get-tuple-element.55), channel_id=1, source_target_pairs={{0,4},{1,5},{2,6},{3,7},{4,12},{5,13},{6,14},{7,15},{8,0},{9,1},{1... | collective-permute-start | bytes 1179656 | tf_op jit(solution)/shard_map/ppermute | solution.py:57
  80.7 0.9 copy-done.2
  82.2 6.3 %collective-permute-done.10 = bf16[48,4096]{1,0:T(8,128)(2,1)S(1)} collective-permute-done((bf16[48,4096]{1,0:T(8,128)(2,1)S(1)}, bf16[48,4096]{1,0:T(8,128)(2,1)S(1)}, u32[]{:S(2)}, u32[]{:S(2)}) %collective-permute-start.10) | collective-permute-done | bytes 393248 | tf_op jit(solution)/shard_map/ppermute | solution.py:57
  89.6 1.6 collective-permute-start.15
  95.4 9.0 %collective-permute-done.8 = bf16[48,4096]{1,0:T(8,128)(2,1)S(1)} collective-permute-done((bf16[48,4096]{1,0:T(8,128)(2,1)S(1)}, bf16[48,4096]{1,0:T(8,128)(2,1)S(1)}, u32[]{:S(2)}, u32[]{:S(2)}) %collective-permute-start.8) | collective-permute-done | bytes 393248 | tf_op jit(solution)/shard_map/ppermute | solution.py:57
  104.4 9.3 %collective-permute-done.15 = bf16[48,4096]{1,0:T(8,128)(2,1)S(1)} collective-permute-done((bf16[48,4096]{1,0:T(8,128)(2,1)S(1)}, bf16[48,4096]{1,0:T(8,128)(2,1)S(1)}, u32[]{:S(2)}, u32[]{:S(2)}) %collective-permute-start.15) | collective-permute-done | bytes 393248 | tf_op jit(solution)/shard_map/ppermute | solution.py:57
  113.8 0.7 fusion.18
  114.5 0.7 convolution_add_fusion.5
  115.2 1.9 %collective-permute-done.18 = bf16[768,1024]{1,0:T(8,128)(2,1)S(1)} collective-permute-done((bf16[768,1024]{1,0:T(8,128)(2,1)S(1)}, bf16[768,1024]{1,0:T(8,128)(2,1)S(1)}, u32[]{:S(2)}, u32[]{:S(2)}) %collective-permute-start.18) | collective-permute-done | bytes 1572896 | tf_op jit(solution)/shard_map/ppermute | solution.py:51
  117.1 0.7 fusion.14
  117.8 0.7 multiply_convert_fusion.1
  119.8 0.7 fusion.2
  120.5 0.7 fusion
  122.3 0.7 fusion.1
  123.7 0.7 fusion.3
  125.7 3.8 %collective-permute-start.21 = (bf16[48,4096]{1,0:T(8,128)(2,1)S(1)}, bf16[48,4096]{1,0:T(8,128)(2,1)S(1)}, u32[]{:S(2)}, u32[]{:S(2)}) collective-permute-start(bf16[48,4096]{1,0:T(8,128)(2,1)S(1)} %get-tuple-element.87), channel_id=1, source_target_pairs={{0,20},{1,21},{2,22},{3,23},{4,28},{5,29},{6,30},{7,31},{8,16},{9,... | collective-permute-start | bytes 1179656 | tf_op jit(solution)/shard_map/ppermute | solution.py:69
  129.6 2.5 %collective-permute-start.22 = (bf16[48,4096]{1,0:T(8,128)(2,1)S(1)}, bf16[48,4096]{1,0:T(8,128)(2,1)S(1)}, u32[]{:S(2)}, u32[]{:S(2)}) collective-permute-start(bf16[48,4096]{1,0:T(8,128)(2,1)S(1)} %get-tuple-element.86), channel_id=1, source_target_pairs={{0,16},{1,17},{2,18},{3,19},{4,24},{5,25},{6,26},{7,27},{8,20},{9,... | collective-permute-start | bytes 1179656 | tf_op jit(solution)/shard_map/ppermute | solution.py:69
  132.7 29.0 %collective-permute-done.16.meta_ref = f32[2,128]{1,0:T(2,128)S(1)} collective-permute-done((f32[2,128]{1,0:T(2,128)S(1)}, f32[2,128]{1,0:T(2,128)S(1)}, u32[]{:S(2)}, u32[]{:S(2)}) %collective-permute-start.16) | collective-permute-done | bytes 1056 | tf_op jit(solution)/shard_map/ppermute | solution.py:69
  161.8 2.8 %shard_map.116 = (bf16[128,4096]{1,0:T(8,128)(2,1)}, bf16[128,4096]{1,0:T(8,128)(2,1)}) custom-call(s32[4]{0:T(128)S(1)} %pad_add_fusion.where_ref, f32[2,128]{1,0:T(2,128)S(1)} %collective-permute-done.16.meta_ref, bf16[48,4096]{1,0:T(8,128)(2,1)S(1)} %collective-permute-done.19.refs_0_, bf16[48,4096]{1,0:T(8,128)(2,1)S(1)} %collective-permute-done.20.refs_1_, ...), custom_call_target="tpu_custom_call" | custom-call | flops 201326592 | bytes 3670016 | tf_op jit(solution)/shard_map/pallas_call | solution.py:175
  (80 shorter events, 18.0 us)
Async XLA Ops:
  0.6 3.7 %collective-permute-start = (bf16[1024,768]{1,0:T(8,128)(2,1)}, bf16[1024,768]{1,0:T(8,128)(2,1)S(1)}, u32[]{:S(2)}, u32[]{:S(2)}) collective-permute-start(bf16[1024,768]{1,0:T(8,128)(2,1)} %bitcast.70), channel_id=1, source_target_pairs={{0,1},{1,0},{2,3},{3,2},{4,5},{5,4},{6,7},{7,6},{8,9},{9,8},{10,11... | collective-permute-start | bytes 4718600 | tf_op jit(solution)/shard_map/ppermute | solution.py:51
  0.7 8.1 %collective-permute-start.1 = (bf16[1024,768]{1,0:T(8,128)(2,1)}, bf16[1024,768]{1,0:T(8,128)(2,1)S(1)}, u32[]{:S(2)}, u32[]{:S(2)}) collective-permute-start(bf16[1024,768]{1,0:T(8,128)(2,1)} %bitcast.74), channel_id=1, source_target_pairs={{0,1},{1,0},{2,3},{3,2},{4,5},{5,4},{6,7},{7,6},{8,9},{9,8},{10,11... | collective-permute-start | bytes 4718600 | tf_op jit(solution)/shard_map/ppermute | solution.py:51
  1.2 7.7 %collective-permute-start.2 = (bf16[768,1024]{1,0:T(8,128)(2,1)}, bf16[768,1024]{1,0:T(8,128)(2,1)}, u32[]{:S(2)}, u32[]{:S(2)}) collective-permute-start(bf16[768,1024]{1,0:T(8,128)(2,1)} %bitcast.72), channel_id=1, source_target_pairs={{0,1},{1,0},{2,3},{3,2},{4,5},{5,4},{6,7},{7,6},{8,9},{9,8},{10,11... | collective-permute-start | bytes 4718600 | tf_op jit(solution)/shard_map/ppermute | solution.py:51
  1.3 37.5 %collective-permute-start.11 = (bf16[1024,768]{1,0:T(8,128)(2,1)}, bf16[1024,768]{1,0:T(8,128)(2,1)}, u32[]{:S(2)}, u32[]{:S(2)}) collective-permute-start(bf16[1024,768]{1,0:T(8,128)(2,1)} %bitcast.71), channel_id=1, source_target_pairs={{0,2},{1,3},{2,0},{3,1},{4,6},{5,7},{6,4},{7,5},{8,10},{9,11},{10,... | collective-permute-start | bytes 4718600 | tf_op jit(solution)/shard_map/ppermute | solution.py:51
  1.8 70.7 %collective-permute-start.13 = (bf16[1024,768]{1,0:T(8,128)(2,1)}, bf16[1024,768]{1,0:T(8,128)(2,1)}, u32[]{:S(2)}, u32[]{:S(2)}) collective-permute-start(bf16[1024,768]{1,0:T(8,128)(2,1)} %bitcast.75), channel_id=1, source_target_pairs={{0,2},{1,3},{2,0},{3,1},{4,6},{5,7},{6,4},{7,5},{8,10},{9,11},{10,... | collective-permute-start | bytes 4718600 | tf_op jit(solution)/shard_map/ppermute | solution.py:51
  4.3 34.5 %copy-start.1 = (bf16[1,1,768,1024]{3,2,1,0:T(8,128)(2,1)S(1)}, bf16[1,1,768,1024]{3,2,1,0:T(8,128)(2,1)}, u32[]{:S(2)}) copy-start(bf16[1,1,768,1024]{3,2,1,0:T(8,128)(2,1)} %param.19) | copy-start | bytes 4718596
  8.9 30.4 %collective-permute-start.3 = (bf16[48,4096]{1,0:T(8,128)(2,1)S(1)}, bf16[48,4096]{1,0:T(8,128)(2,1)S(1)}, u32[]{:S(2)}, u32[]{:S(2)}) collective-permute-start(bf16[48,4096]{1,0:T(8,128)(2,1)S(1)} %get-tuple-element.48), channel_id=1, source_target_pairs={{0,8},{1,9},{2,10},{3,11},{4,0},{5,1},{6,2},{7,3},{8,12},{9,13},{1... | collective-permute-start | bytes 1179656 | tf_op jit(solution)/shard_map/ppermute | solution.py:57
  9.4 30.5 %collective-permute-start.6 = (bf16[48,4096]{1,0:T(8,128)(2,1)S(1)}, bf16[48,4096]{1,0:T(8,128)(2,1)S(1)}, u32[]{:S(2)}, u32[]{:S(2)}) collective-permute-start(bf16[48,4096]{1,0:T(8,128)(2,1)S(1)} %get-tuple-element.53), channel_id=1, source_target_pairs={{0,4},{1,5},{2,6},{3,7},{4,12},{5,13},{6,14},{7,15},{8,0},{9,1},{1... | collective-permute-start | bytes 1179656 | tf_op jit(solution)/shard_map/ppermute | solution.py:57
  11.9 42.9 %collective-permute-start.9 = (bf16[48,4096]{1,0:T(8,128)(2,1)S(1)}, bf16[48,4096]{1,0:T(8,128)(2,1)S(1)}, u32[]{:S(2)}, u32[]{:S(2)}) collective-permute-start(bf16[48,4096]{1,0:T(8,128)(2,1)S(1)} %get-tuple-element.58), channel_id=1, source_target_pairs={{0,12},{1,13},{2,14},{3,15},{4,8},{5,9},{6,10},{7,11},{8,4},{9,5},... | collective-permute-start | bytes 1179656 | tf_op jit(solution)/shard_map/ppermute | solution.py:57
  38.8 74.9 %collective-permute-start.17 = (bf16[768,1024]{1,0:T(8,128)(2,1)S(1)}, bf16[768,1024]{1,0:T(8,128)(2,1)S(1)}, u32[]{:S(2)}, u32[]{:S(2)}) collective-permute-start(bf16[768,1024]{1,0:T(8,128)(2,1)S(1)} %bitcast.73), channel_id=1, source_target_pairs={{0,2},{1,3},{2,0},{3,1},{4,6},{5,7},{6,4},{7,5},{8,10},{9,11},{10,... | collective-permute-start | bytes 4718600 | tf_op jit(solution)/shard_map/ppermute | solution.py:51
  39.4 19.0 %collective-permute-start.4 = (bf16[48,4096]{1,0:T(8,128)(2,1)S(1)}, bf16[48,4096]{1,0:T(8,128)(2,1)S(1)}, u32[]{:S(2)}, u32[]{:S(2)}) collective-permute-start(bf16[48,4096]{1,0:T(8,128)(2,1)S(1)} %get-tuple-element.49), channel_id=1, source_target_pairs={{0,8},{1,9},{2,10},{3,11},{4,0},{5,1},{6,2},{7,3},{8,12},{9,13},{1... | collective-permute-start | bytes 1179656 | tf_op jit(solution)/shard_map/ppermute | solution.py:57
  39.9 35.5 %collective-permute-start.7 = (bf16[48,4096]{1,0:T(8,128)(2,1)S(1)}, bf16[48,4096]{1,0:T(8,128)(2,1)S(1)}, u32[]{:S(2)}, u32[]{:S(2)}) collective-permute-start(bf16[48,4096]{1,0:T(8,128)(2,1)S(1)} %get-tuple-element.54), channel_id=1, source_target_pairs={{0,4},{1,5},{2,6},{3,7},{4,12},{5,13},{6,14},{7,15},{8,0},{9,1},{1... | collective-permute-start | bytes 1179656 | tf_op jit(solution)/shard_map/ppermute | solution.py:57
  54.8 33.7 %collective-permute-start.10 = (bf16[48,4096]{1,0:T(8,128)(2,1)S(1)}, bf16[48,4096]{1,0:T(8,128)(2,1)S(1)}, u32[]{:S(2)}, u32[]{:S(2)}) collective-permute-start(bf16[48,4096]{1,0:T(8,128)(2,1)S(1)} %get-tuple-element.59), channel_id=1, source_target_pairs={{0,12},{1,13},{2,14},{3,15},{4,8},{5,9},{6,10},{7,11},{8,4},{9,5},... | collective-permute-start | bytes 1179656 | tf_op jit(solution)/shard_map/ppermute | solution.py:57
  58.4 18.1 %collective-permute-start.12 = (bf16[1024,768]{1,0:T(8,128)(2,1)}, bf16[1024,768]{1,0:T(8,128)(2,1)S(1)}, u32[]{:S(2)}, u32[]{:S(2)}) collective-permute-start(bf16[1024,768]{1,0:T(8,128)(2,1)} %collective-permute-done.11.refs_0_), channel_id=1, source_target_pairs={{0,1},{1,0},{2,3},{3,2},{4,5},{5,4},{6,7},{7,6},{8,9},{9,8},{10,11... | collective-permute-start | bytes 4718600 | tf_op jit(solution)/shard_map/ppermute | solution.py:51
  72.5 7.7 %collective-permute-start.14 = (bf16[1024,768]{1,0:T(8,128)(2,1)}, bf16[1024,768]{1,0:T(8,128)(2,1)S(1)}, u32[]{:S(2)}, u32[]{:S(2)}) collective-permute-start(bf16[1024,768]{1,0:T(8,128)(2,1)} %collective-permute-done.13.refs_0_), channel_id=1, source_target_pairs={{0,1},{1,0},{2,3},{3,2},{4,5},{5,4},{6,7},{7,6},{8,9},{9,8},{10,11... | collective-permute-start | bytes 4718600 | tf_op jit(solution)/shard_map/ppermute | solution.py:51
  75.4 20.0 %collective-permute-start.5 = (bf16[48,4096]{1,0:T(8,128)(2,1)S(1)}, bf16[48,4096]{1,0:T(8,128)(2,1)S(1)}, u32[]{:S(2)}, u32[]{:S(2)}) collective-permute-start(bf16[48,4096]{1,0:T(8,128)(2,1)S(1)} %get-tuple-element.50), channel_id=1, source_target_pairs={{0,8},{1,9},{2,10},{3,11},{4,0},{5,1},{6,2},{7,3},{8,12},{9,13},{1... | collective-permute-start | bytes 1179656 | tf_op jit(solution)/shard_map/ppermute | solution.py:57
  76.4 3.2 %copy-start = (bf16[1,1,1024,768]{3,2,1,0:T(8,128)(2,1)S(1)}, bf16[1,1,1024,768]{3,2,1,0:T(8,128)(2,1)}, u32[]{:S(2)}) copy-start(bf16[1,1,1024,768]{3,2,1,0:T(8,128)(2,1)} %param.17) | copy-start | bytes 4718596
  76.4 28.0 %collective-permute-start.8 = (bf16[48,4096]{1,0:T(8,128)(2,1)S(1)}, bf16[48,4096]{1,0:T(8,128)(2,1)S(1)}, u32[]{:S(2)}, u32[]{:S(2)}) collective-permute-start(bf16[48,4096]{1,0:T(8,128)(2,1)S(1)} %get-tuple-element.55), channel_id=1, source_target_pairs={{0,4},{1,5},{2,6},{3,7},{4,12},{5,13},{6,14},{7,15},{8,0},{9,1},{1... | collective-permute-start | bytes 1179656 | tf_op jit(solution)/shard_map/ppermute | solution.py:57
  80.2 1.4 copy-start.2
  89.6 24.1 %collective-permute-start.15 = (bf16[48,4096]{1,0:T(8,128)(2,1)S(1)}, bf16[48,4096]{1,0:T(8,128)(2,1)S(1)}, u32[]{:S(2)}, u32[]{:S(2)}) collective-permute-start(bf16[48,4096]{1,0:T(8,128)(2,1)S(1)} %get-tuple-element.66), channel_id=1, source_target_pairs={{0,12},{1,13},{2,14},{3,15},{4,8},{5,9},{6,10},{7,11},{8,4},{9,5},... | collective-permute-start | bytes 1179656 | tf_op jit(solution)/shard_map/ppermute | solution.py:57
  113.7 3.4 %collective-permute-start.18 = (bf16[768,1024]{1,0:T(8,128)(2,1)S(1)}, bf16[768,1024]{1,0:T(8,128)(2,1)S(1)}, u32[]{:S(2)}, u32[]{:S(2)}) collective-permute-start(bf16[768,1024]{1,0:T(8,128)(2,1)S(1)} %collective-permute-done.17), channel_id=1, source_target_pairs={{0,1},{1,0},{2,3},{3,2},{4,5},{5,4},{6,7},{7,6},{8,9},{9,8},{10,11... | collective-permute-start | bytes 4718600 | tf_op jit(solution)/shard_map/ppermute | solution.py:51
  125.0 7.1 %copy-start.3 = (s32[1,128,1]{1,2,0:T(1,128)S(1)}, s32[1,128,1]{1,2,0:T(1,128)}, u32[]{:S(2)}) copy-start(s32[1,128,1]{1,2,0:T(1,128)} %param.15) | copy-start | bytes 1540
  125.0 7.1 %copy-start.4 = (s32[1,128,1]{1,2,0:T(1,128)S(1)}, s32[1,128,1]{1,2,0:T(1,128)}, u32[]{:S(2)}) copy-start(s32[1,128,1]{1,2,0:T(1,128)} %param.11) | copy-start | bytes 1540
  125.0 7.1 %copy-start.5 = (f32[1,128,1]{1,2,0:T(1,128)S(1)}, f32[1,128,1]{1,2,0:T(1,128)}, u32[]{:S(2)}) copy-start(f32[1,128,1]{1,2,0:T(1,128)} %param.12) | copy-start | bytes 1540
  125.2 36.6 %collective-permute-start.19 = (bf16[48,4096]{1,0:T(8,128)(2,1)S(1)}, bf16[48,4096]{1,0:T(8,128)(2,1)S(1)}, u32[]{:S(2)}, u32[]{:S(2)}) collective-permute-start(bf16[48,4096]{1,0:T(8,128)(2,1)S(1)} %get-tuple-element.89), channel_id=1, source_target_pairs={{0,28},{1,29},{2,30},{3,31},{4,20},{5,21},{6,22},{7,23},{8,24},{9,... | collective-permute-start | bytes 1179656 | tf_op jit(solution)/shard_map/ppermute | solution.py:69
  125.7 36.0 %collective-permute-start.20 = (bf16[48,4096]{1,0:T(8,128)(2,1)S(1)}, bf16[48,4096]{1,0:T(8,128)(2,1)S(1)}, u32[]{:S(2)}, u32[]{:S(2)}) collective-permute-start(bf16[48,4096]{1,0:T(8,128)(2,1)S(1)} %get-tuple-element.88), channel_id=1, source_target_pairs={{0,24},{1,25},{2,26},{3,27},{4,16},{5,17},{6,18},{7,19},{8,28},{9,... | collective-permute-start | bytes 1179656 | tf_op jit(solution)/shard_map/ppermute | solution.py:69
  125.7 36.0 %collective-permute-start.21 = (bf16[48,4096]{1,0:T(8,128)(2,1)S(1)}, bf16[48,4096]{1,0:T(8,128)(2,1)S(1)}, u32[]{:S(2)}, u32[]{:S(2)}) collective-permute-start(bf16[48,4096]{1,0:T(8,128)(2,1)S(1)} %get-tuple-element.87), channel_id=1, source_target_pairs={{0,20},{1,21},{2,22},{3,23},{4,28},{5,29},{6,30},{7,31},{8,16},{9,... | collective-permute-start | bytes 1179656 | tf_op jit(solution)/shard_map/ppermute | solution.py:69
  129.6 32.2 %collective-permute-start.22 = (bf16[48,4096]{1,0:T(8,128)(2,1)S(1)}, bf16[48,4096]{1,0:T(8,128)(2,1)S(1)}, u32[]{:S(2)}, u32[]{:S(2)}) collective-permute-start(bf16[48,4096]{1,0:T(8,128)(2,1)S(1)} %get-tuple-element.86), channel_id=1, source_target_pairs={{0,16},{1,17},{2,18},{3,19},{4,24},{5,25},{6,26},{7,27},{8,20},{9,... | collective-permute-start | bytes 1179656 | tf_op jit(solution)/shard_map/ppermute | solution.py:69
  132.1 29.6 %collective-permute-start.16 = (f32[2,128]{1,0:T(2,128)S(1)}, f32[2,128]{1,0:T(2,128)S(1)}, u32[]{:S(2)}, u32[]{:S(2)}) collective-permute-start(f32[2,128]{1,0:T(2,128)S(1)} %maximum_select_fusion), channel_id=1, source_target_pairs={{0,16},{1,17},{2,18},{3,19},{4,20},{5,21},{6,22},{7,23},{8,24},{9,... | collective-permute-start | bytes 3080 | tf_op jit(solution)/shard_map/ppermute | solution.py:69

commit v5 on v4

--- a/solution.py
+++ b/solution.py
@@ -280,35 +280,36 @@
     down_across = paired(down, 2, gate_across)
     gate_diagonal = paired(gate_across, 1, bwd_blocks[last])
     up_diagonal = paired(up_across, 1, bwd_blocks[last])
+    for d in order:
+        before = (gate_diagonal, up_diagonal) if d == last else (up_across,)
+        grad_blocks[d] = sent(grad_spread[d], distances[d], bwd_blocks[d], *before)
+    down_diagonal = paired(down_across, 1, up_diagonal)
     near = lax.optimization_barrier((gate_across, down_beside, fwd_blocks[last]))
     gate_across, down_beside = staged(near[:2])
     near = lax.optimization_barrier((up_across, bwd_blocks[last]))
     (up_across,) = staged(near[:1])
     gate_mats = [gate, gate_beside, gate_across, gate_diagonal]
     up_mats = [up, up_beside, up_across, up_diagonal]
+    down_mats = [down, down_beside, down_across, down_diagonal]
     fwd_blocks = [fwd_spread[0]] + [fwd_blocks[d] for d in range(1, experts)]
+    bwd_blocks = [row_spread[0]] + [bwd_blocks[d] for d in range(1, experts)]
+    grad_blocks = [grad_spread[0]] + [grad_blocks[d] for d in range(1, experts)]
 
     rows = jnp.concatenate(fwd_blocks)
     gate_value, up_value = rows_times(rows, gate_mats), rows_times(rows, up_mats)
     hidden = (jax.nn.silu(gate_value) * up_value).astype(jnp.bfloat16)
-    for d in order:
-        before = () if d == last else (hidden,) if d == order[0] else ()
-        grad_blocks[d] = sent(grad_spread[d], distances[d], bwd_blocks[d], *before)
-    bwd_blocks = [row_spread[0]] + [bwd_blocks[d] for d in range(1, experts)]
-    grad_blocks = [grad_spread[0]] + [grad_blocks[d] for d in range(1, experts)]
-    rows = jnp.concatenate(lax.optimization_barrier((*bwd_blocks, hidden))[:experts])
+    fwd_parts = [
+        jnp.dot(hidden, mat, preferred_element_type=jnp.float32).astype(jnp.bfloat16)
+        for mat in down_mats
+    ]
+
+    rows = jnp.concatenate(bwd_blocks)
     gate_value, up_value = rows_times(rows, gate_mats), rows_times(rows, up_mats)
     sigmoid_value = jax.nn.sigmoid(gate_value)
     gate_factor = up_value * sigmoid_value * (1.0 + gate_value * (1.0 - sigmoid_value))
     up_factor = gate_value * sigmoid_value
 
-    near_parts = [
-        jnp.dot(hidden, mat, preferred_element_type=jnp.float32).astype(jnp.bfloat16)
-        for mat in (down, down_beside)
-    ]
-    landed = lax.optimization_barrier((*grad_blocks[1:], gate_factor, up_factor, *near_parts))
-    down_across = after(down_across, landed[0])
-    down_mats = [down, down_beside, down_across, paired(down_across, 1)]
+    landed = lax.optimization_barrier((*grad_blocks[1:], gate_factor, up_factor, *fwd_parts))
     grads = jnp.concatenate([grad_blocks[0], *landed[: experts - 1]])
     quarter = down.shape[1]
     grad_hidden = sum(
@@ -321,11 +322,7 @@
         (contract_cols(grad_gate, g) + contract_cols(grad_up, u)).astype(jnp.bfloat16)
         for g, u in zip(gate_mats, up_mats)
     ]
-    far_parts = [
-        jnp.dot(hidden, mat, preferred_element_type=jnp.float32).astype(jnp.bfloat16)
-        for mat in down_mats[2:]
-    ]
-    fwd_parts = [*landed[experts + 1 :], *far_parts]
+    fwd_parts = landed[experts + 1 :]
     merged = lax.axis_size("pp") == 2
 
     done = tuple(grad_blocks[1:])

time: 165 us -> 162 us (0.982)
  waiting for transfers between devices: 109 us -> 106 us
    ppermute x9, waiting for transfers between devices: 37.1 us -> 19.6 us  [sent(): lax.ppermute(block, 'ep', [(i, target(i, distance)) for i in range(count)])]
    ppermute x9, waiting for transfers between devices: 43.3 us -> 57.1 us  [paired(): return lax.ppermute(block, 'ep', [(i, i ^ distance) for i in range(count)])]
  transfers between devices with their start and end apart: 23 -> 23, of which waited for: 11 -> 11; matrix products, arithmetic and copies ran while one was open for 7% -> 6% of each run, Pallas kernels for 4% -> 4%
where the time goes in v5:
time: 162 us
  waiting for transfers between devices  106 us (65%)
  starting transfers between devices  24.7 us (15%)
  matrix products  18.1 us (11%)
  Pallas kernels  9.51 us (6%)
  local copies, waits for them, and re-layouts  2.14 us (1%)
    ppermute x9, waiting for transfers between devices, paired(): return lax.ppermute(block, 'ep', [(i, i ^ distance) for i in range(count)])  57.1 us
    ppermute x5, waiting for transfers between devices, handed(): return lax.ppermute(block, ('pp', 'ep'), route)  28.9 us
    ppermute x9, waiting for transfers between devices, sent(): lax.ppermute(block, 'ep', [(i, target(i, distance)) for i in range(count)])  19.6 us
    ppermute x9, starting transfers between devices, sent(): lax.ppermute(block, 'ep', [(i, target(i, distance)) for i in range(count)])  13.5 us
    dot_general x16, matrix products, rows_times(): jnp.dot(rows[:, j * quarter:(j + 1) * quarter], mat, preferred_element_ty...  8.09 us
    dot_general x12, matrix products, contract_cols(): lax.dot_general(left, right, (((1,), (1,)), ((), ())), preferred_element_...  8.05 us
    ppermute x5, starting transfers between devices, handed(): return lax.ppermute(block, ('pp', 'ep'), route)  7.48 us
    ppermute x9, starting transfers between devices, paired(): return lax.ppermute(block, 'ep', [(i, i ^ distance) for i in range(count)])  3.79 us
  transfers between devices with their start and end apart: 23, of which 11 were waited for; matrix products, arithmetic and copies ran while one was open for 6% of the time, Pallas kernels for 4%

profile of v5, /device:TPU:14, one launch (start us, length us, event | category | flops | bytes accessed | tf_op | source)
XLA Modules:
  0.0 161.8 jit_solution(13786293244270466308)
XLA Ops:
  1.8 1.5 collective-permute-start.7
  3.4 0.9 collective-permute-done
  4.3 3.4 %shard_map.113 = (bf16[48,4096]{1,0:T(8,128)(2,1)S(1)}, bf16[48,4096]{1,0:T(8,128)(2,1)S(1)}, bf16[48,4096]{1,0:T(8,128)(2,1)S(1)}, bf16[48,4096]{1,0:T(8,128)(2...) custom-call(s32[4]{0:T(128)S(1)} %pad_add_fusion.where_ref, ...), custom_call_target="tpu_custom_call" | custom-call | flops 603979776 | bytes 7864320 | tf_op jit(solution)/shard_map/pallas_call | solution.py:116
  7.8 1.1 collective-permute-done.1
  9.4 2.5 %collective-permute-start.10 = (bf16[48,4096]{1,0:T(8,128)(2,1)S(1)}, bf16[48,4096]{1,0:T(8,128)(2,1)S(1)}, u32[]{:S(2)}, u32[]{:S(2)}) collective-permute-start(bf16[48,4096]{1,0:T(8,128)(2,1)S(1)} %get-tuple-element.53), channel_id=1, source_target_pairs={{0,4},{1,5},{2,6},{3,7},{4,12},{5,13},{6,14},{7,15},{8,0},{9,1},{1... | collective-permute-start | bytes 1179656 | tf_op jit(solution)/shard_map/ppermute | solution.py:57
  11.9 1.6 collective-permute-start.13
  13.5 25.3 %collective-permute-done.5.refs_0_ = bf16[1024,768]{1,0:T(8,128)(2,1)} collective-permute-done((bf16[1024,768]{1,0:T(8,128)(2,1)}, bf16[1024,768]{1,0:T(8,128)(2,1)}, u32[]{:S(2)}, u32[]{:S(2)}) %collective-permute-start.5) | collective-permute-done | bytes 1572896 | tf_op jit(solution)/shard_map/ppermute | solution.py:51
  39.9 2.5 %collective-permute-start.11 = (bf16[48,4096]{1,0:T(8,128)(2,1)S(1)}, bf16[48,4096]{1,0:T(8,128)(2,1)S(1)}, u32[]{:S(2)}, u32[]{:S(2)}) collective-permute-start(bf16[48,4096]{1,0:T(8,128)(2,1)S(1)} %get-tuple-element.54), channel_id=1, source_target_pairs={{0,4},{1,5},{2,6},{3,7},{4,12},{5,13},{6,14},{7,15},{8,0},{9,1},{1... | collective-permute-start | bytes 1179656 | tf_op jit(solution)/shard_map/ppermute | solution.py:57
  42.4 12.4 %collective-permute-done.13 = bf16[48,4096]{1,0:T(8,128)(2,1)S(1)} collective-permute-done((bf16[48,4096]{1,0:T(8,128)(2,1)S(1)}, bf16[48,4096]{1,0:T(8,128)(2,1)S(1)}, u32[]{:S(2)}, u32[]{:S(2)}) %collective-permute-start.13) | collective-permute-done | bytes 393248 | tf_op jit(solution)/shard_map/ppermute | solution.py:57
  54.8 1.6 collective-permute-start.14
  56.4 1.9 %shard_map.115 = (bf16[1024,768]{1,0:T(8,128)(2,1)S(1)}, bf16[768,1024]{1,0:T(8,128)(2,1)S(1)}) custom-call(bf16[1024,768]{1,0:T(8,128)(2,1)} %collective-permute-done.5.refs_0_, bf16[768,1024]{1,0:T(8,128)(2,1)} %collective-permute-done.2.refs_1_), custom_call_target="tpu_custom_call" | custom-call | bytes 6291456 | tf_op jit(solution)/shard_map/pallas_call | solution.py:203
  59.9 12.6 %collective-permute-done.7.refs_0_ = bf16[1024,768]{1,0:T(8,128)(2,1)} collective-permute-done((bf16[1024,768]{1,0:T(8,128)(2,1)}, bf16[1024,768]{1,0:T(8,128)(2,1)}, u32[]{:S(2)}, u32[]{:S(2)}) %collective-permute-start.7) | collective-permute-done | bytes 1572896 | tf_op jit(solution)/shard_map/ppermute | solution.py:51
  72.5 1.4 shard_map.114
  74.5 2.6 %collective-permute-start.12 = (bf16[48,4096]{1,0:T(8,128)(2,1)S(1)}, bf16[48,4096]{1,0:T(8,128)(2,1)S(1)}, u32[]{:S(2)}, u32[]{:S(2)}) collective-permute-start(bf16[48,4096]{1,0:T(8,128)(2,1)S(1)} %get-tuple-element.55), channel_id=1, source_target_pairs={{0,4},{1,5},{2,6},{3,7},{4,12},{5,13},{6,14},{7,15},{8,0},{9,1},{1... | collective-permute-start | bytes 1179656 | tf_op jit(solution)/shard_map/ppermute | solution.py:57
  77.1 3.0 %collective-permute-done.14 = bf16[48,4096]{1,0:T(8,128)(2,1)S(1)} collective-permute-done((bf16[48,4096]{1,0:T(8,128)(2,1)S(1)}, bf16[48,4096]{1,0:T(8,128)(2,1)S(1)}, u32[]{:S(2)}, u32[]{:S(2)}) %collective-permute-start.14) | collective-permute-done | bytes 393248 | tf_op jit(solution)/shard_map/ppermute | solution.py:57
  80.1 1.6 collective-permute-start.15
  85.5 0.9 copy-done.1
  86.9 0.9 copy-done.2
  89.3 16.3 %collective-permute-done.17 = bf16[768,1024]{1,0:T(8,128)(2,1)S(1)} collective-permute-done((bf16[768,1024]{1,0:T(8,128)(2,1)S(1)}, bf16[768,1024]{1,0:T(8,128)(2,1)S(1)}, u32[]{:S(2)}, u32[]{:S(2)}) %collective-permute-start.17) | collective-permute-done | bytes 1572896 | tf_op jit(solution)/shard_map/ppermute | solution.py:51
  108.3 0.7 collective-permute-done.18
  109.6 4.2 %collective-permute-done.15 = bf16[48,4096]{1,0:T(8,128)(2,1)S(1)} collective-permute-done((bf16[48,4096]{1,0:T(8,128)(2,1)S(1)}, bf16[48,4096]{1,0:T(8,128)(2,1)S(1)}, u32[]{:S(2)}, u32[]{:S(2)}) %collective-permute-start.15) | collective-permute-done | bytes 393248 | tf_op jit(solution)/shard_map/ppermute | solution.py:57
  113.8 0.7 fusion.20
  114.5 0.7 convolution_add_fusion.5
  115.2 0.7 fusion.16
  115.9 0.7 multiply_convert_fusion.1
  118.6 0.7 fusion
  120.0 0.7 fusion.3
  121.4 0.7 fusion.1
  123.4 3.5 %collective-permute-start.21 = (bf16[48,4096]{1,0:T(8,128)(2,1)S(1)}, bf16[48,4096]{1,0:T(8,128)(2,1)S(1)}, u32[]{:S(2)}, u32[]{:S(2)}) collective-permute-start(bf16[48,4096]{1,0:T(8,128)(2,1)S(1)} %get-tuple-element.83), channel_id=1, source_target_pairs={{0,20},{1,21},{2,22},{3,23},{4,28},{5,29},{6,30},{7,31},{8,16},{9,... | collective-permute-start | bytes 1179656 | tf_op jit(solution)/shard_map/ppermute | solution.py:69
  126.9 2.5 %collective-permute-start.22 = (bf16[48,4096]{1,0:T(8,128)(2,1)S(1)}, bf16[48,4096]{1,0:T(8,128)(2,1)S(1)}, u32[]{:S(2)}, u32[]{:S(2)}) collective-permute-start(bf16[48,4096]{1,0:T(8,128)(2,1)S(1)} %get-tuple-element.82), channel_id=1, source_target_pairs={{0,16},{1,17},{2,18},{3,19},{4,24},{5,25},{6,26},{7,27},{8,20},{9,... | collective-permute-start | bytes 1179656 | tf_op jit(solution)/shard_map/ppermute | solution.py:69
  130.0 28.9 %collective-permute-done.16.meta_ref = f32[2,128]{1,0:T(2,128)S(1)} collective-permute-done((f32[2,128]{1,0:T(2,128)S(1)}, f32[2,128]{1,0:T(2,128)S(1)}, u32[]{:S(2)}, u32[]{:S(2)}) %collective-permute-start.16) | collective-permute-done | bytes 1056 | tf_op jit(solution)/shard_map/ppermute | solution.py:69
  159.0 2.8 %shard_map.116 = (bf16[128,4096]{1,0:T(8,128)(2,1)}, bf16[128,4096]{1,0:T(8,128)(2,1)}) custom-call(s32[4]{0:T(128)S(1)} %pad_add_fusion.where_ref, f32[2,128]{1,0:T(2,128)S(1)} %collective-permute-done.16.meta_ref, bf16[48,4096]{1,0:T(8,128)(2,1)S(1)} %collective-permute-done.19.refs_0_, bf16[48,4096]{1,0:T(8,128)(2,1)S(1)} %collective-permute-done.20.refs_1_, ...), custom_call_target="tpu_custom_call" | custom-call | flops 201326592 | bytes 3670016 | tf_op jit(solution)/shard_map/pallas_call | solution.py:175
  (81 shorter events, 19.3 us)
Async XLA Ops:
  0.6 3.7 %collective-permute-start = (bf16[1024,768]{1,0:T(8,128)(2,1)}, bf16[1024,768]{1,0:T(8,128)(2,1)S(1)}, u32[]{:S(2)}, u32[]{:S(2)}) collective-permute-start(bf16[1024,768]{1,0:T(8,128)(2,1)} %bitcast.74), channel_id=1, source_target_pairs={{0,1},{1,0},{2,3},{3,2},{4,5},{5,4},{6,7},{7,6},{8,9},{9,8},{10,11... | collective-permute-start | bytes 4718600 | tf_op jit(solution)/shard_map/ppermute | solution.py:51
  0.7 8.1 %collective-permute-start.1 = (bf16[1024,768]{1,0:T(8,128)(2,1)}, bf16[1024,768]{1,0:T(8,128)(2,1)S(1)}, u32[]{:S(2)}, u32[]{:S(2)}) collective-permute-start(bf16[1024,768]{1,0:T(8,128)(2,1)} %bitcast.76), channel_id=1, source_target_pairs={{0,1},{1,0},{2,3},{3,2},{4,5},{5,4},{6,7},{7,6},{8,9},{9,8},{10,11... | collective-permute-start | bytes 4718600 | tf_op jit(solution)/shard_map/ppermute | solution.py:51
  1.2 7.7 %collective-permute-start.2 = (bf16[768,1024]{1,0:T(8,128)(2,1)}, bf16[768,1024]{1,0:T(8,128)(2,1)}, u32[]{:S(2)}, u32[]{:S(2)}) collective-permute-start(bf16[768,1024]{1,0:T(8,128)(2,1)} %bitcast.72), channel_id=1, source_target_pairs={{0,1},{1,0},{2,3},{3,2},{4,5},{5,4},{6,7},{7,6},{8,9},{9,8},{10,11... | collective-permute-start | bytes 4718600 | tf_op jit(solution)/shard_map/ppermute | solution.py:51
  1.3 37.5 %collective-permute-start.5 = (bf16[1024,768]{1,0:T(8,128)(2,1)}, bf16[1024,768]{1,0:T(8,128)(2,1)}, u32[]{:S(2)}, u32[]{:S(2)}) collective-permute-start(bf16[1024,768]{1,0:T(8,128)(2,1)} %bitcast.75), channel_id=1, source_target_pairs={{0,2},{1,3},{2,0},{3,1},{4,6},{5,7},{6,4},{7,5},{8,10},{9,11},{10,... | collective-permute-start | bytes 4718600 | tf_op jit(solution)/shard_map/ppermute | solution.py:51
  1.8 70.7 %collective-permute-start.7 = (bf16[1024,768]{1,0:T(8,128)(2,1)}, bf16[1024,768]{1,0:T(8,128)(2,1)}, u32[]{:S(2)}, u32[]{:S(2)}) collective-permute-start(bf16[1024,768]{1,0:T(8,128)(2,1)} %bitcast.77), channel_id=1, source_target_pairs={{0,2},{1,3},{2,0},{3,1},{4,6},{5,7},{6,4},{7,5},{8,10},{9,11},{10,... | collective-permute-start | bytes 4718600 | tf_op jit(solution)/shard_map/ppermute | solution.py:51
  7.7 31.1 %copy-start = (bf16[1,1,768,1024]{3,2,1,0:T(8,128)(2,1)S(1)}, bf16[1,1,768,1024]{3,2,1,0:T(8,128)(2,1)}, u32[]{:S(2)}) copy-start(bf16[1,1,768,1024]{3,2,1,0:T(8,128)(2,1)} %param.19) | copy-start | bytes 4718596
  8.9 30.4 %collective-permute-start.3 = (bf16[48,4096]{1,0:T(8,128)(2,1)S(1)}, bf16[48,4096]{1,0:T(8,128)(2,1)S(1)}, u32[]{:S(2)}, u32[]{:S(2)}) collective-permute-start(bf16[48,4096]{1,0:T(8,128)(2,1)S(1)} %get-tuple-element.46), channel_id=1, source_target_pairs={{0,8},{1,9},{2,10},{3,11},{4,0},{5,1},{6,2},{7,3},{8,12},{9,13},{1... | collective-permute-start | bytes 1179656 | tf_op jit(solution)/shard_map/ppermute | solution.py:57
  9.4 30.5 %collective-permute-start.10 = (bf16[48,4096]{1,0:T(8,128)(2,1)S(1)}, bf16[48,4096]{1,0:T(8,128)(2,1)S(1)}, u32[]{:S(2)}, u32[]{:S(2)}) collective-permute-start(bf16[48,4096]{1,0:T(8,128)(2,1)S(1)} %get-tuple-element.53), channel_id=1, source_target_pairs={{0,4},{1,5},{2,6},{3,7},{4,12},{5,13},{6,14},{7,15},{8,0},{9,1},{1... | collective-permute-start | bytes 1179656 | tf_op jit(solution)/shard_map/ppermute | solution.py:57
  11.9 42.9 %collective-permute-start.13 = (bf16[48,4096]{1,0:T(8,128)(2,1)S(1)}, bf16[48,4096]{1,0:T(8,128)(2,1)S(1)}, u32[]{:S(2)}, u32[]{:S(2)}) collective-permute-start(bf16[48,4096]{1,0:T(8,128)(2,1)S(1)} %get-tuple-element.58), channel_id=1, source_target_pairs={{0,12},{1,13},{2,14},{3,15},{4,8},{5,9},{6,10},{7,11},{8,4},{9,5},... | collective-permute-start | bytes 1179656 | tf_op jit(solution)/shard_map/ppermute | solution.py:57
  38.8 66.9 %collective-permute-start.17 = (bf16[768,1024]{1,0:T(8,128)(2,1)S(1)}, bf16[768,1024]{1,0:T(8,128)(2,1)S(1)}, u32[]{:S(2)}, u32[]{:S(2)}) collective-permute-start(bf16[768,1024]{1,0:T(8,128)(2,1)S(1)} %bitcast.73), channel_id=1, source_target_pairs={{0,2},{1,3},{2,0},{3,1},{4,6},{5,7},{6,4},{7,5},{8,10},{9,11},{10,... | collective-permute-start | bytes 4718600 | tf_op jit(solution)/shard_map/ppermute | solution.py:51
  39.4 33.1 %collective-permute-start.4 = (bf16[48,4096]{1,0:T(8,128)(2,1)S(1)}, bf16[48,4096]{1,0:T(8,128)(2,1)S(1)}, u32[]{:S(2)}, u32[]{:S(2)}) collective-permute-start(bf16[48,4096]{1,0:T(8,128)(2,1)S(1)} %get-tuple-element.47), channel_id=1, source_target_pairs={{0,8},{1,9},{2,10},{3,11},{4,0},{5,1},{6,2},{7,3},{8,12},{9,13},{1... | collective-permute-start | bytes 1179656 | tf_op jit(solution)/shard_map/ppermute | solution.py:57
  39.9 34.6 %collective-permute-start.11 = (bf16[48,4096]{1,0:T(8,128)(2,1)S(1)}, bf16[48,4096]{1,0:T(8,128)(2,1)S(1)}, u32[]{:S(2)}, u32[]{:S(2)}) collective-permute-start(bf16[48,4096]{1,0:T(8,128)(2,1)S(1)} %get-tuple-element.54), channel_id=1, source_target_pairs={{0,4},{1,5},{2,6},{3,7},{4,12},{5,13},{6,14},{7,15},{8,0},{9,1},{1... | collective-permute-start | bytes 1179656 | tf_op jit(solution)/shard_map/ppermute | solution.py:57
  54.8 25.3 %collective-permute-start.14 = (bf16[48,4096]{1,0:T(8,128)(2,1)S(1)}, bf16[48,4096]{1,0:T(8,128)(2,1)S(1)}, u32[]{:S(2)}, u32[]{:S(2)}) collective-permute-start(bf16[48,4096]{1,0:T(8,128)(2,1)S(1)} %get-tuple-element.59), channel_id=1, source_target_pairs={{0,12},{1,13},{2,14},{3,15},{4,8},{5,9},{6,10},{7,11},{8,4},{9,5},... | collective-permute-start | bytes 1179656 | tf_op jit(solution)/shard_map/ppermute | solution.py:57
  72.5 11.7 %collective-permute-start.8 = (bf16[1024,768]{1,0:T(8,128)(2,1)}, bf16[1024,768]{1,0:T(8,128)(2,1)S(1)}, u32[]{:S(2)}, u32[]{:S(2)}) collective-permute-start(bf16[1024,768]{1,0:T(8,128)(2,1)} %collective-permute-done.7.refs_0_), channel_id=1, source_target_pairs={{0,1},{1,0},{2,3},{3,2},{4,5},{5,4},{6,7},{7,6},{8,9},{9,8},{10,11... | collective-permute-start | bytes 4718600 | tf_op jit(solution)/shard_map/ppermute | solution.py:51
  73.9 10.3 %collective-permute-start.6 = (bf16[1024,768]{1,0:T(8,128)(2,1)}, bf16[1024,768]{1,0:T(8,128)(2,1)S(1)}, u32[]{:S(2)}, u32[]{:S(2)}) collective-permute-start(bf16[1024,768]{1,0:T(8,128)(2,1)} %collective-permute-done.5.refs_0_), channel_id=1, source_target_pairs={{0,1},{1,0},{2,3},{3,2},{4,5},{5,4},{6,7},{7,6},{8,9},{9,8},{10,11... | collective-permute-start | bytes 4718600 | tf_op jit(solution)/shard_map/ppermute | solution.py:51
  74.5 35.0 %collective-permute-start.12 = (bf16[48,4096]{1,0:T(8,128)(2,1)S(1)}, bf16[48,4096]{1,0:T(8,128)(2,1)S(1)}, u32[]{:S(2)}, u32[]{:S(2)}) collective-permute-start(bf16[48,4096]{1,0:T(8,128)(2,1)S(1)} %get-tuple-element.55), channel_id=1, source_target_pairs={{0,4},{1,5},{2,6},{3,7},{4,12},{5,13},{6,14},{7,15},{8,0},{9,1},{1... | collective-permute-start | bytes 1179656 | tf_op jit(solution)/shard_map/ppermute | solution.py:57
  80.1 33.7 %collective-permute-start.15 = (bf16[48,4096]{1,0:T(8,128)(2,1)S(1)}, bf16[48,4096]{1,0:T(8,128)(2,1)S(1)}, u32[]{:S(2)}, u32[]{:S(2)}) collective-permute-start(bf16[48,4096]{1,0:T(8,128)(2,1)S(1)} %get-tuple-element.60), channel_id=1, source_target_pairs={{0,12},{1,13},{2,14},{3,15},{4,8},{5,9},{6,10},{7,11},{8,4},{9,5},... | collective-permute-start | bytes 1179656 | tf_op jit(solution)/shard_map/ppermute | solution.py:57
  84.3 29.5 %collective-permute-start.9 = (bf16[48,4096]{1,0:T(8,128)(2,1)S(1)}, bf16[48,4096]{1,0:T(8,128)(2,1)S(1)}, u32[]{:S(2)}, u32[]{:S(2)}) collective-permute-start(bf16[48,4096]{1,0:T(8,128)(2,1)S(1)} %get-tuple-element.50), channel_id=1, source_target_pairs={{0,8},{1,9},{2,10},{3,11},{4,0},{5,1},{6,2},{7,3},{8,12},{9,13},{1... | collective-permute-start | bytes 1179656 | tf_op jit(solution)/shard_map/ppermute | solution.py:57
  85.0 1.4 copy-start.1
  86.4 1.4 copy-start.2
  105.7 3.4 %collective-permute-start.18 = (bf16[768,1024]{1,0:T(8,128)(2,1)S(1)}, bf16[768,1024]{1,0:T(8,128)(2,1)S(1)}, u32[]{:S(2)}, u32[]{:S(2)}) collective-permute-start(bf16[768,1024]{1,0:T(8,128)(2,1)S(1)} %collective-permute-done.17), channel_id=1, source_target_pairs={{0,1},{1,0},{2,3},{3,2},{4,5},{5,4},{6,7},{7,6},{8,9},{9,8},{10,11... | collective-permute-start | bytes 4718600 | tf_op jit(solution)/shard_map/ppermute | solution.py:51
  122.4 7.1 %copy-start.3 = (s32[1,128,1]{1,2,0:T(1,128)S(1)}, s32[1,128,1]{1,2,0:T(1,128)}, u32[]{:S(2)}) copy-start(s32[1,128,1]{1,2,0:T(1,128)} %param.15) | copy-start | bytes 1540
  122.4 7.1 %copy-start.4 = (s32[1,128,1]{1,2,0:T(1,128)S(1)}, s32[1,128,1]{1,2,0:T(1,128)}, u32[]{:S(2)}) copy-start(s32[1,128,1]{1,2,0:T(1,128)} %param.11) | copy-start | bytes 1540
  122.4 7.1 %copy-start.5 = (f32[1,128,1]{1,2,0:T(1,128)S(1)}, f32[1,128,1]{1,2,0:T(1,128)}, u32[]{:S(2)}) copy-start(f32[1,128,1]{1,2,0:T(1,128)} %param.12) | copy-start | bytes 1540
  122.5 36.4 %collective-permute-start.19 = (bf16[48,4096]{1,0:T(8,128)(2,1)S(1)}, bf16[48,4096]{1,0:T(8,128)(2,1)S(1)}, u32[]{:S(2)}, u32[]{:S(2)}) collective-permute-start(bf16[48,4096]{1,0:T(8,128)(2,1)S(1)} %get-tuple-element.85), channel_id=1, source_target_pairs={{0,28},{1,29},{2,30},{3,31},{4,20},{5,21},{6,22},{7,23},{8,24},{9,... | collective-permute-start | bytes 1179656 | tf_op jit(solution)/shard_map/ppermute | solution.py:69
  123.1 35.9 %collective-permute-start.20 = (bf16[48,4096]{1,0:T(8,128)(2,1)S(1)}, bf16[48,4096]{1,0:T(8,128)(2,1)S(1)}, u32[]{:S(2)}, u32[]{:S(2)}) collective-permute-start(bf16[48,4096]{1,0:T(8,128)(2,1)S(1)} %get-tuple-element.84), channel_id=1, source_target_pairs={{0,24},{1,25},{2,26},{3,27},{4,16},{5,17},{6,18},{7,19},{8,28},{9,... | collective-permute-start | bytes 1179656 | tf_op jit(solution)/shard_map/ppermute | solution.py:69
  123.4 35.6 %collective-permute-start.21 = (bf16[48,4096]{1,0:T(8,128)(2,1)S(1)}, bf16[48,4096]{1,0:T(8,128)(2,1)S(1)}, u32[]{:S(2)}, u32[]{:S(2)}) collective-permute-start(bf16[48,4096]{1,0:T(8,128)(2,1)S(1)} %get-tuple-element.83), channel_id=1, source_target_pairs={{0,20},{1,21},{2,22},{3,23},{4,28},{5,29},{6,30},{7,31},{8,16},{9,... | collective-permute-start | bytes 1179656 | tf_op jit(solution)/shard_map/ppermute | solution.py:69
  126.9 32.1 %collective-permute-start.22 = (bf16[48,4096]{1,0:T(8,128)(2,1)S(1)}, bf16[48,4096]{1,0:T(8,128)(2,1)S(1)}, u32[]{:S(2)}, u32[]{:S(2)}) collective-permute-start(bf16[48,4096]{1,0:T(8,128)(2,1)S(1)} %get-tuple-element.82), channel_id=1, source_target_pairs={{0,16},{1,17},{2,18},{3,19},{4,24},{5,25},{6,26},{7,27},{8,20},{9,... | collective-permute-start | bytes 1179656 | tf_op jit(solution)/shard_map/ppermute | solution.py:69
  129.5 29.5 %collective-permute-start.16 = (f32[2,128]{1,0:T(2,128)S(1)}, f32[2,128]{1,0:T(2,128)S(1)}, u32[]{:S(2)}, u32[]{:S(2)}) collective-permute-start(f32[2,128]{1,0:T(2,128)S(1)} %maximum_select_fusion), channel_id=1, source_target_pairs={{0,16},{1,17},{2,18},{3,19},{4,20},{5,21},{6,22},{7,23},{8,24},{9,... | collective-permute-start | bytes 3080 | tf_op jit(solution)/shard_map/ppermute | solution.py:69

commit v6 on v5

--- a/solution.py
+++ b/solution.py
@@ -129,7 +129,7 @@
 
 
 def collect_kernel(slot_cap, experts, where_ref, meta_ref, *refs):
-    block_refs, out_refs = refs[:experts], refs[experts:]
+    block_refs, out_refs, (held, stored) = refs[:experts], refs[experts:-2], refs[-2:]
     tokens = meta_ref.shape[1]
     quarter = out_refs[0].shape[1] // QUARTERS
     low = lax.broadcasted_iota(jnp.int32, (tokens, tokens), 1)
@@ -153,29 +153,40 @@
         ],
         axis=1,
     ).astype(jnp.bfloat16)
+    copies = []
     for j in range(QUARTERS):
         part = slice(j * quarter, (j + 1) * quarter)
         rows = jnp.concatenate([ref[:, part] for ref in block_refs])
         total = jnp.dot(chosen, rows, preferred_element_type=jnp.float32) * gate
-        start = pl.multiple_of((where_ref[1] ^ j) * quarter, quarter)
         if len(out_refs) == 1:
-            out_refs[0][:, pl.ds(start, quarter)] = total.astype(jnp.bfloat16)
+            results = [total]
         else:
             first = where_ref[2] == 0
-            fwd, bwd = jnp.where(first, 0.0, total), jnp.where(first, total, 0.0)
-            out_refs[0][:, pl.ds(start, quarter)] = fwd.astype(jnp.bfloat16)
-            out_refs[1][:, pl.ds(start, quarter)] = bwd.astype(jnp.bfloat16)
+            results = [jnp.where(first, 0.0, total), jnp.where(first, total, 0.0)]
+        start = pl.multiple_of((where_ref[1] ^ j) * quarter, quarter)
+        for at, result in enumerate(results):
+            held[at, j] = result.astype(jnp.bfloat16)
+            goal = out_refs[at].at[:, pl.ds(start, quarter)]
+            copies.append(pltpu.make_async_copy(held.at[at, j], goal, stored.at[at, j]))
+            copies[-1].start()
+    for copy in copies:
+        copy.wait()
 
 
 def collect(where, meta, blocks, outputs):
     tokens = meta.shape[1]
     experts = len(blocks)
     slot_cap, width = blocks[0].shape
+    quarter = width // QUARTERS
     vmem = pl.BlockSpec(memory_space=pltpu.VMEM)
     return pl.pallas_call(
         functools.partial(collect_kernel, slot_cap, experts),
         in_specs=[pl.BlockSpec(memory_space=pltpu.SMEM)] + [vmem] * (1 + experts),
-        out_specs=[vmem] * outputs,
+        out_specs=[pl.BlockSpec(memory_space=pl.ANY)] * outputs,
+        scratch_shapes=[
+            pltpu.VMEM((outputs, QUARTERS, tokens, quarter), jnp.bfloat16),
+            pltpu.SemaphoreType.DMA((outputs, QUARTERS)),
+        ],
         out_shape=[jax.ShapeDtypeStruct((tokens, width), jnp.bfloat16)] * outputs,
         cost_estimate=pl.CostEstimate(
             flops=2 * experts * slot_cap * tokens * width,
@@ -213,6 +224,28 @@
         ),
         compiler_params=pltpu.CompilerParams(vmem_limit_bytes=16 << 20),
     )(*[pltpu.with_memory_space_constraint(weight, pltpu.HBM) for weight in weights])
+
+
+def turn_kernel(*refs):
+    count = len(refs) // 2
+    for at in range(count):
+        refs[count + at][...] = refs[at][...].T
+
+
+def turned(mats):
+    vmem = pl.BlockSpec(memory_space=pltpu.VMEM)
+    return pl.pallas_call(
+        turn_kernel,
+        in_specs=[vmem] * len(mats),
+        out_specs=[vmem] * len(mats),
+        out_shape=[jax.ShapeDtypeStruct(mat.shape[::-1], mat.dtype) for mat in mats],
+        cost_estimate=pl.CostEstimate(
+            flops=0,
+            bytes_accessed=sum(2 * mat.size * mat.dtype.itemsize for mat in mats),
+            transcendentals=0,
+        ),
+        compiler_params=pltpu.CompilerParams(vmem_limit_bytes=16 << 20),
+    )(*mats)
 
 
 def rows_times(rows, mats):
@@ -281,16 +314,14 @@
     gate_diagonal = paired(gate_across, 1, bwd_blocks[last])
     up_diagonal = paired(up_across, 1, bwd_blocks[last])
     for d in order:
-        before = (gate_diagonal, up_diagonal) if d == last else (up_across,)
+        before = ()
         grad_blocks[d] = sent(grad_spread[d], distances[d], bwd_blocks[d], *before)
-    down_diagonal = paired(down_across, 1, up_diagonal)
     near = lax.optimization_barrier((gate_across, down_beside, fwd_blocks[last]))
     gate_across, down_beside = staged(near[:2])
     near = lax.optimization_barrier((up_across, bwd_blocks[last]))
     (up_across,) = staged(near[:1])
     gate_mats = [gate, gate_beside, gate_across, gate_diagonal]
     up_mats = [up, up_beside, up_across, up_diagonal]
-    down_mats = [down, down_beside, down_across, down_diagonal]
     fwd_blocks = [fwd_spread[0]] + [fwd_blocks[d] for d in range(1, experts)]
     bwd_blocks = [row_spread[0]] + [bwd_blocks[d] for d in range(1, experts)]
     grad_blocks = [grad_spread[0]] + [grad_blocks[d] for d in range(1, experts)]
@@ -298,6 +329,11 @@
     rows = jnp.concatenate(fwd_blocks)
     gate_value, up_value = rows_times(rows, gate_mats), rows_times(rows, up_mats)
     hidden = (jax.nn.silu(gate_value) * up_value).astype(jnp.bfloat16)
+    ready = lax.optimization_barrier((*gate_mats, *up_mats, hidden))[: 2 * QUARTERS]
+    turned_mats = turned(ready)
+    down_across = after(down_across, turned_mats[0])
+    down_diagonal = paired(down_across, 1)
+    down_mats = [down, down_beside, down_across, down_diagonal]
     fwd_parts = [
         jnp.dot(hidden, mat, preferred_element_type=jnp.float32).astype(jnp.bfloat16)
         for mat in down_mats
@@ -319,8 +355,11 @@
     grad_gate = (grad_hidden * landed[experts - 1]).astype(jnp.bfloat16)
     grad_up = (grad_hidden * landed[experts]).astype(jnp.bfloat16)
     bwd_parts = [
-        (contract_cols(grad_gate, g) + contract_cols(grad_up, u)).astype(jnp.bfloat16)
-        for g, u in zip(gate_mats, up_mats)
+        (
+            jnp.dot(grad_gate, g, preferred_element_type=jnp.float32)
+            + jnp.dot(grad_up, u, preferred_element_type=jnp.float32)
+        ).astype(jnp.bfloat16)
+        for g, u in zip(turned_mats[:QUARTERS], turned_mats[QUARTERS:])
     ]
     fwd_parts = landed[experts + 1 :]
     merged = lax.axis_size("pp") == 2

time: 162 us -> 162 us (level)
  waiting for transfers between devices: 106 us -> 102 us
  Pallas kernels: 9.51 us -> 12.9 us
    ppermute x9, waiting for transfers between devices: 57.1 us -> 31.8 us  [paired(): return lax.ppermute(block, 'ep', [(i, i ^ distance) for i in range(count)])]
    ppermute x9, waiting for transfers between devices: 19.6 us -> 41.2 us  [sent(): lax.ppermute(block, 'ep', [(i, target(i, distance)) for i in range(count)])]
    dot_general x12 -> x4, matrix products: 8.05 us -> 2.78 us  [contract_cols(): lax.dot_general(left, right, (((1,), (1,)), ((), ())), preferred_element_...]
    dot_general x0 -> x8, matrix products: none -> 4.06 us  [the longest x4 2.14 us: on_device(): jnp.dot(grad_gate, g, preferred_element_type=jnp.float32)]
    pallas_call x0 -> x1, Pallas kernels: none -> 3.57 us  [turned(): pl.pallas_call(turn_kernel, in_specs=[vmem] * len(mats), out_specs=[vmem]...]
  transfers between devices with their start and end apart: 23 -> 23, of which waited for: 11 -> 11; matrix products, arithmetic and copies ran while one was open for 6% -> 6% of each run, Pallas kernels for 4% -> 6%
where the time goes in v6:
time: 162 us; the launch traced here: 160 us
  waiting for transfers between devices  102 us (63%)
  starting transfers between devices  24.9 us (15%)
  matrix products  16.7 us (10%)
  Pallas kernels  12.9 us (8%)
  local copies, waits for them, and re-layouts  2.16 us (1%)
    ppermute x9, waiting for transfers between devices, sent(): lax.ppermute(block, 'ep', [(i, target(i, distance)) for i in range(count)])  41.2 us
    ppermute x9, waiting for transfers between devices, paired(): return lax.ppermute(block, 'ep', [(i, i ^ distance) for i in range(count)])  31.8 us
    ppermute x5, waiting for transfers between devices, handed(): return lax.ppermute(block, ('pp', 'ep'), route)  28.9 us
    ppermute x9, starting transfers between devices, sent(): lax.ppermute(block, 'ep', [(i, target(i, distance)) for i in range(count)])  14.1 us
    dot_general x16, matrix products, rows_times(): jnp.dot(rows[:, j * quarter:(j + 1) * quarter], mat, preferred_element_ty...  7.91 us
    ppermute x5, starting transfers between devices, handed(): return lax.ppermute(block, ('pp', 'ep'), route)  7.49 us
    pallas_call x1, Pallas kernels, turned(): pl.pallas_call(turn_kernel, in_specs=[vmem] * len(mats), out_specs=[vmem]...  3.57 us
    pallas_call x1, Pallas kernels, spread(): pl.pallas_call(functools.partial(spread_kernel, slot_cap, experts), in_sp...  3.42 us
  transfers between devices with their start and end apart: 23, of which 11 were waited for; matrix products, arithmetic and copies ran while one was open for 6% of the time, Pallas kernels for 6%

profile of v6, /device:TPU:14, one launch (start us, length us, event | category | flops | bytes accessed | tf_op | source)
XLA Modules:
  0.0 160.5 jit_solution(5184207299549214669)
XLA Ops:
  1.8 1.5 collective-permute-start.13
  3.4 0.9 collective-permute-done.refs_1_
  4.3 3.4 %shard_map.113 = (bf16[48,4096]{1,0:T(8,128)(2,1)S(1)}, bf16[48,4096]{1,0:T(8,128)(2,1)S(1)}, bf16[48,4096]{1,0:T(8,128)(2,1)S(1)}, bf16[48,4096]{1,0:T(8,128)(2...) custom-call(s32[4]{0:T(128)S(1)} %pad_add_fusion.where_ref, ...), custom_call_target="tpu_custom_call" | custom-call | flops 603979776 | bytes 7864320 | tf_op jit(solution)/shard_map/pallas_call | solution.py:116
  7.8 1.1 collective-permute-done.1.refs_5_
  9.4 2.5 %collective-permute-start.6 = (bf16[48,4096]{1,0:T(8,128)(2,1)S(1)}, bf16[48,4096]{1,0:T(8,128)(2,1)S(1)}, u32[]{:S(2)}, u32[]{:S(2)}) collective-permute-start(bf16[48,4096]{1,0:T(8,128)(2,1)S(1)} %get-tuple-element.67), channel_id=1, source_target_pairs={{0,4},{1,5},{2,6},{3,7},{4,12},{5,13},{6,14},{7,15},{8,0},{9,1},{1... | collective-permute-start | bytes 1179656 | tf_op jit(solution)/shard_map/ppermute | solution.py:57
  11.9 1.6 collective-permute-start.9
  13.5 25.3 %collective-permute-done.15.refs_0_ = bf16[1024,768]{1,0:T(8,128)(2,1)} collective-permute-done((bf16[1024,768]{1,0:T(8,128)(2,1)}, bf16[1024,768]{1,0:T(8,128)(2,1)}, u32[]{:S(2)}, u32[]{:S(2)}) %collective-permute-start.15) | collective-permute-done | bytes 1572896 | tf_op jit(solution)/shard_map/ppermute | solution.py:51
  39.9 2.5 %collective-permute-start.7 = (bf16[48,4096]{1,0:T(8,128)(2,1)S(1)}, bf16[48,4096]{1,0:T(8,128)(2,1)S(1)}, u32[]{:S(2)}, u32[]{:S(2)}) collective-permute-start(bf16[48,4096]{1,0:T(8,128)(2,1)S(1)} %get-tuple-element.68), channel_id=1, source_target_pairs={{0,4},{1,5},{2,6},{3,7},{4,12},{5,13},{6,14},{7,15},{8,0},{9,1},{1... | collective-permute-start | bytes 1179656 | tf_op jit(solution)/shard_map/ppermute | solution.py:57
  42.4 12.4 %collective-permute-done.9 = bf16[48,4096]{1,0:T(8,128)(2,1)S(1)} collective-permute-done((bf16[48,4096]{1,0:T(8,128)(2,1)S(1)}, bf16[48,4096]{1,0:T(8,128)(2,1)S(1)}, u32[]{:S(2)}, u32[]{:S(2)}) %collective-permute-start.9) | collective-permute-done | bytes 393248 | tf_op jit(solution)/shard_map/ppermute | solution.py:57
  54.8 1.6 collective-permute-start.10
  56.4 1.9 %shard_map.115 = (bf16[1024,768]{1,0:T(8,128)(2,1)S(1)}, bf16[768,1024]{1,0:T(8,128)(2,1)S(1)}) custom-call(bf16[1024,768]{1,0:T(8,128)(2,1)} %collective-permute-done.15.refs_0_, bf16[768,1024]{1,0:T(8,128)(2,1)} %collective-permute-done.2.refs_1_), custom_call_target="tpu_custom_call" | custom-call | bytes 6291456 | tf_op jit(solution)/shard_map/pallas_call | solution.py:214
  59.9 19.3 %collective-permute-done.7 = bf16[48,4096]{1,0:T(8,128)(2,1)S(1)} collective-permute-done((bf16[48,4096]{1,0:T(8,128)(2,1)S(1)}, bf16[48,4096]{1,0:T(8,128)(2,1)S(1)}, u32[]{:S(2)}, u32[]{:S(2)}) %collective-permute-start.7) | collective-permute-done | bytes 393248 | tf_op jit(solution)/shard_map/ppermute | solution.py:57
  79.2 3.4 %collective-permute-start.8 = (bf16[48,4096]{1,0:T(8,128)(2,1)S(1)}, bf16[48,4096]{1,0:T(8,128)(2,1)S(1)}, u32[]{:S(2)}, u32[]{:S(2)}) collective-permute-start(bf16[48,4096]{1,0:T(8,128)(2,1)S(1)} %get-tuple-element.69), channel_id=1, source_target_pairs={{0,4},{1,5},{2,6},{3,7},{4,12},{5,13},{6,14},{7,15},{8,0},{9,1},{1... | collective-permute-start | bytes 1179656 | tf_op jit(solution)/shard_map/ppermute | solution.py:57
  82.7 5.9 %collective-permute-done.10 = bf16[48,4096]{1,0:T(8,128)(2,1)S(1)} collective-permute-done((bf16[48,4096]{1,0:T(8,128)(2,1)S(1)}, bf16[48,4096]{1,0:T(8,128)(2,1)S(1)}, u32[]{:S(2)}, u32[]{:S(2)}) %collective-permute-start.10) | collective-permute-done | bytes 393248 | tf_op jit(solution)/shard_map/ppermute | solution.py:57
  89.1 1.4 shard_map.114.refs_6_
  92.4 1.6 %collective-permute-start.11 = (bf16[48,4096]{1,0:T(8,128)(2,1)S(1)}, bf16[48,4096]{1,0:T(8,128)(2,1)S(1)}, u32[]{:S(2)}, u32[]{:S(2)}) collective-permute-start(bf16[48,4096]{1,0:T(8,128)(2,1)S(1)} %get-tuple-element.74), channel_id=1, source_target_pairs={{0,12},{1,13},{2,14},{3,15},{4,8},{5,9},{6,10},{7,11},{8,4},{9,5},... | collective-permute-start | bytes 1179656 | tf_op jit(solution)/shard_map/ppermute | solution.py:57
  95.1 0.9 copy-done
  96.5 0.9 copy-done.1
  98.0 3.6 %shard_map.116 = (bf16[768,1024]{1,0:T(8,128)(2,1)S(1)}, bf16[768,1024]{1,0:T(8,128)(2,1)S(1)}, bf16[768,1024]{1,0:T(8,128)(2,1)S(1)}, bf16[768,1024]{1,0:T(8,12...) custom-call(bf16[1024,768]{1,0:T(8,128)(2,1)S(1)} %bitcast.72, ...), custom_call_target="tpu_custom_call" | custom-call | bytes 25165824 | tf_op jit(solution)/shard_map/pallas_call | solution.py:237
  102.0 3.6 %collective-permute-done.17 = bf16[768,1024]{1,0:T(8,128)(2,1)S(1)} collective-permute-done((bf16[768,1024]{1,0:T(8,128)(2,1)S(1)}, bf16[768,1024]{1,0:T(8,128)(2,1)S(1)}, u32[]{:S(2)}, u32[]{:S(2)}) %collective-permute-start.17) | collective-permute-done | bytes 1572896 | tf_op jit(solution)/shard_map/ppermute | solution.py:51
  108.8 0.8 collective-permute-done.18
  110.1 3.6 %collective-permute-done.11 = bf16[48,4096]{1,0:T(8,128)(2,1)S(1)} collective-permute-done((bf16[48,4096]{1,0:T(8,128)(2,1)S(1)}, bf16[48,4096]{1,0:T(8,128)(2,1)S(1)}, u32[]{:S(2)}, u32[]{:S(2)}) %collective-permute-start.11) | collective-permute-done | bytes 393248 | tf_op jit(solution)/shard_map/ppermute | solution.py:57
  113.8 0.7 fusion.20
  114.5 0.7 convolution_add_fusion.5
  115.2 0.7 fusion.16
  115.9 0.7 multiply_convert_fusion
  118.1 0.7 fusion.59
  121.8 0.9 collective-permute-start.20
  122.7 3.0 %collective-permute-start.21 = (bf16[48,4096]{1,0:T(8,128)(2,1)S(1)}, bf16[48,4096]{1,0:T(8,128)(2,1)S(1)}, u32[]{:S(2)}, u32[]{:S(2)}) collective-permute-start(bf16[48,4096]{1,0:T(8,128)(2,1)S(1)} %get-tuple-element.115), channel_id=1, source_target_pairs={{0,20},{1,21},{2,22},{3,23},{4,28},{5,29},{6,30},{7,31},{8,16},{9,... | collective-permute-start | bytes 1179656 | tf_op jit(solution)/shard_map/ppermute | solution.py:69
  125.7 2.5 %collective-permute-start.22 = (bf16[48,4096]{1,0:T(8,128)(2,1)S(1)}, bf16[48,4096]{1,0:T(8,128)(2,1)S(1)}, u32[]{:S(2)}, u32[]{:S(2)}) collective-permute-start(bf16[48,4096]{1,0:T(8,128)(2,1)S(1)} %get-tuple-element.114), channel_id=1, source_target_pairs={{0,16},{1,17},{2,18},{3,19},{4,24},{5,25},{6,26},{7,27},{8,20},{9,... | collective-permute-start | bytes 1179656 | tf_op jit(solution)/shard_map/ppermute | solution.py:69
  128.8 28.9 %collective-permute-done.12.meta_ref = f32[2,128]{1,0:T(2,128)S(1)} collective-permute-done((f32[2,128]{1,0:T(2,128)S(1)}, f32[2,128]{1,0:T(2,128)S(1)}, u32[]{:S(2)}, u32[]{:S(2)}) %collective-permute-start.12) | collective-permute-done | bytes 1056 | tf_op jit(solution)/shard_map/ppermute | solution.py:69
  157.7 2.6 %shard_map.117 = (bf16[128,4096]{1,0:T(8,128)(2,1)}, bf16[128,4096]{1,0:T(8,128)(2,1)}) custom-call(s32[4]{0:T(128)S(1)} %pad_add_fusion.where_ref, f32[2,128]{1,0:T(2,128)S(1)} %collective-permute-done.12.meta_ref, bf16[48,4096]{1,0:T(8,128)(2,1)S(1)} %collective-permute-done.19.refs_0_, bf16[48,4096]{1,0:T(8,128)(2,1)S(1)} %collective-permute-done.20.refs_1_, ...), custom_call_target="tpu_custom_call" | custom-call | flops 201326592 | bytes 3670016 | tf_op jit(solution)/shard_map/pallas_call | solution.py:182
  (82 shorter events, 18.2 us)
Async XLA Ops:
  0.6 3.7 %collective-permute-start = (bf16[1024,768]{1,0:T(8,128)(2,1)}, bf16[1024,768]{1,0:T(8,128)(2,1)S(1)}, u32[]{:S(2)}, u32[]{:S(2)}) collective-permute-start(bf16[1024,768]{1,0:T(8,128)(2,1)} %bitcast.70), channel_id=1, source_target_pairs={{0,1},{1,0},{2,3},{3,2},{4,5},{5,4},{6,7},{7,6},{8,9},{9,8},{10,11... | collective-permute-start | bytes 4718600 | tf_op jit(solution)/shard_map/ppermute | solution.py:51
  0.7 8.1 %collective-permute-start.1 = (bf16[1024,768]{1,0:T(8,128)(2,1)}, bf16[1024,768]{1,0:T(8,128)(2,1)S(1)}, u32[]{:S(2)}, u32[]{:S(2)}) collective-permute-start(bf16[1024,768]{1,0:T(8,128)(2,1)} %bitcast.73), channel_id=1, source_target_pairs={{0,1},{1,0},{2,3},{3,2},{4,5},{5,4},{6,7},{7,6},{8,9},{9,8},{10,11... | collective-permute-start | bytes 4718600 | tf_op jit(solution)/shard_map/ppermute | solution.py:51
  1.2 7.7 %collective-permute-start.2 = (bf16[768,1024]{1,0:T(8,128)(2,1)}, bf16[768,1024]{1,0:T(8,128)(2,1)}, u32[]{:S(2)}, u32[]{:S(2)}) collective-permute-start(bf16[768,1024]{1,0:T(8,128)(2,1)} %bitcast.76), channel_id=1, source_target_pairs={{0,1},{1,0},{2,3},{3,2},{4,5},{5,4},{6,7},{7,6},{8,9},{9,8},{10,11... | collective-permute-start | bytes 4718600 | tf_op jit(solution)/shard_map/ppermute | solution.py:51
  1.3 37.5 %collective-permute-start.15 = (bf16[1024,768]{1,0:T(8,128)(2,1)}, bf16[1024,768]{1,0:T(8,128)(2,1)}, u32[]{:S(2)}, u32[]{:S(2)}) collective-permute-start(bf16[1024,768]{1,0:T(8,128)(2,1)} %bitcast.71), channel_id=1, source_target_pairs={{0,2},{1,3},{2,0},{3,1},{4,6},{5,7},{6,4},{7,5},{8,10},{9,11},{10,... | collective-permute-start | bytes 4718600 | tf_op jit(solution)/shard_map/ppermute | solution.py:51
  1.8 80.8 %collective-permute-start.13 = (bf16[1024,768]{1,0:T(8,128)(2,1)}, bf16[1024,768]{1,0:T(8,128)(2,1)}, u32[]{:S(2)}, u32[]{:S(2)}) collective-permute-start(bf16[1024,768]{1,0:T(8,128)(2,1)} %bitcast.74), channel_id=1, source_target_pairs={{0,2},{1,3},{2,0},{3,1},{4,6},{5,7},{6,4},{7,5},{8,10},{9,11},{10,... | collective-permute-start | bytes 4718600 | tf_op jit(solution)/shard_map/ppermute | solution.py:51
  7.7 31.1 %copy-start.2 = (bf16[1,1,768,1024]{3,2,1,0:T(8,128)(2,1)S(1)}, bf16[1,1,768,1024]{3,2,1,0:T(8,128)(2,1)}, u32[]{:S(2)}) copy-start(bf16[1,1,768,1024]{3,2,1,0:T(8,128)(2,1)} %param.19) | copy-start | bytes 4718596
  8.9 30.4 %collective-permute-start.3 = (bf16[48,4096]{1,0:T(8,128)(2,1)S(1)}, bf16[48,4096]{1,0:T(8,128)(2,1)S(1)}, u32[]{:S(2)}, u32[]{:S(2)}) collective-permute-start(bf16[48,4096]{1,0:T(8,128)(2,1)S(1)} %get-tuple-element.62), channel_id=1, source_target_pairs={{0,8},{1,9},{2,10},{3,11},{4,0},{5,1},{6,2},{7,3},{8,12},{9,13},{1... | collective-permute-start | bytes 1179656 | tf_op jit(solution)/shard_map/ppermute | solution.py:57
  9.4 30.5 %collective-permute-start.6 = (bf16[48,4096]{1,0:T(8,128)(2,1)S(1)}, bf16[48,4096]{1,0:T(8,128)(2,1)S(1)}, u32[]{:S(2)}, u32[]{:S(2)}) collective-permute-start(bf16[48,4096]{1,0:T(8,128)(2,1)S(1)} %get-tuple-element.67), channel_id=1, source_target_pairs={{0,4},{1,5},{2,6},{3,7},{4,12},{5,13},{6,14},{7,15},{8,0},{9,1},{1... | collective-permute-start | bytes 1179656 | tf_op jit(solution)/shard_map/ppermute | solution.py:57
  11.9 42.9 %collective-permute-start.9 = (bf16[48,4096]{1,0:T(8,128)(2,1)S(1)}, bf16[48,4096]{1,0:T(8,128)(2,1)S(1)}, u32[]{:S(2)}, u32[]{:S(2)}) collective-permute-start(bf16[48,4096]{1,0:T(8,128)(2,1)S(1)} %get-tuple-element.72), channel_id=1, source_target_pairs={{0,12},{1,13},{2,14},{3,15},{4,8},{5,9},{6,10},{7,11},{8,4},{9,5},... | collective-permute-start | bytes 1179656 | tf_op jit(solution)/shard_map/ppermute | solution.py:57
  38.8 66.9 %collective-permute-start.17 = (bf16[768,1024]{1,0:T(8,128)(2,1)S(1)}, bf16[768,1024]{1,0:T(8,128)(2,1)S(1)}, u32[]{:S(2)}, u32[]{:S(2)}) collective-permute-start(bf16[768,1024]{1,0:T(8,128)(2,1)S(1)} %bitcast.77), channel_id=1, source_target_pairs={{0,2},{1,3},{2,0},{3,1},{4,6},{5,7},{6,4},{7,5},{8,10},{9,11},{10,... | collective-permute-start | bytes 4718600 | tf_op jit(solution)/shard_map/ppermute | solution.py:51
  39.4 20.5 %collective-permute-start.4 = (bf16[48,4096]{1,0:T(8,128)(2,1)S(1)}, bf16[48,4096]{1,0:T(8,128)(2,1)S(1)}, u32[]{:S(2)}, u32[]{:S(2)}) collective-permute-start(bf16[48,4096]{1,0:T(8,128)(2,1)S(1)} %get-tuple-element.63), channel_id=1, source_target_pairs={{0,8},{1,9},{2,10},{3,11},{4,0},{5,1},{6,2},{7,3},{8,12},{9,13},{1... | collective-permute-start | bytes 1179656 | tf_op jit(solution)/shard_map/ppermute | solution.py:57
  39.9 39.3 %collective-permute-start.7 = (bf16[48,4096]{1,0:T(8,128)(2,1)S(1)}, bf16[48,4096]{1,0:T(8,128)(2,1)S(1)}, u32[]{:S(2)}, u32[]{:S(2)}) collective-permute-start(bf16[48,4096]{1,0:T(8,128)(2,1)S(1)} %get-tuple-element.68), channel_id=1, source_target_pairs={{0,4},{1,5},{2,6},{3,7},{4,12},{5,13},{6,14},{7,15},{8,0},{9,1},{1... | collective-permute-start | bytes 1179656 | tf_op jit(solution)/shard_map/ppermute | solution.py:57
  54.8 33.7 %collective-permute-start.10 = (bf16[48,4096]{1,0:T(8,128)(2,1)S(1)}, bf16[48,4096]{1,0:T(8,128)(2,1)S(1)}, u32[]{:S(2)}, u32[]{:S(2)}) collective-permute-start(bf16[48,4096]{1,0:T(8,128)(2,1)S(1)} %get-tuple-element.73), channel_id=1, source_target_pairs={{0,12},{1,13},{2,14},{3,15},{4,8},{5,9},{6,10},{7,11},{8,4},{9,5},... | collective-permute-start | bytes 1179656 | tf_op jit(solution)/shard_map/ppermute | solution.py:57
  59.8 50.3 %collective-permute-start.5 = (bf16[48,4096]{1,0:T(8,128)(2,1)S(1)}, bf16[48,4096]{1,0:T(8,128)(2,1)S(1)}, u32[]{:S(2)}, u32[]{:S(2)}) collective-permute-start(bf16[48,4096]{1,0:T(8,128)(2,1)S(1)} %get-tuple-element.64), channel_id=1, source_target_pairs={{0,8},{1,9},{2,10},{3,11},{4,0},{5,1},{6,2},{7,3},{8,12},{9,13},{1... | collective-permute-start | bytes 1179656 | tf_op jit(solution)/shard_map/ppermute | solution.py:57
  79.2 30.9 %collective-permute-start.8 = (bf16[48,4096]{1,0:T(8,128)(2,1)S(1)}, bf16[48,4096]{1,0:T(8,128)(2,1)S(1)}, u32[]{:S(2)}, u32[]{:S(2)}) collective-permute-start(bf16[48,4096]{1,0:T(8,128)(2,1)S(1)} %get-tuple-element.69), channel_id=1, source_target_pairs={{0,4},{1,5},{2,6},{3,7},{4,12},{5,13},{6,14},{7,15},{8,0},{9,1},{1... | collective-permute-start | bytes 1179656 | tf_op jit(solution)/shard_map/ppermute | solution.py:57
  82.6 12.0 %collective-permute-start.14 = (bf16[1024,768]{1,0:T(8,128)(2,1)}, bf16[1024,768]{1,0:T(8,128)(2,1)S(1)}, u32[]{:S(2)}, u32[]{:S(2)}) collective-permute-start(bf16[1024,768]{1,0:T(8,128)(2,1)} %collective-permute-done.13.refs_0_), channel_id=1, source_target_pairs={{0,1},{1,0},{2,3},{3,2},{4,5},{5,4},{6,7},{7,6},{8,9},{9,8},{10,11... | collective-permute-start | bytes 4718600 | tf_op jit(solution)/shard_map/ppermute | solution.py:51
  88.5 3.9 %collective-permute-start.16 = (bf16[1024,768]{1,0:T(8,128)(2,1)}, bf16[1024,768]{1,0:T(8,128)(2,1)S(1)}, u32[]{:S(2)}, u32[]{:S(2)}) collective-permute-start(bf16[1024,768]{1,0:T(8,128)(2,1)} %collective-permute-done.15.refs_0_), channel_id=1, source_target_pairs={{0,1},{1,0},{2,3},{3,2},{4,5},{5,4},{6,7},{7,6},{8,9},{9,8},{10,11... | collective-permute-start | bytes 4718600 | tf_op jit(solution)/shard_map/ppermute | solution.py:51
  92.4 21.3 %collective-permute-start.11 = (bf16[48,4096]{1,0:T(8,128)(2,1)S(1)}, bf16[48,4096]{1,0:T(8,128)(2,1)S(1)}, u32[]{:S(2)}, u32[]{:S(2)}) collective-permute-start(bf16[48,4096]{1,0:T(8,128)(2,1)S(1)} %get-tuple-element.74), channel_id=1, source_target_pairs={{0,12},{1,13},{2,14},{3,15},{4,8},{5,9},{6,10},{7,11},{8,4},{9,5},... | collective-permute-start | bytes 1179656 | tf_op jit(solution)/shard_map/ppermute | solution.py:57
  94.5 1.4 copy-start
  96.0 1.4 copy-start.1
  106.1 3.5 %collective-permute-start.18 = (bf16[768,1024]{1,0:T(8,128)(2,1)S(1)}, bf16[768,1024]{1,0:T(8,128)(2,1)S(1)}, u32[]{:S(2)}, u32[]{:S(2)}) collective-permute-start(bf16[768,1024]{1,0:T(8,128)(2,1)S(1)} %collective-permute-done.17), channel_id=1, source_target_pairs={{0,1},{1,0},{2,3},{3,2},{4,5},{5,4},{6,7},{7,6},{8,9},{9,8},{10,11... | collective-permute-start | bytes 4718600 | tf_op jit(solution)/shard_map/ppermute | solution.py:51
  121.1 7.1 %copy-start.3 = (s32[1,128,1]{1,2,0:T(1,128)S(1)}, s32[1,128,1]{1,2,0:T(1,128)}, u32[]{:S(2)}) copy-start(s32[1,128,1]{1,2,0:T(1,128)} %param.15) | copy-start | bytes 1540
  121.1 7.1 %copy-start.4 = (s32[1,128,1]{1,2,0:T(1,128)S(1)}, s32[1,128,1]{1,2,0:T(1,128)}, u32[]{:S(2)}) copy-start(s32[1,128,1]{1,2,0:T(1,128)} %param.11) | copy-start | bytes 1540
  121.1 7.1 %copy-start.5 = (f32[1,128,1]{1,2,0:T(1,128)S(1)}, f32[1,128,1]{1,2,0:T(1,128)}, u32[]{:S(2)}) copy-start(f32[1,128,1]{1,2,0:T(1,128)} %param.12) | copy-start | bytes 1540
  121.3 36.4 %collective-permute-start.19 = (bf16[48,4096]{1,0:T(8,128)(2,1)S(1)}, bf16[48,4096]{1,0:T(8,128)(2,1)S(1)}, u32[]{:S(2)}, u32[]{:S(2)}) collective-permute-start(bf16[48,4096]{1,0:T(8,128)(2,1)S(1)} %get-tuple-element.117), channel_id=1, source_target_pairs={{0,28},{1,29},{2,30},{3,31},{4,20},{5,21},{6,22},{7,23},{8,24},{9,... | collective-permute-start | bytes 1179656 | tf_op jit(solution)/shard_map/ppermute | solution.py:69
  121.8 35.9 %collective-permute-start.20 = (bf16[48,4096]{1,0:T(8,128)(2,1)S(1)}, bf16[48,4096]{1,0:T(8,128)(2,1)S(1)}, u32[]{:S(2)}, u32[]{:S(2)}) collective-permute-start(bf16[48,4096]{1,0:T(8,128)(2,1)S(1)} %get-tuple-element.116), channel_id=1, source_target_pairs={{0,24},{1,25},{2,26},{3,27},{4,16},{5,17},{6,18},{7,19},{8,28},{9,... | collective-permute-start | bytes 1179656 | tf_op jit(solution)/shard_map/ppermute | solution.py:69
  122.7 35.0 %collective-permute-start.21 = (bf16[48,4096]{1,0:T(8,128)(2,1)S(1)}, bf16[48,4096]{1,0:T(8,128)(2,1)S(1)}, u32[]{:S(2)}, u32[]{:S(2)}) collective-permute-start(bf16[48,4096]{1,0:T(8,128)(2,1)S(1)} %get-tuple-element.115), channel_id=1, source_target_pairs={{0,20},{1,21},{2,22},{3,23},{4,28},{5,29},{6,30},{7,31},{8,16},{9,... | collective-permute-start | bytes 1179656 | tf_op jit(solution)/shard_map/ppermute | solution.py:69
  125.7 32.1 %collective-permute-start.22 = (bf16[48,4096]{1,0:T(8,128)(2,1)S(1)}, bf16[48,4096]{1,0:T(8,128)(2,1)S(1)}, u32[]{:S(2)}, u32[]{:S(2)}) collective-permute-start(bf16[48,4096]{1,0:T(8,128)(2,1)S(1)} %get-tuple-element.114), channel_id=1, source_target_pairs={{0,16},{1,17},{2,18},{3,19},{4,24},{5,25},{6,26},{7,27},{8,20},{9,... | collective-permute-start | bytes 1179656 | tf_op jit(solution)/shard_map/ppermute | solution.py:69
  128.2 29.5 %collective-permute-start.12 = (f32[2,128]{1,0:T(2,128)S(1)}, f32[2,128]{1,0:T(2,128)S(1)}, u32[]{:S(2)}, u32[]{:S(2)}) collective-permute-start(f32[2,128]{1,0:T(2,128)S(1)} %maximum_select_fusion), channel_id=1, source_target_pairs={{0,16},{1,17},{2,18},{3,19},{4,20},{5,21},{6,22},{7,23},{8,24},{9,... | collective-permute-start | bytes 3080 | tf_op jit(solution)/shard_map/ppermute | solution.py:69

commit v7 on v6

--- a/solution.py
+++ b/solution.py
@@ -329,8 +329,8 @@
     rows = jnp.concatenate(fwd_blocks)
     gate_value, up_value = rows_times(rows, gate_mats), rows_times(rows, up_mats)
     hidden = (jax.nn.silu(gate_value) * up_value).astype(jnp.bfloat16)
-    ready = lax.optimization_barrier((*gate_mats, *up_mats, hidden))[: 2 * QUARTERS]
-    turned_mats = turned(ready)
+    ready = lax.optimization_barrier((*gate_mats, *up_mats, down, down_beside, hidden))[:-1]
+    *turned_mats, down_turned, beside_turned = turned(ready)
     down_across = after(down_across, turned_mats[0])
     down_diagonal = paired(down_across, 1)
     down_mats = [down, down_beside, down_across, down_diagonal]
@@ -349,8 +349,10 @@
     grads = jnp.concatenate([grad_blocks[0], *landed[: experts - 1]])
     quarter = down.shape[1]
     grad_hidden = sum(
-        contract_cols(grads[:, j * quarter : (j + 1) * quarter], mat)
-        for j, mat in enumerate(down_mats)
+        jnp.dot(grads[:, j * quarter : (j + 1) * quarter], mat, preferred_element_type=jnp.float32)
+        if j < 2
+        else contract_cols(grads[:, j * quarter : (j + 1) * quarter], mat)
+        for j, mat in enumerate([down_turned, beside_turned, *down_mats[2:]])
     )
     grad_gate = (grad_hidden * landed[experts - 1]).astype(jnp.bfloat16)
     grad_up = (grad_hidden * landed[experts]).astype(jnp.bfloat16)

time: 162 us -> 161 us (level)
    ppermute x9, waiting for transfers between devices: 41.2 us -> 28.1 us  [sent(): lax.ppermute(block, 'ep', [(i, target(i, distance)) for i in range(count)])]
    ppermute x9, waiting for transfers between devices: 31.8 us -> 44.8 us  [paired(): return lax.ppermute(block, 'ep', [(i, i ^ distance) for i in range(count)])]
  transfers between devices with their start and end apart: 23 -> 23, of which waited for: 11 -> 12; matrix products, arithmetic and copies ran while one was open for 6% -> 6% of each run, Pallas kernels for 6% -> 7%
where the time goes in v7:
time: 161 us; the launch traced here: 160 us
  waiting for transfers between devices  102 us (63%)
  starting transfers between devices  24.3 us (15%)
  matrix products  16.2 us (10%)
  Pallas kernels  13.7 us (9%)
  local copies, waits for them, and re-layouts  2.18 us (1%)
    ppermute x9, waiting for transfers between devices, paired(): return lax.ppermute(block, 'ep', [(i, i ^ distance) for i in range(count)])  44.8 us
    ppermute x5, waiting for transfers between devices, handed(): return lax.ppermute(block, ('pp', 'ep'), route)  28.9 us
    ppermute x9, waiting for transfers between devices, sent(): lax.ppermute(block, 'ep', [(i, target(i, distance)) for i in range(count)])  28.1 us
    ppermute x9, starting transfers between devices, sent(): lax.ppermute(block, 'ep', [(i, target(i, distance)) for i in range(count)])  13.6 us
    dot_general x16, matrix products, rows_times(): jnp.dot(rows[:, j * quarter:(j + 1) * quarter], mat, preferred_element_ty...  7.79 us
    ppermute x5, starting transfers between devices, handed(): return lax.ppermute(block, ('pp', 'ep'), route)  7.5 us
    pallas_call x1, Pallas kernels, turned(): pl.pallas_call(turn_kernel, in_specs=[vmem] * len(mats), out_specs=[vmem]...  4.39 us
    pallas_call x1, Pallas kernels, spread(): pl.pallas_call(functools.partial(spread_kernel, slot_cap, experts), in_sp...  3.42 us
  transfers between devices with their start and end apart: 23, of which 12 were waited for; matrix products, arithmetic and copies ran while one was open for 6% of the time, Pallas kernels for 7%

profile of v7, /device:TPU:14, one launch (start us, length us, event | category | flops | bytes accessed | tf_op | source)
XLA Modules:
  0.0 160.2 jit_solution(629138100102467433)
XLA Ops:
  1.8 1.5 collective-permute-start.13
  3.4 0.9 collective-permute-done.refs_1_
  4.3 3.4 %shard_map.113 = (bf16[48,4096]{1,0:T(8,128)(2,1)S(1)}, bf16[48,4096]{1,0:T(8,128)(2,1)S(1)}, bf16[48,4096]{1,0:T(8,128)(2,1)S(1)}, bf16[48,4096]{1,0:T(8,128)(2...) custom-call(s32[4]{0:T(128)S(1)} %pad_add_fusion.where_ref, ...), custom_call_target="tpu_custom_call" | custom-call | flops 603979776 | bytes 7864320 | tf_op jit(solution)/shard_map/pallas_call | solution.py:116
  7.8 1.1 collective-permute-done.1.refs_5_
  9.4 2.5 %collective-permute-start.6 = (bf16[48,4096]{1,0:T(8,128)(2,1)S(1)}, bf16[48,4096]{1,0:T(8,128)(2,1)S(1)}, u32[]{:S(2)}, u32[]{:S(2)}) collective-permute-start(bf16[48,4096]{1,0:T(8,128)(2,1)S(1)} %get-tuple-element.71), channel_id=1, source_target_pairs={{0,4},{1,5},{2,6},{3,7},{4,12},{5,13},{6,14},{7,15},{8,0},{9,1},{1... | collective-permute-start | bytes 1179656 | tf_op jit(solution)/shard_map/ppermute | solution.py:57
  11.9 1.6 collective-permute-start.9
  13.5 25.3 %collective-permute-done.15.refs_0_ = bf16[1024,768]{1,0:T(8,128)(2,1)} collective-permute-done((bf16[1024,768]{1,0:T(8,128)(2,1)}, bf16[1024,768]{1,0:T(8,128)(2,1)}, u32[]{:S(2)}, u32[]{:S(2)}) %collective-permute-start.15) | collective-permute-done | bytes 1572896 | tf_op jit(solution)/shard_map/ppermute | solution.py:51
  39.9 2.5 %collective-permute-start.7 = (bf16[48,4096]{1,0:T(8,128)(2,1)S(1)}, bf16[48,4096]{1,0:T(8,128)(2,1)S(1)}, u32[]{:S(2)}, u32[]{:S(2)}) collective-permute-start(bf16[48,4096]{1,0:T(8,128)(2,1)S(1)} %get-tuple-element.72), channel_id=1, source_target_pairs={{0,4},{1,5},{2,6},{3,7},{4,12},{5,13},{6,14},{7,15},{8,0},{9,1},{1... | collective-permute-start | bytes 1179656 | tf_op jit(solution)/shard_map/ppermute | solution.py:57
  42.4 12.4 %collective-permute-done.9 = bf16[48,4096]{1,0:T(8,128)(2,1)S(1)} collective-permute-done((bf16[48,4096]{1,0:T(8,128)(2,1)S(1)}, bf16[48,4096]{1,0:T(8,128)(2,1)S(1)}, u32[]{:S(2)}, u32[]{:S(2)}) %collective-permute-start.9) | collective-permute-done | bytes 393248 | tf_op jit(solution)/shard_map/ppermute | solution.py:57
  54.8 1.6 collective-permute-start.10
  56.4 1.9 %shard_map.115 = (bf16[1024,768]{1,0:T(8,128)(2,1)S(1)}, bf16[768,1024]{1,0:T(8,128)(2,1)S(1)}) custom-call(bf16[1024,768]{1,0:T(8,128)(2,1)} %collective-permute-done.15.refs_0_, bf16[768,1024]{1,0:T(8,128)(2,1)} %collective-permute-done.2.refs_1_), custom_call_target="tpu_custom_call" | custom-call | bytes 6291456 | tf_op jit(solution)/shard_map/pallas_call | solution.py:214
  59.8 12.7 %collective-permute-done.13.refs_0_ = bf16[1024,768]{1,0:T(8,128)(2,1)} collective-permute-done((bf16[1024,768]{1,0:T(8,128)(2,1)}, bf16[1024,768]{1,0:T(8,128)(2,1)}, u32[]{:S(2)}, u32[]{:S(2)}) %collective-permute-start.13) | collective-permute-done | bytes 1572896 | tf_op jit(solution)/shard_map/ppermute | solution.py:51
  72.5 1.4 shard_map.114.refs_6_
  74.4 2.5 %collective-permute-start.8 = (bf16[48,4096]{1,0:T(8,128)(2,1)S(1)}, bf16[48,4096]{1,0:T(8,128)(2,1)S(1)}, u32[]{:S(2)}, u32[]{:S(2)}) collective-permute-start(bf16[48,4096]{1,0:T(8,128)(2,1)S(1)} %get-tuple-element.73), channel_id=1, source_target_pairs={{0,4},{1,5},{2,6},{3,7},{4,12},{5,13},{6,14},{7,15},{8,0},{9,1},{1... | collective-permute-start | bytes 1179656 | tf_op jit(solution)/shard_map/ppermute | solution.py:57
  77.0 11.5 %collective-permute-done.10 = bf16[48,4096]{1,0:T(8,128)(2,1)S(1)} collective-permute-done((bf16[48,4096]{1,0:T(8,128)(2,1)S(1)}, bf16[48,4096]{1,0:T(8,128)(2,1)S(1)}, u32[]{:S(2)}, u32[]{:S(2)}) %collective-permute-start.10) | collective-permute-done | bytes 393248 | tf_op jit(solution)/shard_map/ppermute | solution.py:57
  90.9 1.2 collective-permute-done.16.refs_3_
  92.1 1.6 collective-permute-start.11
  94.7 0.9 copy-done.1
  96.1 0.9 copy-done.2
  97.5 4.4 %shard_map.116 = (bf16[768,1024]{1,0:T(8,128)(2,1)S(1)}, bf16[768,1024]{1,0:T(8,128)(2,1)S(1)}, bf16[768,1024]{1,0:T(8,128)(2,1)S(1)}, bf16[768,1024]{1,0:T(8,12...) custom-call(bf16[1024,768]{1,0:T(8,128)(2,1)S(1)} %bitcast.74, ...), custom_call_target="tpu_custom_call" | custom-call | bytes 31457280 | tf_op jit(solution)/shard_map/pallas_call | solution.py:237
  102.9 2.7 %collective-permute-done.17 = bf16[768,1024]{1,0:T(8,128)(2,1)S(1)} collective-permute-done((bf16[768,1024]{1,0:T(8,128)(2,1)S(1)}, bf16[768,1024]{1,0:T(8,128)(2,1)S(1)}, u32[]{:S(2)}, u32[]{:S(2)}) %collective-permute-start.17) | collective-permute-done | bytes 1572896 | tf_op jit(solution)/shard_map/ppermute | solution.py:51
  108.2 0.8 collective-permute-done.18
  109.6 4.1 %collective-permute-done.11 = bf16[48,4096]{1,0:T(8,128)(2,1)S(1)} collective-permute-done((bf16[48,4096]{1,0:T(8,128)(2,1)S(1)}, bf16[48,4096]{1,0:T(8,128)(2,1)S(1)}, u32[]{:S(2)}, u32[]{:S(2)}) %collective-permute-start.11) | collective-permute-done | bytes 393248 | tf_op jit(solution)/shard_map/ppermute | solution.py:57
  114.8 0.7 fusion.16
  115.4 0.7 multiply_convert_fusion
  117.1 0.7 fusion.59
  120.9 0.6 collective-permute-start.19
  121.9 3.5 %collective-permute-start.21 = (bf16[48,4096]{1,0:T(8,128)(2,1)S(1)}, bf16[48,4096]{1,0:T(8,128)(2,1)S(1)}, u32[]{:S(2)}, u32[]{:S(2)}) collective-permute-start(bf16[48,4096]{1,0:T(8,128)(2,1)S(1)} %get-tuple-element.123), channel_id=1, source_target_pairs={{0,20},{1,21},{2,22},{3,23},{4,28},{5,29},{6,30},{7,31},{8,16},{9,... | collective-permute-start | bytes 1179656 | tf_op jit(solution)/shard_map/ppermute | solution.py:69
  125.3 2.5 %collective-permute-start.22 = (bf16[48,4096]{1,0:T(8,128)(2,1)S(1)}, bf16[48,4096]{1,0:T(8,128)(2,1)S(1)}, u32[]{:S(2)}, u32[]{:S(2)}) collective-permute-start(bf16[48,4096]{1,0:T(8,128)(2,1)S(1)} %get-tuple-element.122), channel_id=1, source_target_pairs={{0,16},{1,17},{2,18},{3,19},{4,24},{5,25},{6,26},{7,27},{8,20},{9,... | collective-permute-start | bytes 1179656 | tf_op jit(solution)/shard_map/ppermute | solution.py:69
  127.9 0.6 collective-permute-start.12
  128.5 28.9 %collective-permute-done.12.meta_ref = f32[2,128]{1,0:T(2,128)S(1)} collective-permute-done((f32[2,128]{1,0:T(2,128)S(1)}, f32[2,128]{1,0:T(2,128)S(1)}, u32[]{:S(2)}, u32[]{:S(2)}) %collective-permute-start.12) | collective-permute-done | bytes 1056 | tf_op jit(solution)/shard_map/ppermute | solution.py:69
  157.4 2.6 %shard_map.117 = (bf16[128,4096]{1,0:T(8,128)(2,1)}, bf16[128,4096]{1,0:T(8,128)(2,1)}) custom-call(s32[4]{0:T(128)S(1)} %pad_add_fusion.where_ref, f32[2,128]{1,0:T(2,128)S(1)} %collective-permute-done.12.meta_ref, bf16[48,4096]{1,0:T(8,128)(2,1)S(1)} %collective-permute-done.19.refs_0_, bf16[48,4096]{1,0:T(8,128)(2,1)S(1)} %collective-permute-done.20.refs_1_, ...), custom_call_target="tpu_custom_call" | custom-call | flops 201326592 | bytes 3670016 | tf_op jit(solution)/shard_map/pallas_call | solution.py:182
  (82 shorter events, 18.8 us)
Async XLA Ops:
  0.6 3.7 %collective-permute-start = (bf16[1024,768]{1,0:T(8,128)(2,1)}, bf16[1024,768]{1,0:T(8,128)(2,1)S(1)}, u32[]{:S(2)}, u32[]{:S(2)}) collective-permute-start(bf16[1024,768]{1,0:T(8,128)(2,1)} %bitcast.72), channel_id=1, source_target_pairs={{0,1},{1,0},{2,3},{3,2},{4,5},{5,4},{6,7},{7,6},{8,9},{9,8},{10,11... | collective-permute-start | bytes 4718600 | tf_op jit(solution)/shard_map/ppermute | solution.py:51
  0.7 8.1 %collective-permute-start.1 = (bf16[1024,768]{1,0:T(8,128)(2,1)}, bf16[1024,768]{1,0:T(8,128)(2,1)S(1)}, u32[]{:S(2)}, u32[]{:S(2)}) collective-permute-start(bf16[1024,768]{1,0:T(8,128)(2,1)} %bitcast.75), channel_id=1, source_target_pairs={{0,1},{1,0},{2,3},{3,2},{4,5},{5,4},{6,7},{7,6},{8,9},{9,8},{10,11... | collective-permute-start | bytes 4718600 | tf_op jit(solution)/shard_map/ppermute | solution.py:51
  1.2 7.7 %collective-permute-start.2 = (bf16[768,1024]{1,0:T(8,128)(2,1)}, bf16[768,1024]{1,0:T(8,128)(2,1)}, u32[]{:S(2)}, u32[]{:S(2)}) collective-permute-start(bf16[768,1024]{1,0:T(8,128)(2,1)} %bitcast.69), channel_id=1, source_target_pairs={{0,1},{1,0},{2,3},{3,2},{4,5},{5,4},{6,7},{7,6},{8,9},{9,8},{10,11... | collective-permute-start | bytes 4718600 | tf_op jit(solution)/shard_map/ppermute | solution.py:51
  1.3 37.5 %collective-permute-start.15 = (bf16[1024,768]{1,0:T(8,128)(2,1)}, bf16[1024,768]{1,0:T(8,128)(2,1)}, u32[]{:S(2)}, u32[]{:S(2)}) collective-permute-start(bf16[1024,768]{1,0:T(8,128)(2,1)} %bitcast.73), channel_id=1, source_target_pairs={{0,2},{1,3},{2,0},{3,1},{4,6},{5,7},{6,4},{7,5},{8,10},{9,11},{10,... | collective-permute-start | bytes 4718600 | tf_op jit(solution)/shard_map/ppermute | solution.py:51
  1.8 70.7 %collective-permute-start.13 = (bf16[1024,768]{1,0:T(8,128)(2,1)}, bf16[1024,768]{1,0:T(8,128)(2,1)}, u32[]{:S(2)}, u32[]{:S(2)}) collective-permute-start(bf16[1024,768]{1,0:T(8,128)(2,1)} %bitcast.76), channel_id=1, source_target_pairs={{0,2},{1,3},{2,0},{3,1},{4,6},{5,7},{6,4},{7,5},{8,10},{9,11},{10,... | collective-permute-start | bytes 4718600 | tf_op jit(solution)/shard_map/ppermute | solution.py:51
  7.7 31.1 %copy-start = (bf16[1,1,768,1024]{3,2,1,0:T(8,128)(2,1)S(1)}, bf16[1,1,768,1024]{3,2,1,0:T(8,128)(2,1)}, u32[]{:S(2)}) copy-start(bf16[1,1,768,1024]{3,2,1,0:T(8,128)(2,1)} %param.19) | copy-start | bytes 4718596
  8.9 30.4 %collective-permute-start.3 = (bf16[48,4096]{1,0:T(8,128)(2,1)S(1)}, bf16[48,4096]{1,0:T(8,128)(2,1)S(1)}, u32[]{:S(2)}, u32[]{:S(2)}) collective-permute-start(bf16[48,4096]{1,0:T(8,128)(2,1)S(1)} %get-tuple-element.66), channel_id=1, source_target_pairs={{0,8},{1,9},{2,10},{3,11},{4,0},{5,1},{6,2},{7,3},{8,12},{9,13},{1... | collective-permute-start | bytes 1179656 | tf_op jit(solution)/shard_map/ppermute | solution.py:57
  9.4 30.5 %collective-permute-start.6 = (bf16[48,4096]{1,0:T(8,128)(2,1)S(1)}, bf16[48,4096]{1,0:T(8,128)(2,1)S(1)}, u32[]{:S(2)}, u32[]{:S(2)}) collective-permute-start(bf16[48,4096]{1,0:T(8,128)(2,1)S(1)} %get-tuple-element.71), channel_id=1, source_target_pairs={{0,4},{1,5},{2,6},{3,7},{4,12},{5,13},{6,14},{7,15},{8,0},{9,1},{1... | collective-permute-start | bytes 1179656 | tf_op jit(solution)/shard_map/ppermute | solution.py:57
  11.9 42.9 %collective-permute-start.9 = (bf16[48,4096]{1,0:T(8,128)(2,1)S(1)}, bf16[48,4096]{1,0:T(8,128)(2,1)S(1)}, u32[]{:S(2)}, u32[]{:S(2)}) collective-permute-start(bf16[48,4096]{1,0:T(8,128)(2,1)S(1)} %get-tuple-element.76), channel_id=1, source_target_pairs={{0,12},{1,13},{2,14},{3,15},{4,8},{5,9},{6,10},{7,11},{8,4},{9,5},... | collective-permute-start | bytes 1179656 | tf_op jit(solution)/shard_map/ppermute | solution.py:57
  38.8 66.9 %collective-permute-start.17 = (bf16[768,1024]{1,0:T(8,128)(2,1)S(1)}, bf16[768,1024]{1,0:T(8,128)(2,1)S(1)}, u32[]{:S(2)}, u32[]{:S(2)}) collective-permute-start(bf16[768,1024]{1,0:T(8,128)(2,1)S(1)} %bitcast.70), channel_id=1, source_target_pairs={{0,2},{1,3},{2,0},{3,1},{4,6},{5,7},{6,4},{7,5},{8,10},{9,11},{10,... | collective-permute-start | bytes 4718600 | tf_op jit(solution)/shard_map/ppermute | solution.py:51
  39.4 33.1 %collective-permute-start.4 = (bf16[48,4096]{1,0:T(8,128)(2,1)S(1)}, bf16[48,4096]{1,0:T(8,128)(2,1)S(1)}, u32[]{:S(2)}, u32[]{:S(2)}) collective-permute-start(bf16[48,4096]{1,0:T(8,128)(2,1)S(1)} %get-tuple-element.67), channel_id=1, source_target_pairs={{0,8},{1,9},{2,10},{3,11},{4,0},{5,1},{6,2},{7,3},{8,12},{9,13},{1... | collective-permute-start | bytes 1179656 | tf_op jit(solution)/shard_map/ppermute | solution.py:57
  39.9 34.6 %collective-permute-start.7 = (bf16[48,4096]{1,0:T(8,128)(2,1)S(1)}, bf16[48,4096]{1,0:T(8,128)(2,1)S(1)}, u32[]{:S(2)}, u32[]{:S(2)}) collective-permute-start(bf16[48,4096]{1,0:T(8,128)(2,1)S(1)} %get-tuple-element.72), channel_id=1, source_target_pairs={{0,4},{1,5},{2,6},{3,7},{4,12},{5,13},{6,14},{7,15},{8,0},{9,1},{1... | collective-permute-start | bytes 1179656 | tf_op jit(solution)/shard_map/ppermute | solution.py:57
  54.8 33.7 %collective-permute-start.10 = (bf16[48,4096]{1,0:T(8,128)(2,1)S(1)}, bf16[48,4096]{1,0:T(8,128)(2,1)S(1)}, u32[]{:S(2)}, u32[]{:S(2)}) collective-permute-start(bf16[48,4096]{1,0:T(8,128)(2,1)S(1)} %get-tuple-element.77), channel_id=1, source_target_pairs={{0,12},{1,13},{2,14},{3,15},{4,8},{5,9},{6,10},{7,11},{8,4},{9,5},... | collective-permute-start | bytes 1179656 | tf_op jit(solution)/shard_map/ppermute | solution.py:57
  72.5 21.7 %collective-permute-start.14 = (bf16[1024,768]{1,0:T(8,128)(2,1)}, bf16[1024,768]{1,0:T(8,128)(2,1)S(1)}, u32[]{:S(2)}, u32[]{:S(2)}) collective-permute-start(bf16[1024,768]{1,0:T(8,128)(2,1)} %collective-permute-done.13.refs_0_), channel_id=1, source_target_pairs={{0,1},{1,0},{2,3},{3,2},{4,5},{5,4},{6,7},{7,6},{8,9},{9,8},{10,11... | collective-permute-start | bytes 4718600 | tf_op jit(solution)/shard_map/ppermute | solution.py:51
  73.9 35.6 %collective-permute-start.5 = (bf16[48,4096]{1,0:T(8,128)(2,1)S(1)}, bf16[48,4096]{1,0:T(8,128)(2,1)S(1)}, u32[]{:S(2)}, u32[]{:S(2)}) collective-permute-start(bf16[48,4096]{1,0:T(8,128)(2,1)S(1)} %get-tuple-element.68), channel_id=1, source_target_pairs={{0,8},{1,9},{2,10},{3,11},{4,0},{5,1},{6,2},{7,3},{8,12},{9,13},{1... | collective-permute-start | bytes 1179656 | tf_op jit(solution)/shard_map/ppermute | solution.py:57
  74.4 35.1 %collective-permute-start.8 = (bf16[48,4096]{1,0:T(8,128)(2,1)S(1)}, bf16[48,4096]{1,0:T(8,128)(2,1)S(1)}, u32[]{:S(2)}, u32[]{:S(2)}) collective-permute-start(bf16[48,4096]{1,0:T(8,128)(2,1)S(1)} %get-tuple-element.73), channel_id=1, source_target_pairs={{0,4},{1,5},{2,6},{3,7},{4,12},{5,13},{6,14},{7,15},{8,0},{9,1},{1... | collective-permute-start | bytes 1179656 | tf_op jit(solution)/shard_map/ppermute | solution.py:57
  88.5 3.6 %collective-permute-start.16 = (bf16[1024,768]{1,0:T(8,128)(2,1)}, bf16[1024,768]{1,0:T(8,128)(2,1)S(1)}, u32[]{:S(2)}, u32[]{:S(2)}) collective-permute-start(bf16[1024,768]{1,0:T(8,128)(2,1)} %collective-permute-done.15.refs_0_), channel_id=1, source_target_pairs={{0,1},{1,0},{2,3},{3,2},{4,5},{5,4},{6,7},{7,6},{8,9},{9,8},{10,11... | collective-permute-start | bytes 4718600 | tf_op jit(solution)/shard_map/ppermute | solution.py:51
  92.1 21.6 %collective-permute-start.11 = (bf16[48,4096]{1,0:T(8,128)(2,1)S(1)}, bf16[48,4096]{1,0:T(8,128)(2,1)S(1)}, u32[]{:S(2)}, u32[]{:S(2)}) collective-permute-start(bf16[48,4096]{1,0:T(8,128)(2,1)S(1)} %get-tuple-element.78), channel_id=1, source_target_pairs={{0,12},{1,13},{2,14},{3,15},{4,8},{5,9},{6,10},{7,11},{8,4},{9,5},... | collective-permute-start | bytes 1179656 | tf_op jit(solution)/shard_map/ppermute | solution.py:57
  94.2 1.4 copy-start.1
  95.6 1.4 copy-start.2
  105.7 3.4 %collective-permute-start.18 = (bf16[768,1024]{1,0:T(8,128)(2,1)S(1)}, bf16[768,1024]{1,0:T(8,128)(2,1)S(1)}, u32[]{:S(2)}, u32[]{:S(2)}) collective-permute-start(bf16[768,1024]{1,0:T(8,128)(2,1)S(1)} %collective-permute-done.17), channel_id=1, source_target_pairs={{0,1},{1,0},{2,3},{3,2},{4,5},{5,4},{6,7},{7,6},{8,9},{9,8},{10,11... | collective-permute-start | bytes 4718600 | tf_op jit(solution)/shard_map/ppermute | solution.py:51
  120.8 7.1 %copy-start.3 = (s32[1,128,1]{1,2,0:T(1,128)S(1)}, s32[1,128,1]{1,2,0:T(1,128)}, u32[]{:S(2)}) copy-start(s32[1,128,1]{1,2,0:T(1,128)} %param.15) | copy-start | bytes 1540
  120.8 7.1 %copy-start.4 = (s32[1,128,1]{1,2,0:T(1,128)S(1)}, s32[1,128,1]{1,2,0:T(1,128)}, u32[]{:S(2)}) copy-start(s32[1,128,1]{1,2,0:T(1,128)} %param.11) | copy-start | bytes 1540
  120.8 7.1 %copy-start.5 = (f32[1,128,1]{1,2,0:T(1,128)S(1)}, f32[1,128,1]{1,2,0:T(1,128)}, u32[]{:S(2)}) copy-start(f32[1,128,1]{1,2,0:T(1,128)} %param.12) | copy-start | bytes 1540
  120.9 36.4 %collective-permute-start.19 = (bf16[48,4096]{1,0:T(8,128)(2,1)S(1)}, bf16[48,4096]{1,0:T(8,128)(2,1)S(1)}, u32[]{:S(2)}, u32[]{:S(2)}) collective-permute-start(bf16[48,4096]{1,0:T(8,128)(2,1)S(1)} %get-tuple-element.125), channel_id=1, source_target_pairs={{0,28},{1,29},{2,30},{3,31},{4,20},{5,21},{6,22},{7,23},{8,24},{9,... | collective-permute-start | bytes 1179656 | tf_op jit(solution)/shard_map/ppermute | solution.py:69
  121.5 35.9 %collective-permute-start.20 = (bf16[48,4096]{1,0:T(8,128)(2,1)S(1)}, bf16[48,4096]{1,0:T(8,128)(2,1)S(1)}, u32[]{:S(2)}, u32[]{:S(2)}) collective-permute-start(bf16[48,4096]{1,0:T(8,128)(2,1)S(1)} %get-tuple-element.124), channel_id=1, source_target_pairs={{0,24},{1,25},{2,26},{3,27},{4,16},{5,17},{6,18},{7,19},{8,28},{9,... | collective-permute-start | bytes 1179656 | tf_op jit(solution)/shard_map/ppermute | solution.py:69
  121.9 35.5 %collective-permute-start.21 = (bf16[48,4096]{1,0:T(8,128)(2,1)S(1)}, bf16[48,4096]{1,0:T(8,128)(2,1)S(1)}, u32[]{:S(2)}, u32[]{:S(2)}) collective-permute-start(bf16[48,4096]{1,0:T(8,128)(2,1)S(1)} %get-tuple-element.123), channel_id=1, source_target_pairs={{0,20},{1,21},{2,22},{3,23},{4,28},{5,29},{6,30},{7,31},{8,16},{9,... | collective-permute-start | bytes 1179656 | tf_op jit(solution)/shard_map/ppermute | solution.py:69
  125.3 32.1 %collective-permute-start.22 = (bf16[48,4096]{1,0:T(8,128)(2,1)S(1)}, bf16[48,4096]{1,0:T(8,128)(2,1)S(1)}, u32[]{:S(2)}, u32[]{:S(2)}) collective-permute-start(bf16[48,4096]{1,0:T(8,128)(2,1)S(1)} %get-tuple-element.122), channel_id=1, source_target_pairs={{0,16},{1,17},{2,18},{3,19},{4,24},{5,25},{6,26},{7,27},{8,20},{9,... | collective-permute-start | bytes 1179656 | tf_op jit(solution)/shard_map/ppermute | solution.py:69
  127.9 29.5 %collective-permute-start.12 = (f32[2,128]{1,0:T(2,128)S(1)}, f32[2,128]{1,0:T(2,128)S(1)}, u32[]{:S(2)}, u32[]{:S(2)}) collective-permute-start(f32[2,128]{1,0:T(2,128)S(1)} %maximum_select_fusion), channel_id=1, source_target_pairs={{0,16},{1,17},{2,18},{3,19},{4,20},{5,21},{6,22},{7,23},{8,24},{9,... | collective-permute-start | bytes 3080 | tf_op jit(solution)/shard_map/ppermute | solution.py:69

commit v8 on v7

--- a/solution.py
+++ b/solution.py
@@ -345,14 +345,15 @@
     gate_factor = up_value * sigmoid_value * (1.0 + gate_value * (1.0 - sigmoid_value))
     up_factor = gate_value * sigmoid_value
 
-    landed = lax.optimization_barrier((*grad_blocks[1:], gate_factor, up_factor, *fwd_parts))
+    late_turned = turned(down_mats[2:])
+    landed = lax.optimization_barrier(
+        (*grad_blocks[1:], gate_factor, up_factor, *fwd_parts, *late_turned)
+    )
     grads = jnp.concatenate([grad_blocks[0], *landed[: experts - 1]])
     quarter = down.shape[1]
     grad_hidden = sum(
         jnp.dot(grads[:, j * quarter : (j + 1) * quarter], mat, preferred_element_type=jnp.float32)
-        if j < 2
-        else contract_cols(grads[:, j * quarter : (j + 1) * quarter], mat)
-        for j, mat in enumerate([down_turned, beside_turned, *down_mats[2:]])
+        for j, mat in enumerate([down_turned, beside_turned, *landed[-2:]])
     )
     grad_gate = (grad_hidden * landed[experts - 1]).astype(jnp.bfloat16)
     grad_up = (grad_hidden * landed[experts]).astype(jnp.bfloat16)
@@ -363,7 +364,7 @@
         ).astype(jnp.bfloat16)
         for g, u in zip(turned_mats[:QUARTERS], turned_mats[QUARTERS:])
     ]
-    fwd_parts = landed[experts + 1 :]
+    fwd_parts = landed[experts + 1 : -2]
     merged = lax.axis_size("pp") == 2
 
     done = tuple(grad_blocks[1:])

time: 161 us -> 161 us (level)
    pallas_call x1 -> x2, Pallas kernels: 4.39 us -> 5.25 us  [turned(): pl.pallas_call(turn_kernel, in_specs=[vmem] * len(mats), out_specs=[vmem]...]
  transfers between devices with their start and end apart: 23 -> 23, of which waited for: 12 -> 14; matrix products, arithmetic and copies ran while one was open for 6% -> 6% of each run, Pallas kernels for 7% -> 8%
where the time goes in v8:
time: 161 us; the launch traced here: 160 us
  waiting for transfers between devices  101 us (63%)
  starting transfers between devices  24.3 us (15%)
  matrix products  15.8 us (10%)
  Pallas kernels  14.6 us (9%)
  local copies, waits for them, and re-layouts  2.18 us (1%)
    ppermute x9, waiting for transfers between devices, paired(): return lax.ppermute(block, 'ep', [(i, i ^ distance) for i in range(count)])  44.8 us
    ppermute x5, waiting for transfers between devices, handed(): return lax.ppermute(block, ('pp', 'ep'), route)  29 us
    ppermute x9, waiting for transfers between devices, sent(): lax.ppermute(block, 'ep', [(i, target(i, distance)) for i in range(count)])  27.2 us
    ppermute x9, starting transfers between devices, sent(): lax.ppermute(block, 'ep', [(i, target(i, distance)) for i in range(count)])  13.6 us
    dot_general x16, matrix products, rows_times(): jnp.dot(rows[:, j * quarter:(j + 1) * quarter], mat, preferred_element_ty...  7.79 us
    ppermute x5, starting transfers between devices, handed(): return lax.ppermute(block, ('pp', 'ep'), route)  7.5 us
    pallas_call x2, Pallas kernels, turned(): pl.pallas_call(turn_kernel, in_specs=[vmem] * len(mats), out_specs=[vmem]...  5.25 us
    pallas_call x1, Pallas kernels, spread(): pl.pallas_call(functools.partial(spread_kernel, slot_cap, experts), in_sp...  3.42 us
  transfers between devices with their start and end apart: 23, of which 14 were waited for; matrix products, arithmetic and copies ran while one was open for 6% of the time, Pallas kernels for 8%

profile of v8, /device:TPU:14, one launch (start us, length us, event | category | flops | bytes accessed | tf_op | source)
XLA Modules:
  0.0 159.7 jit_solution(11785170683767818758)
XLA Ops:
  1.8 1.5 collective-permute-start.13
  3.4 0.9 collective-permute-done.refs_1_
  4.3 3.4 %shard_map.113 = (bf16[48,4096]{1,0:T(8,128)(2,1)S(1)}, bf16[48,4096]{1,0:T(8,128)(2,1)S(1)}, bf16[48,4096]{1,0:T(8,128)(2,1)S(1)}, bf16[48,4096]{1,0:T(8,128)(2...) custom-call(s32[4]{0:T(128)S(1)} %pad_add_fusion.where_ref, ...), custom_call_target="tpu_custom_call" | custom-call | flops 603979776 | bytes 7864320 | tf_op jit(solution)/shard_map/pallas_call | solution.py:116
  7.8 1.1 collective-permute-done.1.refs_5_
  9.4 2.5 %collective-permute-start.6 = (bf16[48,4096]{1,0:T(8,128)(2,1)S(1)}, bf16[48,4096]{1,0:T(8,128)(2,1)S(1)}, u32[]{:S(2)}, u32[]{:S(2)}) collective-permute-start(bf16[48,4096]{1,0:T(8,128)(2,1)S(1)} %get-tuple-element.75), channel_id=1, source_target_pairs={{0,4},{1,5},{2,6},{3,7},{4,12},{5,13},{6,14},{7,15},{8,0},{9,1},{1... | collective-permute-start | bytes 1179656 | tf_op jit(solution)/shard_map/ppermute | solution.py:57
  11.9 1.6 collective-permute-start.9
  13.5 25.3 %collective-permute-done.15.refs_0_ = bf16[1024,768]{1,0:T(8,128)(2,1)} collective-permute-done((bf16[1024,768]{1,0:T(8,128)(2,1)}, bf16[1024,768]{1,0:T(8,128)(2,1)}, u32[]{:S(2)}, u32[]{:S(2)}) %collective-permute-start.15) | collective-permute-done | bytes 1572896 | tf_op jit(solution)/shard_map/ppermute | solution.py:51
  39.9 2.5 %collective-permute-start.7 = (bf16[48,4096]{1,0:T(8,128)(2,1)S(1)}, bf16[48,4096]{1,0:T(8,128)(2,1)S(1)}, u32[]{:S(2)}, u32[]{:S(2)}) collective-permute-start(bf16[48,4096]{1,0:T(8,128)(2,1)S(1)} %get-tuple-element.76), channel_id=1, source_target_pairs={{0,4},{1,5},{2,6},{3,7},{4,12},{5,13},{6,14},{7,15},{8,0},{9,1},{1... | collective-permute-start | bytes 1179656 | tf_op jit(solution)/shard_map/ppermute | solution.py:57
  42.4 12.4 %collective-permute-done.9 = bf16[48,4096]{1,0:T(8,128)(2,1)S(1)} collective-permute-done((bf16[48,4096]{1,0:T(8,128)(2,1)S(1)}, bf16[48,4096]{1,0:T(8,128)(2,1)S(1)}, u32[]{:S(2)}, u32[]{:S(2)}) %collective-permute-start.9) | collective-permute-done | bytes 393248 | tf_op jit(solution)/shard_map/ppermute | solution.py:57
  54.8 1.6 collective-permute-start.10
  56.4 1.9 %shard_map.115 = (bf16[1024,768]{1,0:T(8,128)(2,1)S(1)}, bf16[768,1024]{1,0:T(8,128)(2,1)S(1)}) custom-call(bf16[1024,768]{1,0:T(8,128)(2,1)} %collective-permute-done.15.refs_0_, bf16[768,1024]{1,0:T(8,128)(2,1)} %collective-permute-done.2.refs_1_), custom_call_target="tpu_custom_call" | custom-call | bytes 6291456 | tf_op jit(solution)/shard_map/pallas_call | solution.py:214
  59.8 12.7 %collective-permute-done.13.refs_0_ = bf16[1024,768]{1,0:T(8,128)(2,1)} collective-permute-done((bf16[1024,768]{1,0:T(8,128)(2,1)}, bf16[1024,768]{1,0:T(8,128)(2,1)}, u32[]{:S(2)}, u32[]{:S(2)}) %collective-permute-start.13) | collective-permute-done | bytes 1572896 | tf_op jit(solution)/shard_map/ppermute | solution.py:51
  72.5 1.4 shard_map.114.refs_6_
  74.4 2.5 %collective-permute-start.8 = (bf16[48,4096]{1,0:T(8,128)(2,1)S(1)}, bf16[48,4096]{1,0:T(8,128)(2,1)S(1)}, u32[]{:S(2)}, u32[]{:S(2)}) collective-permute-start(bf16[48,4096]{1,0:T(8,128)(2,1)S(1)} %get-tuple-element.77), channel_id=1, source_target_pairs={{0,4},{1,5},{2,6},{3,7},{4,12},{5,13},{6,14},{7,15},{8,0},{9,1},{1... | collective-permute-start | bytes 1179656 | tf_op jit(solution)/shard_map/ppermute | solution.py:57
  77.0 11.5 %collective-permute-done.10 = bf16[48,4096]{1,0:T(8,128)(2,1)S(1)} collective-permute-done((bf16[48,4096]{1,0:T(8,128)(2,1)S(1)}, bf16[48,4096]{1,0:T(8,128)(2,1)S(1)}, u32[]{:S(2)}, u32[]{:S(2)}) %collective-permute-start.10) | collective-permute-done | bytes 393248 | tf_op jit(solution)/shard_map/ppermute | solution.py:57
  90.9 1.2 collective-permute-done.16.refs_3_
  92.1 1.6 collective-permute-start.11
  94.7 0.9 copy-done.1
  96.1 0.9 copy-done.2
  97.5 4.4 %shard_map.116 = (bf16[768,1024]{1,0:T(8,128)(2,1)S(1)}, bf16[768,1024]{1,0:T(8,128)(2,1)S(1)}, bf16[768,1024]{1,0:T(8,128)(2,1)S(1)}, bf16[768,1024]{1,0:T(8,12...) custom-call(bf16[1024,768]{1,0:T(8,128)(2,1)S(1)} %bitcast.74, ...), custom_call_target="tpu_custom_call" | custom-call | bytes 31457280 | tf_op jit(solution)/shard_map/pallas_call | solution.py:237
  102.9 2.7 %collective-permute-done.17.refs_0_ = bf16[768,1024]{1,0:T(8,128)(2,1)S(1)} collective-permute-done((bf16[768,1024]{1,0:T(8,128)(2,1)S(1)}, bf16[768,1024]{1,0:T(8,128)(2,1)S(1)}, u32[]{:S(2)}, u32[]{:S(2)}) %collective-permute-start.17) | collective-permute-done | bytes 1572896 | tf_op jit(solution)/shard_map/ppermute | solution.py:51
  108.2 0.8 collective-permute-done.18.refs_1_
  109.1 0.9 shard_map.117
  110.4 3.3 %collective-permute-done.11 = bf16[48,4096]{1,0:T(8,128)(2,1)S(1)} collective-permute-done((bf16[48,4096]{1,0:T(8,128)(2,1)S(1)}, bf16[48,4096]{1,0:T(8,128)(2,1)S(1)}, u32[]{:S(2)}, u32[]{:S(2)}) %collective-permute-start.11) | collective-permute-done | bytes 393248 | tf_op jit(solution)/shard_map/ppermute | solution.py:57
  115.8 0.7 fusion.57
  121.0 1.2 collective-permute-start.20
  122.2 2.6 %collective-permute-start.21 = (bf16[48,4096]{1,0:T(8,128)(2,1)S(1)}, bf16[48,4096]{1,0:T(8,128)(2,1)S(1)}, u32[]{:S(2)}, u32[]{:S(2)}) collective-permute-start(bf16[48,4096]{1,0:T(8,128)(2,1)S(1)} %get-tuple-element.131), channel_id=1, source_target_pairs={{0,20},{1,21},{2,22},{3,23},{4,28},{5,29},{6,30},{7,31},{8,16},{9,... | collective-permute-start | bytes 1179656 | tf_op jit(solution)/shard_map/ppermute | solution.py:69
  124.8 2.5 %collective-permute-start.22 = (bf16[48,4096]{1,0:T(8,128)(2,1)S(1)}, bf16[48,4096]{1,0:T(8,128)(2,1)S(1)}, u32[]{:S(2)}, u32[]{:S(2)}) collective-permute-start(bf16[48,4096]{1,0:T(8,128)(2,1)S(1)} %get-tuple-element.130), channel_id=1, source_target_pairs={{0,16},{1,17},{2,18},{3,19},{4,24},{5,25},{6,26},{7,27},{8,20},{9,... | collective-permute-start | bytes 1179656 | tf_op jit(solution)/shard_map/ppermute | solution.py:69
  127.9 12.7 %collective-permute-done.12.meta_ref = f32[2,128]{1,0:T(2,128)S(1)} collective-permute-done((f32[2,128]{1,0:T(2,128)S(1)}, f32[2,128]{1,0:T(2,128)S(1)}, u32[]{:S(2)}, u32[]{:S(2)}) %collective-permute-start.12) | collective-permute-done | bytes 1056 | tf_op jit(solution)/shard_map/ppermute | solution.py:69
  140.7 9.2 %collective-permute-done.21.refs_2_ = bf16[48,4096]{1,0:T(8,128)(2,1)S(1)} collective-permute-done((bf16[48,4096]{1,0:T(8,128)(2,1)S(1)}, bf16[48,4096]{1,0:T(8,128)(2,1)S(1)}, u32[]{:S(2)}, u32[]{:S(2)}) %collective-permute-start.21) | collective-permute-done | bytes 393248 | tf_op jit(solution)/shard_map/ppermute | solution.py:69
  149.9 7.0 %collective-permute-done.22.refs_3_ = bf16[48,4096]{1,0:T(8,128)(2,1)S(1)} collective-permute-done((bf16[48,4096]{1,0:T(8,128)(2,1)S(1)}, bf16[48,4096]{1,0:T(8,128)(2,1)S(1)}, u32[]{:S(2)}, u32[]{:S(2)}) %collective-permute-start.22) | collective-permute-done | bytes 393248 | tf_op jit(solution)/shard_map/ppermute | solution.py:69
  156.9 2.6 %shard_map.118 = (bf16[128,4096]{1,0:T(8,128)(2,1)}, bf16[128,4096]{1,0:T(8,128)(2,1)}) custom-call(s32[4]{0:T(128)S(1)} %pad_add_fusion.where_ref, f32[2,128]{1,0:T(2,128)S(1)} %collective-permute-done.12.meta_ref, bf16[48,4096]{1,0:T(8,128)(2,1)S(1)} %collective-permute-done.19.refs_0_, bf16[48,4096]{1,0:T(8,128)(2,1)S(1)} %collective-permute-done.20.refs_1_, ...), custom_call_target="tpu_custom_call" | custom-call | flops 201326592 | bytes 3670016 | tf_op jit(solution)/shard_map/pallas_call | solution.py:182
  (83 shorter events, 20.4 us)
Async XLA Ops:
  0.6 3.7 %collective-permute-start = (bf16[1024,768]{1,0:T(8,128)(2,1)}, bf16[1024,768]{1,0:T(8,128)(2,1)S(1)}, u32[]{:S(2)}, u32[]{:S(2)}) collective-permute-start(bf16[1024,768]{1,0:T(8,128)(2,1)} %bitcast.72), channel_id=1, source_target_pairs={{0,1},{1,0},{2,3},{3,2},{4,5},{5,4},{6,7},{7,6},{8,9},{9,8},{10,11... | collective-permute-start | bytes 4718600 | tf_op jit(solution)/shard_map/ppermute | solution.py:51
  0.7 8.1 %collective-permute-start.1 = (bf16[1024,768]{1,0:T(8,128)(2,1)}, bf16[1024,768]{1,0:T(8,128)(2,1)S(1)}, u32[]{:S(2)}, u32[]{:S(2)}) collective-permute-start(bf16[1024,768]{1,0:T(8,128)(2,1)} %bitcast.75), channel_id=1, source_target_pairs={{0,1},{1,0},{2,3},{3,2},{4,5},{5,4},{6,7},{7,6},{8,9},{9,8},{10,11... | collective-permute-start | bytes 4718600 | tf_op jit(solution)/shard_map/ppermute | solution.py:51
  1.2 7.7 %collective-permute-start.2 = (bf16[768,1024]{1,0:T(8,128)(2,1)}, bf16[768,1024]{1,0:T(8,128)(2,1)}, u32[]{:S(2)}, u32[]{:S(2)}) collective-permute-start(bf16[768,1024]{1,0:T(8,128)(2,1)} %bitcast.69), channel_id=1, source_target_pairs={{0,1},{1,0},{2,3},{3,2},{4,5},{5,4},{6,7},{7,6},{8,9},{9,8},{10,11... | collective-permute-start | bytes 4718600 | tf_op jit(solution)/shard_map/ppermute | solution.py:51
  1.3 37.5 %collective-permute-start.15 = (bf16[1024,768]{1,0:T(8,128)(2,1)}, bf16[1024,768]{1,0:T(8,128)(2,1)}, u32[]{:S(2)}, u32[]{:S(2)}) collective-permute-start(bf16[1024,768]{1,0:T(8,128)(2,1)} %bitcast.73), channel_id=1, source_target_pairs={{0,2},{1,3},{2,0},{3,1},{4,6},{5,7},{6,4},{7,5},{8,10},{9,11},{10,... | collective-permute-start | bytes 4718600 | tf_op jit(solution)/shard_map/ppermute | solution.py:51
  1.8 70.7 %collective-permute-start.13 = (bf16[1024,768]{1,0:T(8,128)(2,1)}, bf16[1024,768]{1,0:T(8,128)(2,1)}, u32[]{:S(2)}, u32[]{:S(2)}) collective-permute-start(bf16[1024,768]{1,0:T(8,128)(2,1)} %bitcast.76), channel_id=1, source_target_pairs={{0,2},{1,3},{2,0},{3,1},{4,6},{5,7},{6,4},{7,5},{8,10},{9,11},{10,... | collective-permute-start | bytes 4718600 | tf_op jit(solution)/shard_map/ppermute | solution.py:51
  7.7 31.1 %copy-start = (bf16[1,1,768,1024]{3,2,1,0:T(8,128)(2,1)S(1)}, bf16[1,1,768,1024]{3,2,1,0:T(8,128)(2,1)}, u32[]{:S(2)}) copy-start(bf16[1,1,768,1024]{3,2,1,0:T(8,128)(2,1)} %param.19) | copy-start | bytes 4718596
  8.9 30.4 %collective-permute-start.3 = (bf16[48,4096]{1,0:T(8,128)(2,1)S(1)}, bf16[48,4096]{1,0:T(8,128)(2,1)S(1)}, u32[]{:S(2)}, u32[]{:S(2)}) collective-permute-start(bf16[48,4096]{1,0:T(8,128)(2,1)S(1)} %get-tuple-element.70), channel_id=1, source_target_pairs={{0,8},{1,9},{2,10},{3,11},{4,0},{5,1},{6,2},{7,3},{8,12},{9,13},{1... | collective-permute-start | bytes 1179656 | tf_op jit(solution)/shard_map/ppermute | solution.py:57
  9.4 30.5 %collective-permute-start.6 = (bf16[48,4096]{1,0:T(8,128)(2,1)S(1)}, bf16[48,4096]{1,0:T(8,128)(2,1)S(1)}, u32[]{:S(2)}, u32[]{:S(2)}) collective-permute-start(bf16[48,4096]{1,0:T(8,128)(2,1)S(1)} %get-tuple-element.75), channel_id=1, source_target_pairs={{0,4},{1,5},{2,6},{3,7},{4,12},{5,13},{6,14},{7,15},{8,0},{9,1},{1... | collective-permute-start | bytes 1179656 | tf_op jit(solution)/shard_map/ppermute | solution.py:57
  11.9 42.9 %collective-permute-start.9 = (bf16[48,4096]{1,0:T(8,128)(2,1)S(1)}, bf16[48,4096]{1,0:T(8,128)(2,1)S(1)}, u32[]{:S(2)}, u32[]{:S(2)}) collective-permute-start(bf16[48,4096]{1,0:T(8,128)(2,1)S(1)} %get-tuple-element.80), channel_id=1, source_target_pairs={{0,12},{1,13},{2,14},{3,15},{4,8},{5,9},{6,10},{7,11},{8,4},{9,5},... | collective-permute-start | bytes 1179656 | tf_op jit(solution)/shard_map/ppermute | solution.py:57
  38.8 66.9 %collective-permute-start.17 = (bf16[768,1024]{1,0:T(8,128)(2,1)S(1)}, bf16[768,1024]{1,0:T(8,128)(2,1)S(1)}, u32[]{:S(2)}, u32[]{:S(2)}) collective-permute-start(bf16[768,1024]{1,0:T(8,128)(2,1)S(1)} %bitcast.70), channel_id=1, source_target_pairs={{0,2},{1,3},{2,0},{3,1},{4,6},{5,7},{6,4},{7,5},{8,10},{9,11},{10,... | collective-permute-start | bytes 4718600 | tf_op jit(solution)/shard_map/ppermute | solution.py:51
  39.4 33.1 %collective-permute-start.4 = (bf16[48,4096]{1,0:T(8,128)(2,1)S(1)}, bf16[48,4096]{1,0:T(8,128)(2,1)S(1)}, u32[]{:S(2)}, u32[]{:S(2)}) collective-permute-start(bf16[48,4096]{1,0:T(8,128)(2,1)S(1)} %get-tuple-element.71), channel_id=1, source_target_pairs={{0,8},{1,9},{2,10},{3,11},{4,0},{5,1},{6,2},{7,3},{8,12},{9,13},{1... | collective-permute-start | bytes 1179656 | tf_op jit(solution)/shard_map/ppermute | solution.py:57
  39.9 34.6 %collective-permute-start.7 = (bf16[48,4096]{1,0:T(8,128)(2,1)S(1)}, bf16[48,4096]{1,0:T(8,128)(2,1)S(1)}, u32[]{:S(2)}, u32[]{:S(2)}) collective-permute-start(bf16[48,4096]{1,0:T(8,128)(2,1)S(1)} %get-tuple-element.76), channel_id=1, source_target_pairs={{0,4},{1,5},{2,6},{3,7},{4,12},{5,13},{6,14},{7,15},{8,0},{9,1},{1... | collective-permute-start | bytes 1179656 | tf_op jit(solution)/shard_map/ppermute | solution.py:57
  54.8 33.7 %collective-permute-start.10 = (bf16[48,4096]{1,0:T(8,128)(2,1)S(1)}, bf16[48,4096]{1,0:T(8,128)(2,1)S(1)}, u32[]{:S(2)}, u32[]{:S(2)}) collective-permute-start(bf16[48,4096]{1,0:T(8,128)(2,1)S(1)} %get-tuple-element.81), channel_id=1, source_target_pairs={{0,12},{1,13},{2,14},{3,15},{4,8},{5,9},{6,10},{7,11},{8,4},{9,5},... | collective-permute-start | bytes 1179656 | tf_op jit(solution)/shard_map/ppermute | solution.py:57
  72.5 21.7 %collective-permute-start.14 = (bf16[1024,768]{1,0:T(8,128)(2,1)}, bf16[1024,768]{1,0:T(8,128)(2,1)S(1)}, u32[]{:S(2)}, u32[]{:S(2)}) collective-permute-start(bf16[1024,768]{1,0:T(8,128)(2,1)} %collective-permute-done.13.refs_0_), channel_id=1, source_target_pairs={{0,1},{1,0},{2,3},{3,2},{4,5},{5,4},{6,7},{7,6},{8,9},{9,8},{10,11... | collective-permute-start | bytes 4718600 | tf_op jit(solution)/shard_map/ppermute | solution.py:51
  73.9 36.5 %collective-permute-start.5 = (bf16[48,4096]{1,0:T(8,128)(2,1)S(1)}, bf16[48,4096]{1,0:T(8,128)(2,1)S(1)}, u32[]{:S(2)}, u32[]{:S(2)}) collective-permute-start(bf16[48,4096]{1,0:T(8,128)(2,1)S(1)} %get-tuple-element.72), channel_id=1, source_target_pairs={{0,8},{1,9},{2,10},{3,11},{4,0},{5,1},{6,2},{7,3},{8,12},{9,13},{1... | collective-permute-start | bytes 1179656 | tf_op jit(solution)/shard_map/ppermute | solution.py:57
  74.4 36.0 %collective-permute-start.8 = (bf16[48,4096]{1,0:T(8,128)(2,1)S(1)}, bf16[48,4096]{1,0:T(8,128)(2,1)S(1)}, u32[]{:S(2)}, u32[]{:S(2)}) collective-permute-start(bf16[48,4096]{1,0:T(8,128)(2,1)S(1)} %get-tuple-element.77), channel_id=1, source_target_pairs={{0,4},{1,5},{2,6},{3,7},{4,12},{5,13},{6,14},{7,15},{8,0},{9,1},{1... | collective-permute-start | bytes 1179656 | tf_op jit(solution)/shard_map/ppermute | solution.py:57
  88.5 3.6 %collective-permute-start.16 = (bf16[1024,768]{1,0:T(8,128)(2,1)}, bf16[1024,768]{1,0:T(8,128)(2,1)S(1)}, u32[]{:S(2)}, u32[]{:S(2)}) collective-permute-start(bf16[1024,768]{1,0:T(8,128)(2,1)} %collective-permute-done.15.refs_0_), channel_id=1, source_target_pairs={{0,1},{1,0},{2,3},{3,2},{4,5},{5,4},{6,7},{7,6},{8,9},{9,8},{10,11... | collective-permute-start | bytes 4718600 | tf_op jit(solution)/shard_map/ppermute | solution.py:51
  92.1 21.6 %collective-permute-start.11 = (bf16[48,4096]{1,0:T(8,128)(2,1)S(1)}, bf16[48,4096]{1,0:T(8,128)(2,1)S(1)}, u32[]{:S(2)}, u32[]{:S(2)}) collective-permute-start(bf16[48,4096]{1,0:T(8,128)(2,1)S(1)} %get-tuple-element.82), channel_id=1, source_target_pairs={{0,12},{1,13},{2,14},{3,15},{4,8},{5,9},{6,10},{7,11},{8,4},{9,5},... | collective-permute-start | bytes 1179656 | tf_op jit(solution)/shard_map/ppermute | solution.py:57
  94.2 1.4 copy-start.1
  95.6 1.4 copy-start.2
  105.7 3.4 %collective-permute-start.18 = (bf16[768,1024]{1,0:T(8,128)(2,1)S(1)}, bf16[768,1024]{1,0:T(8,128)(2,1)S(1)}, u32[]{:S(2)}, u32[]{:S(2)}) collective-permute-start(bf16[768,1024]{1,0:T(8,128)(2,1)S(1)} %collective-permute-done.17.refs_0_), channel_id=1, source_target_pairs={{0,1},{1,0},{2,3},{3,2},{4,5},{5,4},{6,7},{7,6},{8,9},{9,8},{10,11... | collective-permute-start | bytes 4718600 | tf_op jit(solution)/shard_map/ppermute | solution.py:51
  120.2 7.1 %copy-start.3 = (s32[1,128,1]{1,2,0:T(1,128)S(1)}, s32[1,128,1]{1,2,0:T(1,128)}, u32[]{:S(2)}) copy-start(s32[1,128,1]{1,2,0:T(1,128)} %param.15) | copy-start | bytes 1540
  120.2 7.1 %copy-start.4 = (s32[1,128,1]{1,2,0:T(1,128)S(1)}, s32[1,128,1]{1,2,0:T(1,128)}, u32[]{:S(2)}) copy-start(s32[1,128,1]{1,2,0:T(1,128)} %param.11) | copy-start | bytes 1540
  120.3 7.1 %copy-start.5 = (f32[1,128,1]{1,2,0:T(1,128)S(1)}, f32[1,128,1]{1,2,0:T(1,128)}, u32[]{:S(2)}) copy-start(f32[1,128,1]{1,2,0:T(1,128)} %param.12) | copy-start | bytes 1540
  120.4 20.3 %collective-permute-start.19 = (bf16[48,4096]{1,0:T(8,128)(2,1)S(1)}, bf16[48,4096]{1,0:T(8,128)(2,1)S(1)}, u32[]{:S(2)}, u32[]{:S(2)}) collective-permute-start(bf16[48,4096]{1,0:T(8,128)(2,1)S(1)} %get-tuple-element.133), channel_id=1, source_target_pairs={{0,28},{1,29},{2,30},{3,31},{4,20},{5,21},{6,22},{7,23},{8,24},{9,... | collective-permute-start | bytes 1179656 | tf_op jit(solution)/shard_map/ppermute | solution.py:69
  121.0 19.7 %collective-permute-start.20 = (bf16[48,4096]{1,0:T(8,128)(2,1)S(1)}, bf16[48,4096]{1,0:T(8,128)(2,1)S(1)}, u32[]{:S(2)}, u32[]{:S(2)}) collective-permute-start(bf16[48,4096]{1,0:T(8,128)(2,1)S(1)} %get-tuple-element.132), channel_id=1, source_target_pairs={{0,24},{1,25},{2,26},{3,27},{4,16},{5,17},{6,18},{7,19},{8,28},{9,... | collective-permute-start | bytes 1179656 | tf_op jit(solution)/shard_map/ppermute | solution.py:69
  122.2 27.8 %collective-permute-start.21 = (bf16[48,4096]{1,0:T(8,128)(2,1)S(1)}, bf16[48,4096]{1,0:T(8,128)(2,1)S(1)}, u32[]{:S(2)}, u32[]{:S(2)}) collective-permute-start(bf16[48,4096]{1,0:T(8,128)(2,1)S(1)} %get-tuple-element.131), channel_id=1, source_target_pairs={{0,20},{1,21},{2,22},{3,23},{4,28},{5,29},{6,30},{7,31},{8,16},{9,... | collective-permute-start | bytes 1179656 | tf_op jit(solution)/shard_map/ppermute | solution.py:69
  124.8 32.1 %collective-permute-start.22 = (bf16[48,4096]{1,0:T(8,128)(2,1)S(1)}, bf16[48,4096]{1,0:T(8,128)(2,1)S(1)}, u32[]{:S(2)}, u32[]{:S(2)}) collective-permute-start(bf16[48,4096]{1,0:T(8,128)(2,1)S(1)} %get-tuple-element.130), channel_id=1, source_target_pairs={{0,16},{1,17},{2,18},{3,19},{4,24},{5,25},{6,26},{7,27},{8,20},{9,... | collective-permute-start | bytes 1179656 | tf_op jit(solution)/shard_map/ppermute | solution.py:69
  127.4 13.3 %collective-permute-start.12 = (f32[2,128]{1,0:T(2,128)S(1)}, f32[2,128]{1,0:T(2,128)S(1)}, u32[]{:S(2)}, u32[]{:S(2)}) collective-permute-start(f32[2,128]{1,0:T(2,128)S(1)} %maximum_select_fusion), channel_id=1, source_target_pairs={{0,16},{1,17},{2,18},{3,19},{4,20},{5,21},{6,22},{7,23},{8,24},{9,... | collective-permute-start | bytes 3080 | tf_op jit(solution)/shard_map/ppermute | solution.py:69
